TPU v7x, 512 devices: a whole 4x4x16 slice. The times are simulated.
512 devices in a mesh: dp: 64 (over z_lo, y, core), mp: 8 (over x, z_hi).
Axes of the slice: x: 4, y: 4, z: 16 (z_hi: 2, z_lo: 8; z = z_hi * 8 + z_lo), core: 2. Of those that a mesh axis runs over, the one named last changes fastest.
Arguments:
- hidden: bfloat16 [16384, 4096], P('dp'), may hold values from -6 to 6
- target: bfloat16 [16384, 4096], P('dp'), may hold values from -4 to 4
- query_weight: bfloat16 [4096, 4096], P('dp', 'mp'), may hold values from -0.125 to 0.125
- key_weight: bfloat16 [4096, 1024], P('dp', 'mp'), may hold values from -0.125 to 0.125
- value_weight: bfloat16 [4096, 1024], P('dp', 'mp'), may hold values from -0.125 to 0.125
- out_weight: bfloat16 [4096, 4096], P('mp', 'dp'), may hold values from -0.25 to 0.25
- query_codes: int32 [1024, 4096], P('dp', 'mp'), may hold values from 0 to 5
- key_codes: int32 [1024, 1024], P('dp', 'mp'), may hold values from 0 to 5
- value_codes: int32 [1024, 1024], P('dp', 'mp'), may hold values from 0 to 5
- out_codes: int32 [1024, 4096], P('mp', 'dp'), may hold values from 0 to 5
- doc_lengths: int32 [64, 3], P('dp'), may hold values from 1 to 192, 256 in all within a row
Outputs:
- block_out: bfloat16 [16384, 4096], P('dp', 'mp')
- grad_key: float32 [4096, 1024], P('dp', 'mp')
Inputs may be any that keep to these rules, and one draw needn't show every extreme that they name: `key_codes`: codes as for query_codes. `value_codes`: codes as for query_codes. `out_codes`: codes as for query_codes. `doc_lengths`: each row sums to 256; its last entry is the count of padding slots.
All inputs are finite; a program needn't handle non-finite values.
Results may differ from a plain program's by a relative error of at most 0.015.
Values may be sent and summed in bfloat16 or wider, within the bound.
No kernel may reach another device: no remote copies, remote signals or barrier semaphores. Data moves between devices by JAX's collectives and lax.ppermute only.
A program may use at most 64 MiB of HBM per device.

v0:
```python
import jax
import jax.numpy as jnp
from jax import lax
from jax.sharding import PartitionSpec as P

HEAD_DIM = 128
LOSS_DIV = 16


KEPT_PAIRS = ((0, 1), (0, 2), (0, 3), (1, 2), (1, 3), (2, 3))
ROPE_BASE = 500000.0


def apply_mask(weight, group_codes):
    chosen_rows = []
    for within in range(4):
        chosen = jnp.zeros(group_codes.shape, jnp.bool_)
        for number, kept_pair in enumerate(KEPT_PAIRS):
            if within in kept_pair:
                chosen = chosen | (group_codes == number)
        chosen_rows.append(chosen)
    keep_mask = jnp.stack(chosen_rows, axis=1).reshape(weight.shape)
    return jnp.where(keep_mask, weight, jnp.zeros_like(weight))


def doc_layout(lengths, row_total):
    doc_ends = jnp.cumsum(lengths, dtype=jnp.int32)
    positions = jnp.arange(row_total, dtype=jnp.int32)
    passed = positions[:, None] >= doc_ends[None, :]
    segment = jnp.sum(passed.astype(jnp.int32), axis=1, dtype=jnp.int32)
    begins = jnp.sum(jnp.where(passed, lengths[None, :], 0), axis=1, dtype=jnp.int32)
    return (segment, positions - begins, segment < lengths.shape[0] - 1)


def angles(doc_pos, head_dim):
    exponent = jnp.arange(head_dim // 2, dtype=jnp.float32) * (2.0 / head_dim)
    inverse_freq = jnp.power(jnp.float32(ROPE_BASE), -exponent)
    phases = doc_pos.astype(jnp.float32)[..., None] * inverse_freq
    return (jnp.cos(phases)[..., None, :], jnp.sin(phases)[..., None, :])


def rotate(values, angle_cos, angle_sin):
    half_dim = values.shape[-1] // 2
    front_half = values[..., :half_dim]
    back_half = values[..., half_dim:]
    return jnp.concatenate(
        [
            front_half * angle_cos - back_half * angle_sin,
            back_half * angle_cos + front_half * angle_sin,
        ],
        axis=-1,
    )


def probabilities(queries, key_heads, segment):
    row_total = queries.shape[0]
    scores = jnp.einsum("qkgd,skd->kgqs", queries, key_heads, preferred_element_type=jnp.float32)
    scores = scores * queries.shape[-1] ** (-0.5)
    positions = jnp.arange(row_total)
    allowed = (segment[:, None] == segment[None, :]) & (positions[None, :] <= positions[:, None])
    raised = jnp.where(allowed, jnp.exp(scores), jnp.zeros_like(scores))
    return raised / jnp.sum(raised, axis=-1, keepdims=True)


def shards(
    hidden,
    target,
    query_weight,
    key_weight,
    value_weight,
    out_weight,
    query_codes,
    key_codes,
    value_codes,
    out_codes,
    doc_lengths,
):
    row_total = hidden.shape[0]
    local_heads = query_weight.shape[1] // HEAD_DIM
    local_groups = key_weight.shape[1] // HEAD_DIM
    group_size = local_heads // local_groups
    masked_query = apply_mask(query_weight, query_codes)
    masked_key = apply_mask(key_weight, key_codes)
    masked_value = apply_mask(value_weight, value_codes)
    masked_out = apply_mask(out_weight, out_codes)
    pieces = (
        lax.all_gather(masked_query, "dp", axis=0, tiled=True),
        lax.all_gather(masked_key, "dp", axis=0, tiled=True),
        lax.all_gather(masked_value, "dp", axis=0, tiled=True),
    )
    columns = hidden
    query_raw, key_raw, value_raw = tuple(
        (
            jnp.dot(columns, weight_piece, preferred_element_type=jnp.float32)
            for weight_piece in pieces
        )
    )
    out_full = lax.all_gather(masked_out, "dp", axis=1, tiled=True)
    segment, doc_pos, live_rows = doc_layout(doc_lengths[0], row_total)
    angle_cos, angle_sin = angles(doc_pos, HEAD_DIM)
    queries = rotate(query_raw.reshape(row_total, local_heads, HEAD_DIM), angle_cos, angle_sin)
    queries = queries.astype(jnp.bfloat16).reshape(row_total, local_groups, group_size, HEAD_DIM)
    key_heads = rotate(
        key_raw.reshape(row_total, local_groups, HEAD_DIM), angle_cos, angle_sin
    ).astype(jnp.bfloat16)
    values = value_raw.astype(jnp.bfloat16).reshape(row_total, local_groups, HEAD_DIM)
    probability = probabilities(queries, key_heads, segment)
    attended = jnp.einsum(
        "kgqs,skd->qkgd",
        probability.astype(jnp.bfloat16),
        values,
        preferred_element_type=jnp.float32,
    )
    attended = attended.reshape(row_total, -1).astype(jnp.bfloat16)
    partial_out = jnp.dot(attended, out_full, preferred_element_type=jnp.float32)
    column_width = target.shape[1] // lax.axis_size("mp")
    live_column = live_rows[:, None].astype(jnp.float32)
    out_share = lax.psum_scatter(
        partial_out.astype(jnp.bfloat16), "mp", scatter_dimension=1, tiled=True
    ).astype(jnp.float32)
    target_share = lax.dynamic_slice_in_dim(
        target, lax.axis_index("mp") * column_width, column_width, 1
    )
    error_share = ((out_share - target_share.astype(jnp.float32)) * live_column / LOSS_DIV).astype(
        jnp.bfloat16
    )
    out_error = lax.all_gather(error_share, "mp", axis=1, tiled=True)
    block_out = out_share.astype(jnp.bfloat16)
    d_attended = lax.dot_general(
        out_error, out_full, (((1,), (1,)), ((), ())), preferred_element_type=jnp.float32
    ).astype(jnp.bfloat16)
    d_attended = d_attended.reshape(row_total, local_groups, group_size, HEAD_DIM)
    d_prob = jnp.einsum("qkgd,skd->kgqs", d_attended, values, preferred_element_type=jnp.float32)
    row_dot = jnp.sum(probability * d_prob, axis=-1, keepdims=True)
    d_score = (probability * (d_prob - row_dot) * HEAD_DIM ** (-0.5)).astype(jnp.bfloat16)
    d_key_rot = jnp.einsum("kgqs,qkgd->skd", d_score, queries, preferred_element_type=jnp.float32)
    d_key = rotate(d_key_rot, angle_cos, -angle_sin).astype(jnp.bfloat16).reshape(row_total, -1)
    columns = hidden
    grad_share = lax.psum_scatter(
        lax.dot_general(
            columns, d_key, (((0,), (0,)), ((), ())), preferred_element_type=jnp.float32
        ),
        "dp",
        scatter_dimension=0,
        tiled=True,
    )
    grad_key = apply_mask(grad_share, key_codes)
    return (block_out, grad_key)


def solution(mesh):
    placed = (
        P("dp", None),
        P("dp", None),
        P("dp", "mp"),
        P("dp", "mp"),
        P("dp", "mp"),
        P("mp", "dp"),
        P("dp", "mp"),
        P("dp", "mp"),
        P("dp", "mp"),
        P("mp", "dp"),
        P("dp", None),
    )
    return jax.shard_map(
        shards,
        mesh=mesh,
        in_specs=placed,
        out_specs=(P("dp", "mp"), P("dp", "mp")),
        check_vma=False,
    )
```

profile of v0, /device:TPU:4, one launch (start us, length us, event | category | flops | bytes accessed | tf_op | source)
XLA Modules:
  0.0 1204.2 jit_solution(3738776893711533306)
XLA Ops:
  7.2 0.8 or_bitcast_fusion.11
  9.5 1.3 broadcast_select_fusion.3
  13.1 1.3 broadcast_select_fusion.4
  14.5 0.8 or_bitcast_fusion.7
  15.3 0.8 or_bitcast_fusion.6
  16.1 0.8 or_bitcast_fusion.5
  16.9 1.5 broadcast_select_fusion.1
  18.5 0.8 or_bitcast_fusion.3
  19.3 0.8 or_bitcast_fusion.2
  20.1 0.8 or_bitcast_fusion.1
  21.0 1.0 copy.64
  23.9 1.2 multiply_cosine_fusion
  25.0 109.7 %all-gather.8.cloned.1.call-done = bf16[4096,128]{1,0:T(8,128)(2,1)} async-done(((bf16[64,128]{1,0:T(8,128)(2,1)}), bf16[4096,128]{1,0:T(8,128)(2,1)}) %all-gather.8.cloned.1.call-update) | async-done | bytes 1048592 | tf_op jit(solution)/shard_map/all_gather | solution.py:88
  134.7 2.0 convolution_bitcast_fusion.3
  136.8 0.9 fusion.37
  137.7 114.1 %all-gather.6.cloned.1.call-done = bf16[4096,128]{1,0:T(8,128)(2,1)} async-done(((bf16[64,128]{1,0:T(8,128)(2,1)}), bf16[4096,128]{1,0:T(8,128)(2,1)}) %all-gather.6.cloned.1.call-update) | async-done | bytes 1048592 | tf_op jit(solution)/shard_map/all_gather | solution.py:89
  251.8 2.7 fusion.4
  254.5 117.9 %all-gather.10.cloned.1.call-done = bf16[4096,512]{1,0:T(8,128)(2,1)} async-done(((bf16[64,512]{1,0:T(8,128)(2,1)}), bf16[4096,512]{1,0:T(8,128)(2,1)}) %all-gather.10.cloned.1.call-update) | async-done | bytes 4194320 | tf_op jit(solution)/shard_map/all_gather | solution.py:87
  372.5 3.5 fusion.46
  376.4 1.1 subtract_convert_fusion
  378.2 1.4 fusion.45
  379.6 0.9 copy-done.8
  380.8 112.2 %all-gather.12.cloned.1.call-done = bf16[512,4096]{0,1:T(8,128)(2,1)} async-done(((bf16[512,64]{0,1:T(8,128)(2,1)}), bf16[512,4096]{0,1:T(8,128)(2,1)}) %all-gather.12.cloned.1.call-update) | async-done | bytes 4194320 | tf_op jit(solution)/shard_map/all_gather | solution.py:98
  493.0 4.9 convolution_convert_fusion
  498.0 141.0 %reduce-scatter.5.cloned.1.call-done = bf16[256,512]{1,0:T(8,128)(2,1)} async-done(((bf16[256,4096]{1,0:T(8,128)(2,1)}), bf16[256,512]{1,0:T(8,128)(2,1)}) %reduce-scatter.5.cloned.1.call-update) | async-done | bytes 262160 | tf_op jit(solution)/shard_map/reduce_scatter | solution.py:118
  638.9 1.9 multiply_convert_fusion.1
  640.9 111.9 %all-gather.14.cloned.1.call-done = bf16[256,4096]{1,0:T(8,128)(2,1)} async-done(((bf16[256,512]{1,0:T(8,128)(2,1)}), bf16[256,4096]{1,0:T(8,128)(2,1)}) %all-gather.14.cloned.1.call-update) | async-done | bytes 2097168 | tf_op jit(solution)/shard_map/all_gather | solution.py:127
  752.8 4.1 fusion.3
  758.8 1.8 convolution_bitcast_fusion
  760.5 2.9 copy.78
  763.5 432.5 %reduce-scatter.7.cloned.1.call-done = f32[64,128]{1,0:T(8,128)} async-done(((f32[4096,128]{1,0:T(8,128)}), f32[64,128]{1,0:T(8,128)}) %reduce-scatter.7.cloned.1.call-update) | async-done | bytes 32784 | tf_op jit(solution)/shard_map/reduce_scatter | solution.py:139
  1196.0 1.4 broadcast_select_fusion.2
  (66 shorter events, 9.3 us)
Async XLA Ops:
  7.2 127.6 %copy-start = (bf16[256,4096]{1,0:T(8,128)(2,1)S(1)}, bf16[256,4096]{1,0:T(8,128)(2,1)}, u32[]{:S(2)}) copy-start(bf16[256,4096]{1,0:T(8,128)(2,1)} %param.11) | copy-start | bytes 6291460
  7.2 15.6 %copy-start.7 = (s32[1,3]{1,0:T(1,128)S(1)}, s32[1,3]{1,0:T(1,128)}, u32[]{:S(2)}) copy-start(s32[1,3]{1,0:T(1,128)} %param.21) | copy-start | bytes 40
  7.2 127.5 %all-gather.8.cloned.1.call-start = ((), (), s32[]{:S(2)}) async-start(), calls=%async_computation.3 | async-start | bytes 1064960 | tf_op jit(solution)/shard_map/all_gather | solution.py:88
  10.9 240.9 %all-gather.6.cloned.1.call-start = ((), (), s32[]{:S(2)}) async-start(), calls=%async_computation.2 | async-start | bytes 1064960 | tf_op jit(solution)/shard_map/all_gather | solution.py:89
  14.4 358.0 %all-gather.10.cloned.1.call-start = ((), (), s32[]{:S(2)}) async-start(), calls=%async_computation.4 | async-start | bytes 4259840 | tf_op jit(solution)/shard_map/all_gather | solution.py:87
  18.4 474.6 %all-gather.12.cloned.1.call-start = ((), (), s32[]{:S(2)}) async-start(), calls=%async_computation.5 | async-start | bytes 4259840 | tf_op jit(solution)/shard_map/all_gather | solution.py:98
  22.8 616.2 %reduce-scatter.5.cloned.1.call-start = ((), (), s32[]{:S(2)}) async-start(), calls=%async_computation.6 | async-start | bytes 2359296 | tf_op jit(solution)/shard_map/reduce_scatter | solution.py:118
  23.0 231.5 %copy-start.5 = (f32[64]{0:T(128)}, f32[64]{0:T(128)S(1)}, u32[]{:S(2)}) copy-start(f32[64]{0:T(128)S(1)} %negate_power_fusion) | copy-start | bytes 772
  376.4 4.1 copy-start.3
  377.5 0.7 copy-start.1
  379.6 1.0 copy-start.8
  497.9 254.9 %all-gather.14.cloned.1.call-start = ((), (), s32[]{:S(2)}) async-start(), calls=%async_computation.7 | async-start | bytes 2359296 | tf_op jit(solution)/shard_map/all_gather | solution.py:127
  640.8 116.1 %copy-start.4 = (bf16[128,256,1]{1,0,2:T(8,128)(2,1)S(1)}, bf16[128,256,1]{1,0,2:T(8,128)(2,1)}, u32[]{:S(2)}) copy-start(bf16[128,256,1]{1,0,2:T(8,128)(2,1)} %fusion.4) | copy-start | bytes 196612
  640.8 116.1 %copy-start.9 = (f32[1,4,256,256]{2,3,1,0:T(8,128)S(1)}, f32[1,4,256,256]{2,3,1,0:T(8,128)}, u32[]{:S(2)}) copy-start(f32[1,4,256,256]{2,3,1,0:T(8,128)} %copy-done.8) | copy-start | bytes 3145732
  640.8 555.1 %reduce-scatter.7.cloned.1.call-start = ((), (), s32[]{:S(2)}) async-start(), calls=%async_computation.8 | async-start | bytes 2129920 | tf_op jit(solution)/shard_map/reduce_scatter | solution.py:139
  756.9 1.0 copy-start.2
  757.9 0.6 copy-start.6
Sparse Core Ops, SparseCore 0:
  11.0 123.6 all-gather.7
  136.9 114.9 all-gather.5
  254.0 118.4 all-gather.9
  374.5 118.5 all-gather.11
  498.1 140.7 reduce-scatter.4
  642.3 110.4 all-gather.13
  763.6 432.3 reduce-scatter.6
where the time goes:
time: 1210 us; the launch traced here: 1200 us
  waiting for transfers between devices  1140 us (94%)
  matrix products  21.3 us (2%)
  other arithmetic  21 us (2%)
  between operations  14.4 us (1%)
    reduce_scatter x1, waiting for transfers between devices, shards(): lax.psum_scatter(lax.dot_general(columns, d_key, (((0,), (0,)), ((), ()))...  432 us
    reduce_scatter x1, waiting for transfers between devices, shards(): lax.psum_scatter(partial_out.astype(jnp.bfloat16), 'mp', scatter_dimensio...  141 us
    all_gather x1, waiting for transfers between devices, shards(): lax.all_gather(masked_query, 'dp', axis=0, tiled=True)  118 us
    all_gather x1, waiting for transfers between devices, shards(): lax.all_gather(masked_value, 'dp', axis=0, tiled=True)  114 us
    all_gather x1, waiting for transfers between devices, shards(): out_full = lax.all_gather(masked_out, 'dp', axis=1, tiled=True)  112 us
    all_gather x1, waiting for transfers between devices, shards(): out_error = lax.all_gather(error_share, 'mp', axis=1, tiled=True)  112 us
    all_gather x1, waiting for transfers between devices, shards(): lax.all_gather(masked_key, 'dp', axis=0, tiled=True)  110 us
  transfers between devices with their start and end apart: 7, of which 7 were waited for; matrix products, arithmetic and copies ran while one was open for 2% of the time, Pallas kernels for 0%

commit v1 on v0

v1 whole, which is shorter than its diff:
```python
import functools

import jax
import jax.numpy as jnp
from jax import lax
from jax.experimental import pallas as pl
from jax.experimental.pallas import tpu as pltpu
from jax.sharding import Mesh, PartitionSpec as P

HEAD_DIM = 128
LOSS_DIV = 16
ROPE_BASE = 500000.0
KEEP_BITS = (0b000111, 0b011001, 0b101010, 0b110100)
VMEM = pltpu.CompilerParams(vmem_limit_bytes=58 * 1024 * 1024)
F32 = jnp.float32
BF16 = jnp.bfloat16
NT = (((1,), (1,)), ((), ()))
TN = (((0,), (0,)), ((), ()))


def keep_mask(codes, rows):
    groups = codes.shape[0]
    at_row = lax.broadcasted_iota(jnp.int32, (rows, groups), 0)
    at_group = lax.broadcasted_iota(jnp.int32, (rows, groups), 1)
    spread = jnp.where(at_row // 4 == at_group, 1.0, 0.0).astype(BF16)
    wide = jnp.dot(spread, codes.astype(F32).astype(BF16), preferred_element_type=F32)
    wide = wide.astype(jnp.int32)
    within = lax.broadcasted_iota(jnp.int32, wide.shape, 0) % 4
    bits = jnp.where(
        within == 0,
        KEEP_BITS[0],
        jnp.where(within == 1, KEEP_BITS[1], jnp.where(within == 2, KEEP_BITS[2], KEEP_BITS[3])),
    )
    return (lax.shift_right_logical(bits, wide) & 1) == 1


def masked(weight, codes):
    kept = jnp.where(keep_mask(codes, weight.shape[0]), weight.astype(F32), 0.0)
    return kept.astype(BF16)


def mask_qkv_kernel(qw, kw, vw, qc, kc, vc, out):
    weight = jnp.concatenate([qw[...], kw[...], vw[...]], axis=1)
    codes = jnp.concatenate([qc[...], kc[...], vc[...]], axis=1)
    kept = masked(weight, codes)
    for copy in range(out.shape[0]):
        out[copy] = kept


def mask_out_kernel(ow, oc, out):
    kept = masked(ow[...], oc[...])
    cols = kept.shape[1]
    eye = lax.broadcasted_iota(jnp.int32, (cols, cols), 0) == lax.broadcasted_iota(
        jnp.int32, (cols, cols), 1
    )
    eye = jnp.where(eye, 1.0, 0.0).astype(BF16)
    out[...] = lax.dot_general(eye, kept, NT, preferred_element_type=F32).astype(BF16)


def split_hidden_kernel(at_ref, hidden, out):
    shifts, tokens, width = out.shape
    n_z = width // 128
    half = width // 2
    low = lax.broadcasted_iota(jnp.int32, (tokens, 128), 1) < 64
    own = low == (at_ref[1] == 0)
    for shift in range(shifts):
        y_to = lax.rem(at_ref[0] + shift, shifts)
        for pair in range(n_z // 2):
            both = []
            for z in (2 * pair, 2 * pair + 1):
                lane = pl.multiple_of((z * shifts + y_to) * 128, 128)
                both.append(hidden[:, pl.ds(lane, 128)].astype(F32))
            mine = [jnp.where(own, v, pltpu.roll(v, 64, 1)) for v in both]
            rest = [jnp.where(own, pltpu.roll(v, 64, 1), v) for v in both]
            for part, (first, last) in enumerate((mine, rest)):
                start = part * half + pair * 128
                out[shift, :, start : start + 128] = jnp.where(low, first, last).astype(BF16)


def rotate(values, cos, sin):
    return values * cos + pltpu.roll(values, HEAD_DIM // 2, 1) * sin


def project_kernel(w_own, w_oth, s0, s1, s2, s3, p0, p1, p2, p3):
    half = w_own.shape[0]
    for slot, term in ((s2, p2), (s1, p1), (s3, p3), (s0, p0)):
        total = jnp.dot(slot[:, :half], w_own[...], preferred_element_type=F32)
        total += jnp.dot(slot[:, half:], w_oth[...], preferred_element_type=F32)
        term[...] = total.astype(term.dtype)


def attend_kernel(p0, p1, p2, p3, cos, sin, allow, q_out, v_out, prob_out, att_out):
    raw = p0[...] + p1[...].astype(F32) + p2[...].astype(F32) + p3[...].astype(F32)
    heads = q_out.shape[1] // HEAD_DIM
    at = heads * HEAD_DIM
    keys = rotate(raw[:, at : at + HEAD_DIM], cos[...], sin[...]).astype(BF16)
    values = raw[:, at + HEAD_DIM :].astype(BF16)
    v_out[...] = values
    for head in range(heads):
        cut = slice(head * HEAD_DIM, (head + 1) * HEAD_DIM)
        query = rotate(raw[:, cut], cos[...], sin[...]).astype(BF16)
        q_out[:, cut] = query
        scores = lax.dot_general(query, keys, NT, preferred_element_type=F32)
        raised = jnp.where(allow[...] > 0.5, jnp.exp(scores * HEAD_DIM**-0.5), 0.0)
        prob = raised / jnp.sum(raised, axis=1, keepdims=True)
        prob_out[head] = prob
        att_out[:, cut] = jnp.dot(prob.astype(BF16), values, preferred_element_type=F32).astype(
            BF16
        )


def key_grad_kernel(d_own, d_other, q_ref, v_ref, prob_ref, cos, sin, out):
    d_att = (d_own[...] + d_other[...].astype(F32)).astype(BF16)
    total = jnp.zeros(out.shape, F32)
    for head in range(prob_ref.shape[0]):
        cut = slice(head * HEAD_DIM, (head + 1) * HEAD_DIM)
        d_prob = lax.dot_general(d_att[:, cut], v_ref[...], NT, preferred_element_type=F32)
        prob = prob_ref[head]
        row_dot = jnp.sum(prob * d_prob, axis=1, keepdims=True)
        d_score = (prob * (d_prob - row_dot) * HEAD_DIM**-0.5).astype(BF16)
        total += lax.dot_general(d_score, q_ref[:, cut], TN, preferred_element_type=F32)
    out[...] = rotate(total, cos[...], -sin[...]).astype(BF16)


def out_block(pieces, k, r):
    return jnp.concatenate([piece[k, r] for piece in pieces], axis=0)


def out_kernel(at_ref, own, oth, *refs):
    pieces, out = refs[:-1], refs[-1]
    zh = at_ref[2]
    for k in range(out.shape[0]):
        total = lax.dot_general(own[...], out_block(pieces, k, zh), NT, preferred_element_type=F32)
        total += lax.dot_general(
            oth[...], out_block(pieces, k, 1 - zh), NT, preferred_element_type=F32
        )
        out[k] = total.astype(out.dtype)


def d_att_kernel(which, at_ref, errors, *refs):
    pieces, out = refs[:-1], refs[-1]
    r = at_ref[2] if which == 0 else 1 - at_ref[2]
    total = jnp.zeros(out.shape, F32)
    for k in range(errors.shape[0]):
        total += jnp.dot(errors[k], out_block(pieces, k, r), preferred_element_type=F32)
    out[...] = total.astype(out.dtype)


def error_kernel(at_ref, blocks, target, live, block_out, errors):
    tokens = target.shape[0]
    n_y = target.shape[1] // 128
    swap = at_ref[1] == 1
    for shift in range(n_y):
        y_from = lax.rem(at_ref[0] + n_y - shift, n_y)
        lane = pl.multiple_of(y_from * 128, 128)
        cut = slice(shift * 128, (shift + 1) * 128)
        total = jnp.sum(blocks[:, :, cut].astype(F32), axis=0)
        placed = jnp.where(swap, pltpu.roll(total, 64, 1), total)
        block_out[:, pl.ds(lane, 128)] = placed.astype(BF16)
        want = target[:, pl.ds(lane, 128)].astype(F32)
        want = jnp.where(swap, pltpu.roll(want, 64, 1), want)
        error = ((total - want) * live[...] / LOSS_DIV).astype(BF16)
        for k in range(errors.shape[0]):
            errors[k, :, cut] = error


def grad_kernel(s0, s1, s2, s3, d0, d1, d2, d3, own, oth):
    half = own.shape[0]
    for at, out in ((0, own), (half, oth)):
        total = jnp.zeros(out.shape, F32)
        for slot, d_key in ((s0, d0), (s1, d1), (s2, d2), (s3, d3)):
            total += lax.dot_general(
                slot[:, at : at + half], d_key[...], TN, preferred_element_type=F32
            )
        out[...] = total.astype(out.dtype)


def final_kernel(parts, codes, out):
    total = jnp.sum(parts[...].astype(F32), axis=0)
    out[...] = jnp.where(keep_mask(codes[...], out.shape[0]), total, 0.0)


def doc_layout(lengths, row_total):
    doc_ends = jnp.cumsum(lengths, dtype=jnp.int32)
    positions = jnp.arange(row_total, dtype=jnp.int32)
    passed = positions[:, None] >= doc_ends[None, :]
    segment = jnp.sum(passed.astype(jnp.int32), axis=1, dtype=jnp.int32)
    begins = jnp.sum(jnp.where(passed, lengths[None, :], 0), axis=1, dtype=jnp.int32)
    return segment, positions - begins, segment < lengths.shape[0] - 1


def angles(doc_pos):
    exponent = jnp.arange(HEAD_DIM // 2, dtype=F32) * (2.0 / HEAD_DIM)
    phases = doc_pos.astype(F32)[:, None] * jnp.power(F32(ROPE_BASE), -exponent)
    cos, sin = jnp.cos(phases), jnp.sin(phases)
    return jnp.concatenate([cos, cos], axis=1), jnp.concatenate([-sin, sin], axis=1)


def call(kernel, out_shape, *args, at=None):
    specs = [pl.BlockSpec(memory_space=pltpu.VMEM)] * len(args)
    if at is not None:
        args, specs = (at,) + args, [pl.BlockSpec(memory_space=pltpu.SMEM)] + specs
    return pl.pallas_call(kernel, out_shape=out_shape, in_specs=specs, compiler_params=VMEM)(*args)


def shape(dims, kind=BF16):
    return jax.ShapeDtypeStruct(dims, kind)


def shifted(value, axis, by):
    size = lax.axis_size(axis)
    return lax.ppermute(value, axis, [(i, (i + by) % size) for i in range(size)])


def copies(value, count):
    return jnp.broadcast_to(value[None], (count,) + value.shape)


def after(value, *earlier):
    return lax.optimization_barrier((value,) + earlier)[0]


def shards(hidden, target, qw, kw, vw, ow, qc, kc, vc, oc, doc_lengths):
    tokens = hidden.shape[0]
    n_z, n_y, n_c, n_x = (lax.axis_size(a) for a in ("zl", "y", "c", "x"))
    y_at, c_at, zh_at, x_at = (lax.axis_index(a) for a in ("y", "c", "zh", "x"))
    at = jnp.stack([y_at, c_at, zh_at])
    rows, q_width = qw.shape
    width = q_width + 2 * kw.shape[1]
    heads = q_width // HEAD_DIM
    depth = n_z * n_c * rows

    mine = call(mask_qkv_kernel, shape((n_z, rows, width)), qw, kw, vw, qc, kc, vc)
    w_own = lax.all_to_all(mine, "zl", 0, 0)

    split = call(split_hidden_kernel, shape((n_y, tokens, depth)), hidden, at=at)
    slots = [split[0]] + [shifted(split[s], "y", s) for s in range(1, n_y)]
    w_own, *slots = lax.optimization_barrier((w_own, *slots))

    out_mine = call(mask_out_kernel, shape((ow.shape[1], ow.shape[0])), ow, oc)
    trade = []
    for z in range(n_z):
        for half in range(2):
            other = (z - 1 if half == 0 else z + 1) * 2 + 1 - half
            trade.append((z * 2 + half, other if z % 2 != half else z * 2 + half))
    out_mine = lax.ppermute(out_mine, ("zl", "zh"), trade)
    out_mine = after(out_mine, w_own)
    out_z = lax.all_to_all(copies(out_mine, n_z), "zl", 0, 0)

    w_oth = shifted(w_own, "c", 1)
    terms = call(
        project_kernel,
        [shape((tokens, width), F32)] + [shape((tokens, width))] * (n_y - 1),
        w_own.reshape(-1, width),
        w_oth.reshape(-1, width),
        *slots,
    )
    terms = [terms[0]] + [shifted(terms[s], "y", -s) for s in range(1, n_y)]

    out_z = after(out_z, *terms).reshape(n_z // 2, 2, ow.shape[1], ow.shape[0])
    out_y = [out_z] + [shifted(out_z, "y", s) for s in range(1, n_y)]
    pieces = []
    for piece in out_y:
        pieces += [piece, shifted(piece, "c", 1)]

    segment, doc_pos, live = doc_layout(doc_lengths[0], tokens)
    cos, sin = angles(doc_pos)
    spot = jnp.arange(tokens)
    allow = (segment[:, None] == segment[None, :]) & (spot[None, :] <= spot[:, None])
    queries, values, prob, att = call(
        attend_kernel,
        (
            shape((tokens, q_width)),
            shape((tokens, HEAD_DIM)),
            shape((heads, tokens, tokens), F32),
            shape((tokens, q_width)),
        ),
        *terms,
        cos,
        sin,
        allow.astype(F32),
    )

    att_oth = shifted(att, "zh", 1)
    block = target.shape[1] // (n_x * 2)
    part = call(out_kernel, shape((n_x, tokens, block)), att, att_oth, *pieces, at=at)
    blocks = lax.all_to_all(part, "x", 0, 0)
    target_share = lax.dynamic_slice_in_dim(target, (x_at * 2 + zh_at) * block, block, 1)
    block_out, error = call(
        error_kernel,
        (shape((tokens, block)), shape((n_x, tokens, block))),
        blocks,
        target_share,
        live[:, None].astype(F32),
        at=at,
    )
    errors = lax.all_to_all(error, "x", 0, 0)
    d_oth = call(functools.partial(d_att_kernel, 1), shape(att.shape), errors, *pieces, at=at)
    d_oth = shifted(d_oth, "zh", 1)
    d_own = call(functools.partial(d_att_kernel, 0), shape(att.shape, F32), errors, *pieces, at=at)

    d_key = call(
        key_grad_kernel, shape((tokens, HEAD_DIM)), d_own, d_oth, queries, values, prob, cos, sin
    )
    d_keys = [d_key] + [shifted(d_key, "y", s) for s in range(1, n_y)]
    half = (depth // 2, HEAD_DIM)
    g_own, g_oth = call(grad_kernel, (shape(half, F32), shape(half)), *slots, *d_keys)
    grad = (g_own + shifted(g_oth, "c", 1).astype(F32)).astype(BF16)
    grad = lax.all_to_all(grad.reshape(n_z, rows, HEAD_DIM), "zl", 0, 0)
    grad_key = call(final_kernel, shape((rows, HEAD_DIM), F32), grad, kc)
    return block_out, grad_key


def solution(mesh):
    fine = Mesh(mesh.devices.reshape(8, 4, 2, 4, 2), ("zl", "y", "c", "x", "zh"))
    dp, mp = ("zl", "y", "c"), ("x", "zh")
    by_dp, by_both, by_mp = P(dp, None), P(dp, mp), P(mp, dp)
    placed = (by_dp, by_dp) + (by_both,) * 3 + (by_mp,) + (by_both,) * 3 + (by_mp, by_dp)
    return jax.shard_map(
        shards, mesh=fine, in_specs=placed, out_specs=(by_both, by_both), check_vma=False
    )
```

time: 1210 us -> 300 us (0.25)
  the two profiles are of different devices: /device:TPU:4 before, /device:TPU:8 now
where the time goes in v1:
time: 300 us; the launch traced here: 299 us
  starting transfers between devices  93.3 us (31%)
  waiting for transfers between devices  91 us (30%)
  blocking collectives  58.6 us (20%)
  Pallas kernels  39.6 us (13%)
  local copies, waits for them, and re-layouts  11.3 us (4%)
  other arithmetic  4.08 us (1%)
    ppermute x20, waiting for transfers between devices, shifted(): lax.ppermute(value, axis, [(i, (i + by) % size) for i in range(size)])  74.1 us
    ppermute x20, starting transfers between devices, shifted(): lax.ppermute(value, axis, [(i, (i + by) % size) for i in range(size)])  67.5 us
    all_to_all x1, blocking collectives, shards(): grad = lax.all_to_all(grad.reshape(n_z, rows, HEAD_DIM), 'zl', 0, 0)  40.4 us
    pallas_call x12, Pallas kernels, call(): pl.pallas_call(kernel, out_shape=out_shape, in_specs=specs, compiler_para...  39.6 us
    all_to_all x1, blocking collectives, shards(): errors = lax.all_to_all(error, 'x', 0, 0)  18.2 us
    all_to_all x1, waiting for transfers between devices, shards(): blocks = lax.all_to_all(part, 'x', 0, 0)  13.2 us
    all_to_all x1, starting transfers between devices, shards(): w_own = lax.all_to_all(mine, 'zl', 0, 0)  12.5 us
    all_to_all x1, starting transfers between devices, shards(): out_z = lax.all_to_all(copies(out_mine, n_z), 'zl', 0, 0)  7.52 us
  transfers between devices with their start and end apart: 24, of which 17 were waited for; matrix products, arithmetic and copies ran while one was open for 3% of the time, Pallas kernels for 6%

profile of v1, /device:TPU:8, one launch (start us, length us, event | category | flops | bytes accessed | tf_op | source)
XLA Modules:
  0.0 298.9 jit_solution(15283217767865789303)
XLA Ops:
  2.8 12.5 %all-to-all-start = ((bf16[8,64,768]{2,1,0:T(8,128)(2,1)}), bf16[8,64,768]{2,1,0:T(8,128)(2,1)S(1)}, u32[]{:S(2)}, u32[]{:S(2)}) async-start(bf16[8,64,768]{2,1,0:T(8,128)(2,1)} %shard_map.122), calls=%async_computation | async-start | bytes 1572864 | tf_op jit(solution)/shard_map/all_to_all | solution.py:234
  15.9 4.0 %shard_map.123 = bf16[4,256,1024]{2,1,0:T(8,128)(2,1)} custom-call(s32[3]{0:T(128)} %pad_add_fusion.at_ref, bf16[256,4096]{1,0:T(8,128)(2,1)} %hidden.1), custom_call_target="tpu_custom_call" | custom-call | tf_op jit(solution)/shard_map/pallas_call | solution.py:203
  22.8 3.5 %collective-permute-start = (bf16[256,1024]{1,0:T(8,128)(2,1)}, bf16[256,1024]{1,0:T(8,128)(2,1)S(1)}, u32[]{:S(2)}, u32[]{:S(2)}) collective-permute-start(bf16[256,1024]{1,0:T(8,128)(2,1)} %get-tuple-element.44), channel_id=1, source_target_pairs={{0,16},{16,32},{32,48},{48,0},{1,17},{17,33},{33,49},{49,1},{2,18}... | collective-permute-start | bytes 1572872 | tf_op jit(solution)/shard_map/ppermute | solution.py:212
  29.2 4.3 %collective-permute-start.2 = (bf16[256,1024]{1,0:T(8,128)(2,1)}, bf16[256,1024]{1,0:T(8,128)(2,1)}, u32[]{:S(2)}, u32[]{:S(2)}) collective-permute-start(bf16[256,1024]{1,0:T(8,128)(2,1)} %get-tuple-element.42), channel_id=1, source_target_pairs={{0,48},{16,0},{32,16},{48,32},{1,49},{17,1},{33,17},{49,33},{2,50}... | collective-permute-start | bytes 1572872 | tf_op jit(solution)/shard_map/ppermute | solution.py:212
  39.8 5.1 %collective-permute-done.1.s2 = bf16[256,1024]{1,0:T(8,128)(2,1)} collective-permute-done((bf16[256,1024]{1,0:T(8,128)(2,1)}, bf16[256,1024]{1,0:T(8,128)(2,1)}, u32[]{:S(2)}, u32[]{:S(2)}) %collective-permute-start.1) | collective-permute-done | bytes 524320 | tf_op jit(solution)/shard_map/ppermute | solution.py:212
  44.9 9.4 %collective-permute-done.2.s3 = bf16[256,1024]{1,0:T(8,128)(2,1)} collective-permute-done((bf16[256,1024]{1,0:T(8,128)(2,1)}, bf16[256,1024]{1,0:T(8,128)(2,1)}, u32[]{:S(2)}, u32[]{:S(2)}) %collective-permute-start.2) | collective-permute-done | bytes 524320 | tf_op jit(solution)/shard_map/ppermute | solution.py:212
  54.4 3.7 %all-to-all-done = bf16[8,64,768]{2,1,0:T(8,128)(2,1)S(1)} async-done(((bf16[8,64,768]{2,1,0:T(8,128)(2,1)}), bf16[8,64,768]{2,1,0:T(8,128)(2,1)S(1)}, u32[]{:S(2)}, u32[]{:S(2)}) %all-to-all-start) | async-done | bytes 786464 | tf_op jit(solution)/shard_map/all_to_all | solution.py:234
  59.0 7.5 %all-to-all-start.1 = ((bf16[8,64,512]{2,1,0:T(8,128)(2,1)}), bf16[8,64,512]{2,1,0:T(8,128)(2,1)S(1)}, u32[]{:S(2)}, u32[]{:S(2)}) async-start(bf16[8,64,512]{2,1,0:T(8,128)(2,1)} %broadcast_in_dim.19), calls=%async_computation.1 | async-start | bytes 1048576 | tf_op jit(solution)/shard_map/all_to_all | solution.py:248
  71.6 4.7 %shard_map.124 = (f32[256,768]{1,0:T(8,128)}, bf16[256,768]{1,0:T(8,128)(2,1)}, bf16[256,768]{1,0:T(8,128)(2,1)}, bf16[256,768]{1,0:T(8,128)(2,1)}) custom-call(bf16[512,768]{1,0:T(8,128)(2,1)} %bitcast.26, bf16[512,768]{1,0:T(8,128)(2,1)} %bitcast.27, bf16[256,1024]{1,0:T(8,128)(2,1)} %get-tuple-element.22.s0, bf16[256,1024]{1,0:T(8,128)(2,1)} %copy-done.10, ...), custom_call_target="tpu_custom_call" | custom-call | tf_op jit(solution)/shard_map/pallas_call | solution.py:203
  78.6 4.5 %collective-permute-start.5 = (bf16[256,768]{1,0:T(8,128)(2,1)}, bf16[256,768]{1,0:T(8,128)(2,1)S(1)}, u32[]{:S(2)}, u32[]{:S(2)}) collective-permute-start(bf16[256,768]{1,0:T(8,128)(2,1)} %get-tuple-element.28), channel_id=1, source_target_pairs={{0,32},{16,48},{32,0},{48,16},{1,33},{17,49},{33,1},{49,17},{2,34}... | collective-permute-start | bytes 1179656 | tf_op jit(solution)/shard_map/ppermute | solution.py:212
  83.1 3.8 %collective-permute-start.6 = (bf16[256,768]{1,0:T(8,128)(2,1)}, bf16[256,768]{1,0:T(8,128)(2,1)}, u32[]{:S(2)}, u32[]{:S(2)}) collective-permute-start(bf16[256,768]{1,0:T(8,128)(2,1)} %get-tuple-element.29), channel_id=1, source_target_pairs={{0,16},{16,32},{32,48},{48,0},{1,17},{17,33},{33,49},{49,1},{2,18}... | collective-permute-start | bytes 1179656 | tf_op jit(solution)/shard_map/ppermute | solution.py:212
  89.5 9.4 %collective-permute-done.5.p2 = bf16[256,768]{1,0:T(8,128)(2,1)S(1)} collective-permute-done((bf16[256,768]{1,0:T(8,128)(2,1)}, bf16[256,768]{1,0:T(8,128)(2,1)S(1)}, u32[]{:S(2)}, u32[]{:S(2)}) %collective-permute-start.5) | collective-permute-done | bytes 393248 | tf_op jit(solution)/shard_map/ppermute | solution.py:212
  101.8 3.3 %collective-permute-start.10 = (bf16[4,2,64,512]{3,2,1,0:T(8,128)(2,1)S(1)}, bf16[4,2,64,512]{3,2,1,0:T(8,128)(2,1)S(1)}, u32[]{:S(2)}, u32[]{:S(2)}) collective-permute-start(bf16[4,2,64,512]{3,2,1,0:T(8,128)(2,1)S(1)} %bitcast.19), channel_id=1, source_target_pairs={{0,16},{16,32},{32,48},{48,0},{1,17},{17,33},{33,49},{49,1},{2,18}... | collective-permute-start | bytes 1572872 | tf_op jit(solution)/shard_map/ppermute | solution.py:212
  105.1 5.4 %collective-permute-start.12 = (bf16[4,2,64,512]{3,2,1,0:T(8,128)(2,1)S(1)}, bf16[4,2,64,512]{3,2,1,0:T(8,128)(2,1)S(1)}, u32[]{:S(2)}, u32[]{:S(2)}) collective-permute-start(bf16[4,2,64,512]{3,2,1,0:T(8,128)(2,1)S(1)} %bitcast.20), channel_id=1, source_target_pairs={{0,32},{16,48},{32,0},{48,16},{1,33},{17,49},{33,1},{49,17},{2,34}... | collective-permute-start | bytes 1572872 | tf_op jit(solution)/shard_map/ppermute | solution.py:212
  115.0 4.3 %collective-permute-done.10.refs_2_ = bf16[4,2,64,512]{3,2,1,0:T(8,128)(2,1)S(1)} collective-permute-done((bf16[4,2,64,512]{3,2,1,0:T(8,128)(2,1)S(1)}, bf16[4,2,64,512]{3,2,1,0:T(8,128)(2,1)S(1)}, u32[]{:S(2)}, u32[]{:S(2)}) %collective-permute-start.10) | collective-permute-done | bytes 524320 | tf_op jit(solution)/shard_map/ppermute | solution.py:212
  125.3 8.3 %collective-permute-done.14.refs_6_ = bf16[4,2,64,512]{3,2,1,0:T(8,128)(2,1)S(1)} collective-permute-done((bf16[4,2,64,512]{3,2,1,0:T(8,128)(2,1)S(1)}, bf16[4,2,64,512]{3,2,1,0:T(8,128)(2,1)S(1)}, u32[]{:S(2)}, u32[]{:S(2)}) %collective-permute-start.14) | collective-permute-done | bytes 524320 | tf_op jit(solution)/shard_map/ppermute | solution.py:212
  137.2 3.6 %shard_map.125 = (bf16[256,512]{1,0:T(8,128)(2,1)}, bf16[256,128]{1,0:T(8,128)(2,1)}, f32[4,256,256]{2,1,0:T(8,128)}, bf16[256,512]{1,0:T(8,128)(2,1)}) custom-call(f32[256,768]{1,0:T(8,128)} %get-tuple-element.26.p0, bf16[256,768]{1,0:T(8,128)(2,1)} %copy-done.12, bf16[256,768]{1,0:T(8,128)(2,1)} %copy-done.13, bf16[256,768]{1,0:T(8,128)(2,1)} %collective-permute-done.6.p3, ...), custom_call_target="tpu_custom_call" | custom-call | tf_op jit(solution)/shard_map/pallas_call | solution.py:203
  140.8 6.4 %collective-permute-start.7 = (bf16[256,512]{1,0:T(8,128)(2,1)}, bf16[256,512]{1,0:T(8,128)(2,1)S(1)}, u32[]{:S(2)}, u32[]{:S(2)}) collective-permute-start(bf16[256,512]{1,0:T(8,128)(2,1)} %get-tuple-element.30.own), channel_id=1, source_target_pairs={{0,1},{1,0},{2,3},{3,2},{4,5},{5,4},{6,7},{7,6},{8,9},{9,8},{10,11... | collective-permute-start | bytes 786440 | tf_op jit(solution)/shard_map/ppermute | solution.py:212
  147.1 13.6 %collective-permute-done.7.oth = bf16[256,512]{1,0:T(8,128)(2,1)S(1)} collective-permute-done((bf16[256,512]{1,0:T(8,128)(2,1)}, bf16[256,512]{1,0:T(8,128)(2,1)S(1)}, u32[]{:S(2)}, u32[]{:S(2)}) %collective-permute-start.7) | collective-permute-done | bytes 262176 | tf_op jit(solution)/shard_map/ppermute | solution.py:212
  162.0 4.6 %shard_map.127 = bf16[4,256,512]{2,1,0:T(8,128)(2,1)} custom-call(s32[3]{0:T(128)} %pad_add_fusion.at_ref, bf16[256,512]{1,0:T(8,128)(2,1)} %get-tuple-element.30.own, bf16[256,512]{1,0:T(8,128)(2,1)} %copy-done.15, bf16[4,2,64,512]{3,2,1,0:T(8,128)(2,1)} %bitcast.23, bf16[4,2,64,512]{3,2,1,0:T(8,128)(2,1)} %copy-done.5, bf16[4,2,64,512]{3,2,1,0:T(8,128)(2,1)} %copy-done.2, ...), custom_call_target="tpu_custom_call" | custom-call | tf_op jit(solution)/shard_map/pallas_call | solution.py:203
  166.6 4.3 %all-to-all-start.2 = ((bf16[4,256,512]{2,1,0:T(8,128)(2,1)}), bf16[4,256,512]{2,1,0:T(8,128)(2,1)S(1)}, u32[]{:S(2)}, u32[]{:S(2)}) async-start(bf16[4,256,512]{2,1,0:T(8,128)(2,1)} %shard_map.127), calls=%async_computation.2 | async-start | bytes 2097152 | tf_op jit(solution)/shard_map/all_to_all | solution.py:287
  172.4 13.2 %all-to-all-done.2.blocks = bf16[4,256,512]{2,1,0:T(8,128)(2,1)S(1)} async-done(((bf16[4,256,512]{2,1,0:T(8,128)(2,1)}), bf16[4,256,512]{2,1,0:T(8,128)(2,1)S(1)}, u32[]{:S(2)}, u32[]{:S(2)}) %all-to-all-start.2) | async-done | bytes 1048608 | tf_op jit(solution)/shard_map/all_to_all | solution.py:287
  189.4 18.2 %all_to_all.25.errors = bf16[4,256,512]{2,1,0:T(8,128)(2,1)} all-to-all(bf16[4,256,512]{2,1,0:T(8,128)(2,1)} %get-tuple-element.34), channel_id=1, replica_groups=mesh['zl'=8,'y'=4,'c'=2,'x'=4,'zh'=2] {'x'}, dimensions={0} | all-to-all | bytes 2097152 | tf_op jit(solution)/shard_map/all_to_all | solution.py:297
  207.5 3.9 %shard_map.130 = bf16[256,512]{1,0:T(8,128)(2,1)} custom-call(s32[3]{0:T(128)} %pad_add_fusion.at_ref, bf16[4,256,512]{2,1,0:T(8,128)(2,1)} %all_to_all.25.errors, bf16[4,2,64,512]{3,2,1,0:T(8,128)(2,1)} %bitcast.24, bf16[4,2,64,512]{3,2,1,0:T(8,128)(2,1)} %copy-done.5, bf16[4,2,64,512]{3,2,1,0:T(8,128)(2,1)} %copy-done.2, ...), custom_call_target="tpu_custom_call" | custom-call | tf_op jit(solution)/shard_map/pallas_call | solution.py:203
  211.4 6.0 %collective-permute-start.16 = (bf16[256,512]{1,0:T(8,128)(2,1)}, bf16[256,512]{1,0:T(8,128)(2,1)S(1)}, u32[]{:S(2)}, u32[]{:S(2)}) collective-permute-start(bf16[256,512]{1,0:T(8,128)(2,1)} %shard_map.130), channel_id=1, source_target_pairs={{0,1},{1,0},{2,3},{3,2},{4,5},{5,4},{6,7},{7,6},{8,9},{9,8},{10,11... | collective-permute-start | bytes 786440 | tf_op jit(solution)/shard_map/ppermute | solution.py:212
  217.5 4.0 %shard_map.129.d_own = f32[256,512]{1,0:T(8,128)} custom-call(s32[3]{0:T(128)} %pad_add_fusion.at_ref, bf16[4,256,512]{2,1,0:T(8,128)(2,1)} %all_to_all.25.errors, bf16[4,2,64,512]{3,2,1,0:T(8,128)(2,1)} %bitcast.25, bf16[4,2,64,512]{3,2,1,0:T(8,128)(2,1)} %copy-done.5, bf16[4,2,64,512]{3,2,1,0:T(8,128)(2,1)} %copy-done.2, ...), custom_call_target="tpu_custom_call" | custom-call | tf_op jit(solution)/shard_map/pallas_call | solution.py:203
  221.5 7.1 %collective-permute-done.16.d_other = bf16[256,512]{1,0:T(8,128)(2,1)S(1)} collective-permute-done((bf16[256,512]{1,0:T(8,128)(2,1)}, bf16[256,512]{1,0:T(8,128)(2,1)S(1)}, u32[]{:S(2)}, u32[]{:S(2)}) %collective-permute-start.16) | collective-permute-done | bytes 262176 | tf_op jit(solution)/shard_map/ppermute | solution.py:212
  229.3 3.4 %shard_map.131.d0 = bf16[256,128]{1,0:T(8,128)(2,1)} custom-call(f32[256,512]{1,0:T(8,128)} %shard_map.129.d_own, bf16[256,512]{1,0:T(8,128)(2,1)} %copy-done.14, bf16[256,512]{1,0:T(8,128)(2,1)} %get-tuple-element.35.q_ref, bf16[256,128]{1,0:T(8,128)(2,1)} %get-tuple-element.36.v_ref, f32[4,256,256]{2,1,0:T(8,128)} %get-tuple-element.37.prob_ref, ...), custom_call_target="tpu_custom_call" | custom-call | tf_op jit(solution)/shard_map/pallas_call | solution.py:203
  234.9 7.5 %collective-permute-start.18 = (bf16[256,128]{1,0:T(8,128)(2,1)}, bf16[256,128]{1,0:T(8,128)(2,1)S(1)}, u32[]{:S(2)}, u32[]{:S(2)}) collective-permute-start(bf16[256,128]{1,0:T(8,128)(2,1)} %shard_map.131.d0), channel_id=1, source_target_pairs={{0,32},{16,48},{32,0},{48,16},{1,33},{17,49},{33,1},{49,17},{2,34}... | collective-permute-start | bytes 196616 | tf_op jit(solution)/shard_map/ppermute | solution.py:212
  244.8 3.9 %collective-permute-done.19.d3 = bf16[256,128]{1,0:T(8,128)(2,1)S(1)} collective-permute-done((bf16[256,128]{1,0:T(8,128)(2,1)}, bf16[256,128]{1,0:T(8,128)(2,1)S(1)}, u32[]{:S(2)}, u32[]{:S(2)}) %collective-permute-start.19) | collective-permute-done | bytes 65568 | tf_op jit(solution)/shard_map/ppermute | solution.py:212
  249.4 3.0 %shard_map.132 = (f32[512,128]{1,0:T(8,128)}, bf16[512,128]{1,0:T(8,128)(2,1)}) custom-call(bf16[256,1024]{1,0:T(8,128)(2,1)} %get-tuple-element.22.s0, bf16[256,1024]{1,0:T(8,128)(2,1)} %copy-done.10, bf16[256,1024]{1,0:T(8,128)(2,1)} %collective-permute-done.1.s2, bf16[256,1024]{1,0:T(8,128)(2,1)} %collective-permute-done.2.s3, ...), custom_call_target="tpu_custom_call" | custom-call | tf_op jit(solution)/shard_map/pallas_call | solution.py:203
  256.8 40.4 %all_to_all.26.parts = bf16[8,64,128]{2,1,0:T(8,128)(2,1)} all-to-all(bf16[8,64,128]{2,1,0:T(8,128)(2,1)S(1)} %bitcast.28), channel_id=1, replica_groups=mesh['zl'=8,'y'=4,'c'=2,'x'=4,'zh'=2] {'zl'}, dimensions={0} | all-to-all | bytes 262144 | tf_op jit(solution)/shard_map/all_to_all | solution.py:309
  (90 shorter events, 61.0 us)
Async XLA Ops:
  0.6 171.0 %copy-start = (bf16[256,4096]{1,0:T(8,128)(2,1)S(1)}, bf16[256,4096]{1,0:T(8,128)(2,1)}, u32[]{:S(2)}) copy-start(bf16[256,4096]{1,0:T(8,128)(2,1)} %param.12) | copy-start | bytes 6291460
  2.8 55.3 %all-to-all-start = ((bf16[8,64,768]{2,1,0:T(8,128)(2,1)}), bf16[8,64,768]{2,1,0:T(8,128)(2,1)S(1)}, u32[]{:S(2)}, u32[]{:S(2)}) async-start(bf16[8,64,768]{2,1,0:T(8,128)(2,1)} %shard_map.122), calls=%async_computation | async-start | bytes 1572864 | tf_op jit(solution)/shard_map/all_to_all | solution.py:234
  22.8 16.9 %collective-permute-start = (bf16[256,1024]{1,0:T(8,128)(2,1)}, bf16[256,1024]{1,0:T(8,128)(2,1)S(1)}, u32[]{:S(2)}, u32[]{:S(2)}) collective-permute-start(bf16[256,1024]{1,0:T(8,128)(2,1)} %get-tuple-element.44), channel_id=1, source_target_pairs={{0,16},{16,32},{32,48},{48,0},{1,17},{17,33},{33,49},{49,1},{2,18}... | collective-permute-start | bytes 1572872 | tf_op jit(solution)/shard_map/ppermute | solution.py:212
  26.3 18.6 %collective-permute-start.1 = (bf16[256,1024]{1,0:T(8,128)(2,1)}, bf16[256,1024]{1,0:T(8,128)(2,1)}, u32[]{:S(2)}, u32[]{:S(2)}) collective-permute-start(bf16[256,1024]{1,0:T(8,128)(2,1)} %get-tuple-element.43), channel_id=1, source_target_pairs={{0,32},{16,48},{32,0},{48,16},{1,33},{17,49},{33,1},{49,17},{2,34}... | collective-permute-start | bytes 1572872 | tf_op jit(solution)/shard_map/ppermute | solution.py:212
  29.2 25.2 %collective-permute-start.2 = (bf16[256,1024]{1,0:T(8,128)(2,1)}, bf16[256,1024]{1,0:T(8,128)(2,1)}, u32[]{:S(2)}, u32[]{:S(2)}) collective-permute-start(bf16[256,1024]{1,0:T(8,128)(2,1)} %get-tuple-element.42), channel_id=1, source_target_pairs={{0,48},{16,0},{32,16},{48,32},{1,49},{17,1},{33,17},{49,33},{2,50}... | collective-permute-start | bytes 1572872 | tf_op jit(solution)/shard_map/ppermute | solution.py:212
  36.9 21.2 %collective-permute-start.8 = (bf16[64,512]{1,0:T(8,128)(2,1)}, bf16[64,512]{1,0:T(8,128)(2,1)S(1)}, u32[]{:S(2)}, u32[]{:S(2)}) collective-permute-start(bf16[64,512]{1,0:T(8,128)(2,1)} %shard_map.126), channel_id=1, source_target_pairs={{0,0},{1,64},{64,1},{65,65},{128,128},{129,192},{192,129},{193,193... | collective-permute-start | bytes 196616 | tf_op jit(solution)/shard_map/ppermute | solution.py:246
  59.0 42.8 %all-to-all-start.1 = ((bf16[8,64,512]{2,1,0:T(8,128)(2,1)}), bf16[8,64,512]{2,1,0:T(8,128)(2,1)S(1)}, u32[]{:S(2)}, u32[]{:S(2)}) async-start(bf16[8,64,512]{2,1,0:T(8,128)(2,1)} %broadcast_in_dim.19), calls=%async_computation.1 | async-start | bytes 1048576 | tf_op jit(solution)/shard_map/all_to_all | solution.py:248
  66.5 20.4 %copy-start.21 = (s32[1,3]{1,0:T(1,128)S(1)}, s32[1,3]{1,0:T(1,128)}, u32[]{:S(2)}) copy-start(s32[1,3]{1,0:T(1,128)} %param.21) | copy-start | bytes 40
  66.5 4.2 %collective-permute-start.3 = (bf16[8,64,768]{2,1,0:T(8,128)(2,1)S(1)}, bf16[8,64,768]{2,1,0:T(8,128)(2,1)S(1)}, u32[]{:S(2)}, u32[]{:S(2)}) collective-permute-start(bf16[8,64,768]{2,1,0:T(8,128)(2,1)S(1)} %all-to-all-done), channel_id=1, source_target_pairs={{0,8},{8,0},{1,9},{9,1},{2,10},{10,2},{3,11},{11,3},{4,12},{12,4},... | collective-permute-start | bytes 2359304 | tf_op jit(solution)/shard_map/ppermute | solution.py:212
  76.2 13.2 %collective-permute-start.4 = (bf16[256,768]{1,0:T(8,128)(2,1)}, bf16[256,768]{1,0:T(8,128)(2,1)S(1)}, u32[]{:S(2)}, u32[]{:S(2)}) collective-permute-start(bf16[256,768]{1,0:T(8,128)(2,1)} %get-tuple-element.27), channel_id=1, source_target_pairs={{0,48},{16,0},{32,16},{48,32},{1,49},{17,1},{33,17},{49,33},{2,50}... | collective-permute-start | bytes 1179656 | tf_op jit(solution)/shard_map/ppermute | solution.py:212
  78.6 20.3 %collective-permute-start.5 = (bf16[256,768]{1,0:T(8,128)(2,1)}, bf16[256,768]{1,0:T(8,128)(2,1)S(1)}, u32[]{:S(2)}, u32[]{:S(2)}) collective-permute-start(bf16[256,768]{1,0:T(8,128)(2,1)} %get-tuple-element.28), channel_id=1, source_target_pairs={{0,32},{16,48},{32,0},{48,16},{1,33},{17,49},{33,1},{49,17},{2,34}... | collective-permute-start | bytes 1179656 | tf_op jit(solution)/shard_map/ppermute | solution.py:212
  83.1 18.7 %collective-permute-start.6 = (bf16[256,768]{1,0:T(8,128)(2,1)}, bf16[256,768]{1,0:T(8,128)(2,1)}, u32[]{:S(2)}, u32[]{:S(2)}) collective-permute-start(bf16[256,768]{1,0:T(8,128)(2,1)} %get-tuple-element.29), channel_id=1, source_target_pairs={{0,16},{16,32},{32,48},{48,0},{1,17},{17,33},{33,49},{49,1},{2,18}... | collective-permute-start | bytes 1179656 | tf_op jit(solution)/shard_map/ppermute | solution.py:212
  89.5 47.7 %copy-start.12 = (bf16[256,768]{1,0:T(8,128)(2,1)}, bf16[256,768]{1,0:T(8,128)(2,1)S(1)}, u32[]{:S(2)}) copy-start(bf16[256,768]{1,0:T(8,128)(2,1)S(1)} %collective-permute-done.4.p1) | copy-start | bytes 1179652
  98.9 22.2 %copy-start.13 = (bf16[256,768]{1,0:T(8,128)(2,1)}, bf16[256,768]{1,0:T(8,128)(2,1)S(1)}, u32[]{:S(2)}) copy-start(bf16[256,768]{1,0:T(8,128)(2,1)S(1)} %collective-permute-done.5.p2) | copy-start | bytes 1179652
  101.8 59.0 %copy-start.1 = (bf16[8,64,512]{2,1,0:T(8,128)(2,1)}, bf16[8,64,512]{2,1,0:T(8,128)(2,1)S(1)}, u32[]{:S(2)}) copy-start(bf16[8,64,512]{2,1,0:T(8,128)(2,1)S(1)} %all-to-all-done.1) | copy-start | bytes 1572868
  101.8 17.5 %collective-permute-start.10 = (bf16[4,2,64,512]{3,2,1,0:T(8,128)(2,1)S(1)}, bf16[4,2,64,512]{3,2,1,0:T(8,128)(2,1)S(1)}, u32[]{:S(2)}, u32[]{:S(2)}) collective-permute-start(bf16[4,2,64,512]{3,2,1,0:T(8,128)(2,1)S(1)} %bitcast.19), channel_id=1, source_target_pairs={{0,16},{16,32},{32,48},{48,0},{1,17},{17,33},{33,49},{49,1},{2,18}... | collective-permute-start | bytes 1572872 | tf_op jit(solution)/shard_map/ppermute | solution.py:212
  105.1 18.2 %collective-permute-start.12 = (bf16[4,2,64,512]{3,2,1,0:T(8,128)(2,1)S(1)}, bf16[4,2,64,512]{3,2,1,0:T(8,128)(2,1)S(1)}, u32[]{:S(2)}, u32[]{:S(2)}) collective-permute-start(bf16[4,2,64,512]{3,2,1,0:T(8,128)(2,1)S(1)} %bitcast.20), channel_id=1, source_target_pairs={{0,32},{16,48},{32,0},{48,16},{1,33},{17,49},{33,1},{49,17},{2,34}... | collective-permute-start | bytes 1572872 | tf_op jit(solution)/shard_map/ppermute | solution.py:212
  110.5 23.0 %collective-permute-start.14 = (bf16[4,2,64,512]{3,2,1,0:T(8,128)(2,1)S(1)}, bf16[4,2,64,512]{3,2,1,0:T(8,128)(2,1)S(1)}, u32[]{:S(2)}, u32[]{:S(2)}) collective-permute-start(bf16[4,2,64,512]{3,2,1,0:T(8,128)(2,1)S(1)} %bitcast.21), channel_id=1, source_target_pairs={{0,48},{16,0},{32,16},{48,32},{1,49},{17,1},{33,17},{49,33},{2,50}... | collective-permute-start | bytes 1572872 | tf_op jit(solution)/shard_map/ppermute | solution.py:212
  113.0 47.7 %collective-permute-start.9 = (bf16[4,2,64,512]{3,2,1,0:T(8,128)(2,1)S(1)}, bf16[4,2,64,512]{3,2,1,0:T(8,128)(2,1)S(1)}, u32[]{:S(2)}, u32[]{:S(2)}) collective-permute-start(bf16[4,2,64,512]{3,2,1,0:T(8,128)(2,1)S(1)} %bitcast.22), channel_id=1, source_target_pairs={{0,8},{8,0},{1,9},{9,1},{2,10},{10,2},{3,11},{11,3},{4,12},{12,4},... | collective-permute-start | bytes 1572872 | tf_op jit(solution)/shard_map/ppermute | solution.py:212
  119.3 41.5 %copy-start.2 = (bf16[4,2,64,512]{3,2,1,0:T(8,128)(2,1)}, bf16[4,2,64,512]{3,2,1,0:T(8,128)(2,1)S(1)}, u32[]{:S(2)}) copy-start(bf16[4,2,64,512]{3,2,1,0:T(8,128)(2,1)S(1)} %collective-permute-done.10.refs_2_) | copy-start | bytes 1572868
  119.3 41.5 %collective-permute-start.11 = (bf16[4,2,64,512]{3,2,1,0:T(8,128)(2,1)S(1)}, bf16[4,2,64,512]{3,2,1,0:T(8,128)(2,1)S(1)}, u32[]{:S(2)}, u32[]{:S(2)}) collective-permute-start(bf16[4,2,64,512]{3,2,1,0:T(8,128)(2,1)S(1)} %collective-permute-done.10.refs_2_), channel_id=1, source_target_pairs={{0,8},{8,0},{1,9},{9,1},{2,10},{10,2},{3,11},{11,3},{4,12},{12,4},... | collective-permute-start | bytes 1572872 | tf_op jit(solution)/shard_map/ppermute | solution.py:212
  123.3 37.5 %copy-start.3 = (bf16[4,2,64,512]{3,2,1,0:T(8,128)(2,1)}, bf16[4,2,64,512]{3,2,1,0:T(8,128)(2,1)S(1)}, u32[]{:S(2)}) copy-start(bf16[4,2,64,512]{3,2,1,0:T(8,128)(2,1)S(1)} %collective-permute-done.12.refs_4_) | copy-start | bytes 1572868
  123.3 37.4 %collective-permute-start.13 = (bf16[4,2,64,512]{3,2,1,0:T(8,128)(2,1)S(1)}, bf16[4,2,64,512]{3,2,1,0:T(8,128)(2,1)S(1)}, u32[]{:S(2)}, u32[]{:S(2)}) collective-permute-start(bf16[4,2,64,512]{3,2,1,0:T(8,128)(2,1)S(1)} %collective-permute-done.12.refs_4_), channel_id=1, source_target_pairs={{0,8},{8,0},{1,9},{9,1},{2,10},{10,2},{3,11},{11,3},{4,12},{12,4},... | collective-permute-start | bytes 1572872 | tf_op jit(solution)/shard_map/ppermute | solution.py:212
  133.6 27.2 %copy-start.4 = (bf16[4,2,64,512]{3,2,1,0:T(8,128)(2,1)}, bf16[4,2,64,512]{3,2,1,0:T(8,128)(2,1)S(1)}, u32[]{:S(2)}) copy-start(bf16[4,2,64,512]{3,2,1,0:T(8,128)(2,1)S(1)} %collective-permute-done.14.refs_6_) | copy-start | bytes 1572868
  133.6 27.2 %collective-permute-start.15 = (bf16[4,2,64,512]{3,2,1,0:T(8,128)(2,1)S(1)}, bf16[4,2,64,512]{3,2,1,0:T(8,128)(2,1)}, u32[]{:S(2)}, u32[]{:S(2)}) collective-permute-start(bf16[4,2,64,512]{3,2,1,0:T(8,128)(2,1)S(1)} %collective-permute-done.14.refs_6_), channel_id=1, source_target_pairs={{0,8},{8,0},{1,9},{9,1},{2,10},{10,2},{3,11},{11,3},{4,12},{12,4},... | collective-permute-start | bytes 1572872 | tf_op jit(solution)/shard_map/ppermute | solution.py:212
  140.8 19.9 %collective-permute-start.7 = (bf16[256,512]{1,0:T(8,128)(2,1)}, bf16[256,512]{1,0:T(8,128)(2,1)S(1)}, u32[]{:S(2)}, u32[]{:S(2)}) collective-permute-start(bf16[256,512]{1,0:T(8,128)(2,1)} %get-tuple-element.30.own), channel_id=1, source_target_pairs={{0,1},{1,0},{2,3},{3,2},{4,5},{5,4},{6,7},{7,6},{8,9},{9,8},{10,11... | collective-permute-start | bytes 786440 | tf_op jit(solution)/shard_map/ppermute | solution.py:212
  166.6 19.1 %all-to-all-start.2 = ((bf16[4,256,512]{2,1,0:T(8,128)(2,1)}), bf16[4,256,512]{2,1,0:T(8,128)(2,1)S(1)}, u32[]{:S(2)}, u32[]{:S(2)}) async-start(bf16[4,256,512]{2,1,0:T(8,128)(2,1)} %shard_map.127), calls=%async_computation.2 | async-start | bytes 2097152 | tf_op jit(solution)/shard_map/all_to_all | solution.py:287
  211.4 17.2 %collective-permute-start.16 = (bf16[256,512]{1,0:T(8,128)(2,1)}, bf16[256,512]{1,0:T(8,128)(2,1)S(1)}, u32[]{:S(2)}, u32[]{:S(2)}) collective-permute-start(bf16[256,512]{1,0:T(8,128)(2,1)} %shard_map.130), channel_id=1, source_target_pairs={{0,1},{1,0},{2,3},{3,2},{4,5},{5,4},{6,7},{7,6},{8,9},{9,8},{10,11... | collective-permute-start | bytes 786440 | tf_op jit(solution)/shard_map/ppermute | solution.py:212
  232.7 11.7 %collective-permute-start.17 = (bf16[256,128]{1,0:T(8,128)(2,1)}, bf16[256,128]{1,0:T(8,128)(2,1)S(1)}, u32[]{:S(2)}, u32[]{:S(2)}) collective-permute-start(bf16[256,128]{1,0:T(8,128)(2,1)} %shard_map.131.d0), channel_id=1, source_target_pairs={{0,16},{16,32},{32,48},{48,0},{1,17},{17,33},{33,49},{49,1},{2,18}... | collective-permute-start | bytes 196616 | tf_op jit(solution)/shard_map/ppermute | solution.py:212
  234.9 9.9 %collective-permute-start.18 = (bf16[256,128]{1,0:T(8,128)(2,1)}, bf16[256,128]{1,0:T(8,128)(2,1)S(1)}, u32[]{:S(2)}, u32[]{:S(2)}) collective-permute-start(bf16[256,128]{1,0:T(8,128)(2,1)} %shard_map.131.d0), channel_id=1, source_target_pairs={{0,32},{16,48},{32,0},{48,16},{1,33},{17,49},{33,1},{49,17},{2,34}... | collective-permute-start | bytes 196616 | tf_op jit(solution)/shard_map/ppermute | solution.py:212
  242.4 6.4 %collective-permute-start.19 = (bf16[256,128]{1,0:T(8,128)(2,1)}, bf16[256,128]{1,0:T(8,128)(2,1)S(1)}, u32[]{:S(2)}, u32[]{:S(2)}) collective-permute-start(bf16[256,128]{1,0:T(8,128)(2,1)} %shard_map.131.d0), channel_id=1, source_target_pairs={{0,48},{16,0},{32,16},{48,32},{1,49},{17,1},{33,17},{49,33},{2,50}... | collective-permute-start | bytes 196616 | tf_op jit(solution)/shard_map/ppermute | solution.py:212
  252.4 3.4 %collective-permute-start.20 = (bf16[512,128]{1,0:T(8,128)(2,1)}, bf16[512,128]{1,0:T(8,128)(2,1)S(1)}, u32[]{:S(2)}, u32[]{:S(2)}) collective-permute-start(bf16[512,128]{1,0:T(8,128)(2,1)} %get-tuple-element.39), channel_id=1, source_target_pairs={{0,8},{8,0},{1,9},{9,1},{2,10},{10,2},{3,11},{11,3},{4,12},{12,4},... | collective-permute-start | bytes 393224 | tf_op jit(solution)/shard_map/ppermute | solution.py:212
  (14 other events, 75.1 us)

commit v2 on v1

--- a/solution.py
+++ b/solution.py
@@ -11,7 +11,7 @@
 LOSS_DIV = 16
 ROPE_BASE = 500000.0
 KEEP_BITS = (0b000111, 0b011001, 0b101010, 0b110100)
-VMEM = pltpu.CompilerParams(vmem_limit_bytes=58 * 1024 * 1024)
+MIB = 1024 * 1024
 F32 = jnp.float32
 BF16 = jnp.bfloat16
 NT = (((1,), (1,)), ((), ()))
@@ -57,12 +57,13 @@
     out[...] = lax.dot_general(eye, kept, NT, preferred_element_type=F32).astype(BF16)
 
 
-def split_hidden_kernel(at_ref, hidden, out):
-    shifts, tokens, width = out.shape
+def split_hidden_kernel(at_ref, hidden, *outs):
+    shifts = len(outs)
+    tokens, width = outs[0].shape
     n_z = width // 128
     half = width // 2
     low = lax.broadcasted_iota(jnp.int32, (tokens, 128), 1) < 64
-    own = low == (at_ref[1] == 0)
+    own = low == (at_ref[2] == 0)
     for shift in range(shifts):
         y_to = lax.rem(at_ref[0] + shift, shifts)
         for pair in range(n_z // 2):
@@ -74,7 +75,7 @@
             rest = [jnp.where(own, pltpu.roll(v, 64, 1), v) for v in both]
             for part, (first, last) in enumerate((mine, rest)):
                 start = part * half + pair * 128
-                out[shift, :, start : start + 128] = jnp.where(low, first, last).astype(BF16)
+                outs[shift][:, start : start + 128] = jnp.where(low, first, last).astype(BF16)
 
 
 def rotate(values, cos, sin):
@@ -111,7 +112,7 @@
 
 def key_grad_kernel(d_own, d_other, q_ref, v_ref, prob_ref, cos, sin, out):
     d_att = (d_own[...] + d_other[...].astype(F32)).astype(BF16)
-    total = jnp.zeros(out.shape, F32)
+    total = jnp.zeros(out.shape[1:], F32)
     for head in range(prob_ref.shape[0]):
         cut = slice(head * HEAD_DIM, (head + 1) * HEAD_DIM)
         d_prob = lax.dot_general(d_att[:, cut], v_ref[...], NT, preferred_element_type=F32)
@@ -119,59 +120,47 @@
         row_dot = jnp.sum(prob * d_prob, axis=1, keepdims=True)
         d_score = (prob * (d_prob - row_dot) * HEAD_DIM**-0.5).astype(BF16)
         total += lax.dot_general(d_score, q_ref[:, cut], TN, preferred_element_type=F32)
-    out[...] = rotate(total, cos[...], -sin[...]).astype(BF16)
-
-
-def out_block(pieces, k, r):
-    return jnp.concatenate([piece[k, r] for piece in pieces], axis=0)
-
-
-def out_kernel(at_ref, own, oth, *refs):
-    pieces, out = refs[:-1], refs[-1]
-    zh = at_ref[2]
+    d_key = rotate(total, cos[...], -sin[...]).astype(BF16)
+    for copy in range(out.shape[0]):
+        out[copy] = d_key
+
+
+def out_block(weight, k, r):
+    return jnp.concatenate([weight[part, k, r] for part in range(weight.shape[0])], axis=0)
+
+
+def out_kernel(at_ref, own, oth, weight, out):
+    zh = at_ref[1]
     for k in range(out.shape[0]):
-        total = lax.dot_general(own[...], out_block(pieces, k, zh), NT, preferred_element_type=F32)
-        total += lax.dot_general(
-            oth[...], out_block(pieces, k, 1 - zh), NT, preferred_element_type=F32
-        )
+        total = lax.dot_general(own[...], out_block(weight, k, zh), NT, preferred_element_type=F32)
+        total += lax.dot_general(oth[...], out_block(weight, k, 1 - zh), NT, preferred_element_type=F32)
         out[k] = total.astype(out.dtype)
 
 
-def d_att_kernel(which, at_ref, errors, *refs):
-    pieces, out = refs[:-1], refs[-1]
-    r = at_ref[2] if which == 0 else 1 - at_ref[2]
+def d_att_kernel(which, at_ref, errors, weight, out):
+    r = at_ref[1] if which == 0 else 1 - at_ref[1]
     total = jnp.zeros(out.shape, F32)
     for k in range(errors.shape[0]):
-        total += jnp.dot(errors[k], out_block(pieces, k, r), preferred_element_type=F32)
+        total += jnp.dot(errors[k], out_block(weight, k, r), preferred_element_type=F32)
     out[...] = total.astype(out.dtype)
 
 
-def error_kernel(at_ref, blocks, target, live, block_out, errors):
-    tokens = target.shape[0]
-    n_y = target.shape[1] // 128
-    swap = at_ref[1] == 1
-    for shift in range(n_y):
-        y_from = lax.rem(at_ref[0] + n_y - shift, n_y)
-        lane = pl.multiple_of(y_from * 128, 128)
-        cut = slice(shift * 128, (shift + 1) * 128)
-        total = jnp.sum(blocks[:, :, cut].astype(F32), axis=0)
-        placed = jnp.where(swap, pltpu.roll(total, 64, 1), total)
-        block_out[:, pl.ds(lane, 128)] = placed.astype(BF16)
-        want = target[:, pl.ds(lane, 128)].astype(F32)
-        want = jnp.where(swap, pltpu.roll(want, 64, 1), want)
-        error = ((total - want) * live[...] / LOSS_DIV).astype(BF16)
-        for k in range(errors.shape[0]):
-            errors[k, :, cut] = error
-
-
-def grad_kernel(s0, s1, s2, s3, d0, d1, d2, d3, own, oth):
+def error_kernel(blocks, target, live, block_out, errors):
+    total = jnp.sum(blocks[...].astype(F32), axis=0)
+    block_out[...] = total.astype(BF16)
+    error = ((total - target[...].astype(F32)) * live[...] / LOSS_DIV).astype(BF16)
+    for k in range(errors.shape[0]):
+        errors[k] = error
+
+
+def grad_kernel(at_ref, s0, s1, s2, s3, d_keys, own, oth):
     half = own.shape[0]
-    for at, out in ((0, own), (half, oth)):
+    n_y = d_keys.shape[0]
+    for at, out in ((half, oth), (0, own)):
         total = jnp.zeros(out.shape, F32)
-        for slot, d_key in ((s0, d0), (s1, d1), (s2, d2), (s3, d3)):
-            total += lax.dot_general(
-                slot[:, at : at + half], d_key[...], TN, preferred_element_type=F32
-            )
+        for shift, slot in enumerate((s0, s1, s2, s3)):
+            d_key = d_keys[lax.rem(at_ref[0] + n_y - shift, n_y)]
+            total += lax.dot_general(slot[:, at : at + half], d_key, TN, preferred_element_type=F32)
         out[...] = total.astype(out.dtype)
 
 
@@ -196,11 +185,15 @@
     return jnp.concatenate([cos, cos], axis=1), jnp.concatenate([-sin, sin], axis=1)
 
 
-def call(kernel, out_shape, *args, at=None):
+def call(kernel, out_shape, *args, at=None, mib=20, flops=None):
     specs = [pl.BlockSpec(memory_space=pltpu.VMEM)] * len(args)
     if at is not None:
         args, specs = (at,) + args, [pl.BlockSpec(memory_space=pltpu.SMEM)] + specs
-    return pl.pallas_call(kernel, out_shape=out_shape, in_specs=specs, compiler_params=VMEM)(*args)
+    params = pltpu.CompilerParams(vmem_limit_bytes=mib * MIB)
+    cost = flops and pl.CostEstimate(flops=flops, bytes_accessed=0, transcendentals=0)
+    return pl.pallas_call(
+        kernel, out_shape=out_shape, in_specs=specs, compiler_params=params, cost_estimate=cost
+    )(*args)
 
 
 def shape(dims, kind=BF16):
@@ -224,16 +217,16 @@
     tokens = hidden.shape[0]
     n_z, n_y, n_c, n_x = (lax.axis_size(a) for a in ("zl", "y", "c", "x"))
     y_at, c_at, zh_at, x_at = (lax.axis_index(a) for a in ("y", "c", "zh", "x"))
-    at = jnp.stack([y_at, c_at, zh_at])
+    at = jnp.stack([y_at, zh_at, c_at])
     rows, q_width = qw.shape
     width = q_width + 2 * kw.shape[1]
     heads = q_width // HEAD_DIM
     depth = n_z * n_c * rows
 
-    mine = call(mask_qkv_kernel, shape((n_z, rows, width)), qw, kw, vw, qc, kc, vc)
+    mine = call(mask_qkv_kernel, shape((n_z, rows, width)), qw, kw, vw, qc, kc, vc, mib=58)
     w_own = lax.all_to_all(mine, "zl", 0, 0)
 
-    split = call(split_hidden_kernel, shape((n_y, tokens, depth)), hidden, at=at)
+    split = call(split_hidden_kernel, [shape((tokens, depth))] * n_y, hidden, at=at)
     slots = [split[0]] + [shifted(split[s], "y", s) for s in range(1, n_y)]
     w_own, *slots = lax.optimization_barrier((w_own, *slots))
 
@@ -258,10 +251,7 @@
     terms = [terms[0]] + [shifted(terms[s], "y", -s) for s in range(1, n_y)]
 
     out_z = after(out_z, *terms).reshape(n_z // 2, 2, ow.shape[1], ow.shape[0])
-    out_y = [out_z] + [shifted(out_z, "y", s) for s in range(1, n_y)]
-    pieces = []
-    for piece in out_y:
-        pieces += [piece, shifted(piece, "c", 1)]
+    out_w = lax.all_gather(out_z, ("y", "c"), axis=0)
 
     segment, doc_pos, live = doc_layout(doc_lengths[0], tokens)
     cos, sin = angles(doc_pos)
@@ -279,11 +269,12 @@
         cos,
         sin,
         allow.astype(F32),
+        mib=58,
     )
 
     att_oth = shifted(att, "zh", 1)
     block = target.shape[1] // (n_x * 2)
-    part = call(out_kernel, shape((n_x, tokens, block)), att, att_oth, *pieces, at=at)
+    part = call(out_kernel, shape((n_x, tokens, block)), att, att_oth, out_w, at=at)
     blocks = lax.all_to_all(part, "x", 0, 0)
     target_share = lax.dynamic_slice_in_dim(target, (x_at * 2 + zh_at) * block, block, 1)
     block_out, error = call(
@@ -292,19 +283,18 @@
         blocks,
         target_share,
         live[:, None].astype(F32),
-        at=at,
     )
     errors = lax.all_to_all(error, "x", 0, 0)
-    d_oth = call(functools.partial(d_att_kernel, 1), shape(att.shape), errors, *pieces, at=at)
+    d_oth = call(functools.partial(d_att_kernel, 1), shape(att.shape), errors, out_w, at=at)
     d_oth = shifted(d_oth, "zh", 1)
-    d_own = call(functools.partial(d_att_kernel, 0), shape(att.shape, F32), errors, *pieces, at=at)
+    d_own = call(functools.partial(d_att_kernel, 0), shape(att.shape, F32), errors, out_w, at=at)
 
     d_key = call(
-        key_grad_kernel, shape((tokens, HEAD_DIM)), d_own, d_oth, queries, values, prob, cos, sin
-    )
-    d_keys = [d_key] + [shifted(d_key, "y", s) for s in range(1, n_y)]
+        key_grad_kernel, shape((n_y, tokens, HEAD_DIM)), d_own, d_oth, queries, values, prob, cos, sin
+    )
+    d_keys = lax.all_to_all(d_key, "y", 0, 0)
     half = (depth // 2, HEAD_DIM)
-    g_own, g_oth = call(grad_kernel, (shape(half, F32), shape(half)), *slots, *d_keys)
+    g_own, g_oth = call(grad_kernel, (shape(half, F32), shape(half)), *slots, d_keys, at=at)
     grad = (g_own + shifted(g_oth, "c", 1).astype(F32)).astype(BF16)
     grad = lax.all_to_all(grad.reshape(n_z, rows, HEAD_DIM), "zl", 0, 0)
     grad_key = call(final_kernel, shape((rows, HEAD_DIM), F32), grad, kc)

time: 300 us -> 273 us (0.910)
  the two profiles are of different devices: /device:TPU:8 before, /device:TPU:32 now
where the time goes in v2:
time: 273 us; the launch traced here: 272 us
  waiting for transfers between devices  86.9 us (32%)
  starting transfers between devices  76.4 us (28%)
  blocking collectives  56.5 us (21%)
  Pallas kernels  21.6 us (8%)
  between operations  14.4 us (5%)
  local copies, waits for them, and re-layouts  13.2 us (5%)
    ppermute x10, waiting for transfers between devices, shifted(): lax.ppermute(value, axis, [(i, (i + by) % size) for i in range(size)])  61.8 us
    ppermute x10, starting transfers between devices, shifted(): lax.ppermute(value, axis, [(i, (i + by) % size) for i in range(size)])  42.7 us
    all_to_all x1, blocking collectives, shards(): grad = lax.all_to_all(grad.reshape(n_z, rows, HEAD_DIM), 'zl', 0, 0)  25.2 us
    pallas_call x12, Pallas kernels, call(): pl.pallas_call(kernel, out_shape=out_shape, in_specs=specs, compiler_para...  21.6 us
    all_to_all x1, blocking collectives, shards(): errors = lax.all_to_all(error, 'x', 0, 0)  17.1 us
    all_to_all x1, waiting for transfers between devices, shards(): blocks = lax.all_to_all(part, 'x', 0, 0)  15.3 us
    all_to_all x1, blocking collectives, shards(): d_keys = lax.all_to_all(d_key, 'y', 0, 0)  14.3 us
    all_to_all x1, starting transfers between devices, shards(): w_own = lax.all_to_all(mine, 'zl', 0, 0)  12.6 us
  transfers between devices with their start and end apart: 15, of which 11 were waited for; matrix products, arithmetic and copies ran while one was open for 2% of the time, Pallas kernels for 4%

profile of v2, /device:TPU:32, one launch (start us, length us, event | category | flops | bytes accessed | tf_op | source)
XLA Modules:
  0.0 271.5 jit_solution(16147072814297144038)
XLA Ops:
  7.2 2.1 shard_map.122
  9.3 12.6 %all-to-all-start = ((bf16[8,64,768]{2,1,0:T(8,128)(2,1)}), bf16[8,64,768]{2,1,0:T(8,128)(2,1)S(1)}, u32[]{:S(2)}, u32[]{:S(2)}) async-start(bf16[8,64,768]{2,1,0:T(8,128)(2,1)} %shard_map.122), calls=%async_computation | async-start | bytes 1572864 | tf_op jit(solution)/shard_map/all_to_all | solution.py:227
  23.6 2.5 shard_map.123
  26.1 3.5 %collective-permute-start = (bf16[256,1024]{1,0:T(8,128)(2,1)}, bf16[256,1024]{1,0:T(8,128)(2,1)}, u32[]{:S(2)}, u32[]{:S(2)}) collective-permute-start(bf16[256,1024]{1,0:T(8,128)(2,1)} %get-tuple-element.26), channel_id=1, source_target_pairs={{0,16},{16,32},{32,48},{48,0},{1,17},{17,33},{33,49},{49,1},{2,18}... | collective-permute-start | bytes 1572872 | tf_op jit(solution)/shard_map/ppermute | solution.py:205
  29.6 4.8 %collective-permute-start.1 = (bf16[256,1024]{1,0:T(8,128)(2,1)}, bf16[256,1024]{1,0:T(8,128)(2,1)}, u32[]{:S(2)}, u32[]{:S(2)}) collective-permute-start(bf16[256,1024]{1,0:T(8,128)(2,1)} %get-tuple-element.27), channel_id=1, source_target_pairs={{0,32},{16,48},{32,0},{48,16},{1,33},{17,49},{33,1},{49,17},{2,34}... | collective-permute-start | bytes 1572872 | tf_op jit(solution)/shard_map/ppermute | solution.py:205
  34.4 3.3 %collective-permute-start.2 = (bf16[256,1024]{1,0:T(8,128)(2,1)}, bf16[256,1024]{1,0:T(8,128)(2,1)}, u32[]{:S(2)}, u32[]{:S(2)}) collective-permute-start(bf16[256,1024]{1,0:T(8,128)(2,1)} %get-tuple-element.28), channel_id=1, source_target_pairs={{0,48},{16,0},{32,16},{48,32},{1,49},{17,1},{33,17},{49,33},{2,50}... | collective-permute-start | bytes 1572872 | tf_op jit(solution)/shard_map/ppermute | solution.py:205
  42.0 6.8 %collective-permute-start.8 = (bf16[64,512]{1,0:T(8,128)(2,1)}, bf16[64,512]{1,0:T(8,128)(2,1)S(1)}, u32[]{:S(2)}, u32[]{:S(2)}) collective-permute-start(bf16[64,512]{1,0:T(8,128)(2,1)} %shard_map.126), channel_id=1, source_target_pairs={{0,0},{1,64},{64,1},{65,65},{128,128},{129,192},{192,129},{193,193... | collective-permute-start | bytes 196616 | tf_op jit(solution)/shard_map/ppermute | solution.py:239
  48.8 6.4 %collective-permute-done.1.s2 = bf16[256,1024]{1,0:T(8,128)(2,1)} collective-permute-done((bf16[256,1024]{1,0:T(8,128)(2,1)}, bf16[256,1024]{1,0:T(8,128)(2,1)}, u32[]{:S(2)}, u32[]{:S(2)}) %collective-permute-start.1) | collective-permute-done | bytes 524320 | tf_op jit(solution)/shard_map/ppermute | solution.py:205
  56.5 5.7 %all-to-all-done = bf16[8,64,768]{2,1,0:T(8,128)(2,1)S(1)} async-done(((bf16[8,64,768]{2,1,0:T(8,128)(2,1)}), bf16[8,64,768]{2,1,0:T(8,128)(2,1)S(1)}, u32[]{:S(2)}, u32[]{:S(2)}) %all-to-all-start) | async-done | bytes 786464 | tf_op jit(solution)/shard_map/all_to_all | solution.py:227
  63.0 10.1 %all-to-all-start.1 = ((bf16[8,64,512]{2,1,0:T(8,128)(2,1)}), bf16[8,64,512]{2,1,0:T(8,128)(2,1)}, u32[]{:S(2)}, u32[]{:S(2)}) async-start(bf16[8,64,512]{2,1,0:T(8,128)(2,1)} %broadcast_in_dim.19), calls=%async_computation.1 | async-start | bytes 1048576 | tf_op jit(solution)/shard_map/all_to_all | solution.py:241
  75.0 2.3 collective-permute-done.3
  77.3 3.2 %shard_map.124 = (f32[256,768]{1,0:T(8,128)S(1)}, bf16[256,768]{1,0:T(8,128)(2,1)S(1)}, bf16[256,768]{1,0:T(8,128)(2,1)S(1)}, bf16[256,768]{1,0:T(8,128)(2,1)S(1)}) custom-call(bf16[512,768]{1,0:T(8,128)(2,1)S(1)} %bitcast.11, bf16[512,768]{1,0:T(8,128)(2,1)S(1)} %bitcast.12, bf16[256,1024]{1,0:T(8,128)(2,1)S(1)} %get-tuple-element.30.s0, ...), custom_call_target="tpu_custom_call" | custom-call | tf_op jit(solution)/shard_map/pallas_call | solution.py:194
  81.4 4.9 %collective-permute-start.4 = (bf16[256,768]{1,0:T(8,128)(2,1)S(1)}, bf16[256,768]{1,0:T(8,128)(2,1)S(1)}, u32[]{:S(2)}, u32[]{:S(2)}) collective-permute-start(bf16[256,768]{1,0:T(8,128)(2,1)S(1)} %get-tuple-element.35), channel_id=1, source_target_pairs={{0,48},{16,0},{32,16},{48,32},{1,49},{17,1},{33,17},{49,33},{2,50}... | collective-permute-start | bytes 1179656 | tf_op jit(solution)/shard_map/ppermute | solution.py:205
  86.3 2.5 collective-permute-start.5
  88.8 2.9 %collective-permute-start.6 = (bf16[256,768]{1,0:T(8,128)(2,1)S(1)}, bf16[256,768]{1,0:T(8,128)(2,1)S(1)}, u32[]{:S(2)}, u32[]{:S(2)}) collective-permute-start(bf16[256,768]{1,0:T(8,128)(2,1)S(1)} %get-tuple-element.37), channel_id=1, source_target_pairs={{0,16},{16,32},{32,48},{48,0},{1,17},{17,33},{33,49},{49,1},{2,18}... | collective-permute-start | bytes 1179656 | tf_op jit(solution)/shard_map/ppermute | solution.py:205
  91.7 11.6 %collective-permute-done.4.p1 = bf16[256,768]{1,0:T(8,128)(2,1)S(1)} collective-permute-done((bf16[256,768]{1,0:T(8,128)(2,1)S(1)}, bf16[256,768]{1,0:T(8,128)(2,1)S(1)}, u32[]{:S(2)}, u32[]{:S(2)}) %collective-permute-start.4) | collective-permute-done | bytes 393248 | tf_op jit(solution)/shard_map/ppermute | solution.py:205
  103.4 5.6 %collective-permute-done.6.p3 = bf16[256,768]{1,0:T(8,128)(2,1)S(1)} collective-permute-done((bf16[256,768]{1,0:T(8,128)(2,1)S(1)}, bf16[256,768]{1,0:T(8,128)(2,1)S(1)}, u32[]{:S(2)}, u32[]{:S(2)}) %collective-permute-start.6) | collective-permute-done | bytes 393248 | tf_op jit(solution)/shard_map/ppermute | solution.py:205
  111.5 3.6 %shard_map.125 = (bf16[256,512]{1,0:T(8,128)(2,1)}, bf16[256,128]{1,0:T(8,128)(2,1)}, f32[4,256,256]{2,1,0:T(8,128)}, bf16[256,512]{1,0:T(8,128)(2,1)}) custom-call(f32[256,768]{1,0:T(8,128)} %copy-done.10, bf16[256,768]{1,0:T(8,128)(2,1)} %copy-done.16, bf16[256,768]{1,0:T(8,128)(2,1)} %copy-done.17, bf16[256,768]{1,0:T(8,128)(2,1)} %copy-done.18, ...), custom_call_target="tpu_custom_call" | custom-call | tf_op jit(solution)/shard_map/pallas_call | solution.py:194
  115.1 4.9 %collective-permute-start.7 = (bf16[256,512]{1,0:T(8,128)(2,1)}, bf16[256,512]{1,0:T(8,128)(2,1)S(1)}, u32[]{:S(2)}, u32[]{:S(2)}) collective-permute-start(bf16[256,512]{1,0:T(8,128)(2,1)} %get-tuple-element.38.own), channel_id=1, source_target_pairs={{0,1},{1,0},{2,3},{3,2},{4,5},{5,4},{6,7},{7,6},{8,9},{9,8},{10,11... | collective-permute-start | bytes 786440 | tf_op jit(solution)/shard_map/ppermute | solution.py:205
  120.1 21.1 %collective-permute-done.7.oth = bf16[256,512]{1,0:T(8,128)(2,1)S(1)} collective-permute-done((bf16[256,512]{1,0:T(8,128)(2,1)}, bf16[256,512]{1,0:T(8,128)(2,1)S(1)}, u32[]{:S(2)}, u32[]{:S(2)}) %collective-permute-start.7) | collective-permute-done | bytes 262176 | tf_op jit(solution)/shard_map/ppermute | solution.py:205
  141.1 4.1 %all-gather.2.cloned.1.call-done.weight = bf16[8,4,2,64,512]{4,3,2,1,0:T(8,128)(2,1)} async-done(((bf16[1,4,2,64,512]{4,3,2,1,0:T(8,128)(2,1)}), bf16[8,4,2,64,512]{4,3,2,1,0:T(8,128)(2,1)}) %all-gather.2.cloned.1.call-update) | async-done | bytes 4194320 | tf_op jit(solution)/shard_map/all_gather | solution.py:254
  145.2 2.2 copy-done.1
  151.2 4.2 %all-to-all-start.2 = ((bf16[4,256,512]{2,1,0:T(8,128)(2,1)}), bf16[4,256,512]{2,1,0:T(8,128)(2,1)S(1)}, u32[]{:S(2)}, u32[]{:S(2)}) async-start(bf16[4,256,512]{2,1,0:T(8,128)(2,1)} %copy-done.3), calls=%async_computation.2 | async-start | bytes 2097152 | tf_op jit(solution)/shard_map/all_to_all | solution.py:278
  155.7 15.3 %all-to-all-done.2.blocks = bf16[4,256,512]{2,1,0:T(8,128)(2,1)S(1)} async-done(((bf16[4,256,512]{2,1,0:T(8,128)(2,1)}), bf16[4,256,512]{2,1,0:T(8,128)(2,1)S(1)}, u32[]{:S(2)}, u32[]{:S(2)}) %all-to-all-start.2) | async-done | bytes 1048608 | tf_op jit(solution)/shard_map/all_to_all | solution.py:278
  171.9 17.1 %all_to_all.30.errors = bf16[4,256,512]{2,1,0:T(8,128)(2,1)S(1)} all-to-all(bf16[4,256,512]{2,1,0:T(8,128)(2,1)S(1)} %get-tuple-element.42), channel_id=1, replica_groups=mesh['zl'=8,'y'=4,'c'=2,'x'=4,'zh'=2] {'x'}, dimensions={0} | all-to-all | bytes 2097152 | tf_op jit(solution)/shard_map/all_to_all | solution.py:287
  188.9 2.2 copy-done.2
  192.4 12.1 %collective-permute-start.9 = (bf16[256,512]{1,0:T(8,128)(2,1)S(1)}, bf16[256,512]{1,0:T(8,128)(2,1)S(1)}, u32[]{:S(2)}, u32[]{:S(2)}) collective-permute-start(bf16[256,512]{1,0:T(8,128)(2,1)S(1)} %shard_map.130), channel_id=1, source_target_pairs={{0,1},{1,0},{2,3},{3,2},{4,5},{5,4},{6,7},{7,6},{8,9},{9,8},{10,11... | collective-permute-start | bytes 786440 | tf_op jit(solution)/shard_map/ppermute | solution.py:205
  205.8 12.1 %collective-permute-done.9.d_other = bf16[256,512]{1,0:T(8,128)(2,1)S(1)} collective-permute-done((bf16[256,512]{1,0:T(8,128)(2,1)S(1)}, bf16[256,512]{1,0:T(8,128)(2,1)S(1)}, u32[]{:S(2)}, u32[]{:S(2)}) %collective-permute-start.9) | collective-permute-done | bytes 262176 | tf_op jit(solution)/shard_map/ppermute | solution.py:205
  219.1 14.3 %all_to_all.31.d_keys = bf16[4,256,128]{2,1,0:T(8,128)(2,1)S(1)} all-to-all(bf16[4,256,128]{2,1,0:T(8,128)(2,1)S(1)} %shard_map.131), channel_id=1, replica_groups=mesh['zl'=8,'y'=4,'c'=2,'x'=4,'zh'=2] {'y'}, dimensions={0} | all-to-all | bytes 524288 | tf_op jit(solution)/shard_map/all_to_all | solution.py:295
  233.4 2.1 shard_map.132
  235.5 1.9 collective-permute-start.10
  238.8 25.2 %all_to_all.32.parts = bf16[8,64,128]{2,1,0:T(8,128)(2,1)S(1)} all-to-all(bf16[8,64,128]{2,1,0:T(8,128)(2,1)S(1)} %bitcast.13), channel_id=1, replica_groups=mesh['zl'=8,'y'=4,'c'=2,'x'=4,'zh'=2] {'zl'}, dimensions={0} | all-to-all | bytes 262144 | tf_op jit(solution)/shard_map/all_to_all | solution.py:299
  (69 shorter events, 24.1 us)
Async XLA Ops:
  7.2 148.4 %copy-start = (bf16[256,4096]{1,0:T(8,128)(2,1)S(1)}, bf16[256,4096]{1,0:T(8,128)(2,1)}, u32[]{:S(2)}) copy-start(bf16[256,4096]{1,0:T(8,128)(2,1)} %param.12) | copy-start | bytes 6291460
  9.3 52.9 %all-to-all-start = ((bf16[8,64,768]{2,1,0:T(8,128)(2,1)}), bf16[8,64,768]{2,1,0:T(8,128)(2,1)S(1)}, u32[]{:S(2)}, u32[]{:S(2)}) async-start(bf16[8,64,768]{2,1,0:T(8,128)(2,1)} %shard_map.122), calls=%async_computation | async-start | bytes 1572864 | tf_op jit(solution)/shard_map/all_to_all | solution.py:227
  22.0 1.6 copy-start.6
  26.1 54.3 %copy-start.4 = (bf16[256,1024]{1,0:T(8,128)(2,1)}, bf16[256,1024]{1,0:T(8,128)(2,1)S(1)}, u32[]{:S(2)}) copy-start(bf16[256,1024]{1,0:T(8,128)(2,1)S(1)} %get-tuple-element.30.s0) | copy-start | bytes 1572868
  26.1 22.6 %collective-permute-start = (bf16[256,1024]{1,0:T(8,128)(2,1)}, bf16[256,1024]{1,0:T(8,128)(2,1)}, u32[]{:S(2)}, u32[]{:S(2)}) collective-permute-start(bf16[256,1024]{1,0:T(8,128)(2,1)} %get-tuple-element.26), channel_id=1, source_target_pairs={{0,16},{16,32},{32,48},{48,0},{1,17},{17,33},{33,49},{49,1},{2,18}... | collective-permute-start | bytes 1572872 | tf_op jit(solution)/shard_map/ppermute | solution.py:205
  29.6 25.5 %collective-permute-start.1 = (bf16[256,1024]{1,0:T(8,128)(2,1)}, bf16[256,1024]{1,0:T(8,128)(2,1)}, u32[]{:S(2)}, u32[]{:S(2)}) collective-permute-start(bf16[256,1024]{1,0:T(8,128)(2,1)} %get-tuple-element.27), channel_id=1, source_target_pairs={{0,32},{16,48},{32,0},{48,16},{1,33},{17,49},{33,1},{49,17},{2,34}... | collective-permute-start | bytes 1572872 | tf_op jit(solution)/shard_map/ppermute | solution.py:205
  34.4 22.1 %collective-permute-start.2 = (bf16[256,1024]{1,0:T(8,128)(2,1)}, bf16[256,1024]{1,0:T(8,128)(2,1)}, u32[]{:S(2)}, u32[]{:S(2)}) collective-permute-start(bf16[256,1024]{1,0:T(8,128)(2,1)} %get-tuple-element.28), channel_id=1, source_target_pairs={{0,48},{16,0},{32,16},{48,32},{1,49},{17,1},{33,17},{49,33},{2,50}... | collective-permute-start | bytes 1572872 | tf_op jit(solution)/shard_map/ppermute | solution.py:205
  42.0 20.2 %collective-permute-start.8 = (bf16[64,512]{1,0:T(8,128)(2,1)}, bf16[64,512]{1,0:T(8,128)(2,1)S(1)}, u32[]{:S(2)}, u32[]{:S(2)}) collective-permute-start(bf16[64,512]{1,0:T(8,128)(2,1)} %shard_map.126), channel_id=1, source_target_pairs={{0,0},{1,64},{64,1},{65,65},{128,128},{129,192},{192,129},{193,193... | collective-permute-start | bytes 196616 | tf_op jit(solution)/shard_map/ppermute | solution.py:239
  63.0 46.0 %all-to-all-start.1 = ((bf16[8,64,512]{2,1,0:T(8,128)(2,1)}), bf16[8,64,512]{2,1,0:T(8,128)(2,1)}, u32[]{:S(2)}, u32[]{:S(2)}) async-start(bf16[8,64,512]{2,1,0:T(8,128)(2,1)} %broadcast_in_dim.19), calls=%async_computation.1 | async-start | bytes 1048576 | tf_op jit(solution)/shard_map/all_to_all | solution.py:241
  73.1 72.1 %all-gather.2.cloned.1.call-start = ((), (), s32[]{:S(2)}) async-start(), calls=%async_computation.6 | async-start | bytes 4718592 | tf_op jit(solution)/shard_map/all_gather | solution.py:254
  73.1 4.2 %collective-permute-start.3 = (bf16[8,64,768]{2,1,0:T(8,128)(2,1)S(1)}, bf16[8,64,768]{2,1,0:T(8,128)(2,1)S(1)}, u32[]{:S(2)}, u32[]{:S(2)}) collective-permute-start(bf16[8,64,768]{2,1,0:T(8,128)(2,1)S(1)} %all-to-all-done), channel_id=1, source_target_pairs={{0,8},{8,0},{1,9},{9,1},{2,10},{10,2},{3,11},{11,3},{4,12},{12,4},... | collective-permute-start | bytes 2359304 | tf_op jit(solution)/shard_map/ppermute | solution.py:205
  77.3 31.7 %copy-start.19 = (s32[1,3]{1,0:T(1,128)S(1)}, s32[1,3]{1,0:T(1,128)}, u32[]{:S(2)}) copy-start(s32[1,3]{1,0:T(1,128)} %param.21) | copy-start | bytes 40
  81.4 22.0 %collective-permute-start.4 = (bf16[256,768]{1,0:T(8,128)(2,1)S(1)}, bf16[256,768]{1,0:T(8,128)(2,1)S(1)}, u32[]{:S(2)}, u32[]{:S(2)}) collective-permute-start(bf16[256,768]{1,0:T(8,128)(2,1)S(1)} %get-tuple-element.35), channel_id=1, source_target_pairs={{0,48},{16,0},{32,16},{48,32},{1,49},{17,1},{33,17},{49,33},{2,50}... | collective-permute-start | bytes 1179656 | tf_op jit(solution)/shard_map/ppermute | solution.py:205
  86.3 17.1 %collective-permute-start.5 = (bf16[256,768]{1,0:T(8,128)(2,1)S(1)}, bf16[256,768]{1,0:T(8,128)(2,1)S(1)}, u32[]{:S(2)}, u32[]{:S(2)}) collective-permute-start(bf16[256,768]{1,0:T(8,128)(2,1)S(1)} %get-tuple-element.36), channel_id=1, source_target_pairs={{0,32},{16,48},{32,0},{48,16},{1,33},{17,49},{33,1},{49,17},{2,34}... | collective-permute-start | bytes 1179656 | tf_op jit(solution)/shard_map/ppermute | solution.py:205
  88.8 20.2 %collective-permute-start.6 = (bf16[256,768]{1,0:T(8,128)(2,1)S(1)}, bf16[256,768]{1,0:T(8,128)(2,1)S(1)}, u32[]{:S(2)}, u32[]{:S(2)}) collective-permute-start(bf16[256,768]{1,0:T(8,128)(2,1)S(1)} %get-tuple-element.37), channel_id=1, source_target_pairs={{0,16},{16,32},{32,48},{48,0},{1,17},{17,33},{33,49},{49,1},{2,18}... | collective-permute-start | bytes 1179656 | tf_op jit(solution)/shard_map/ppermute | solution.py:205
  103.4 8.2 %copy-start.16 = (bf16[256,768]{1,0:T(8,128)(2,1)}, bf16[256,768]{1,0:T(8,128)(2,1)S(1)}, u32[]{:S(2)}) copy-start(bf16[256,768]{1,0:T(8,128)(2,1)S(1)} %collective-permute-done.4.p1) | copy-start | bytes 1179652
  103.4 8.2 %copy-start.17 = (bf16[256,768]{1,0:T(8,128)(2,1)}, bf16[256,768]{1,0:T(8,128)(2,1)S(1)}, u32[]{:S(2)}) copy-start(bf16[256,768]{1,0:T(8,128)(2,1)S(1)} %collective-permute-done.5.p2) | copy-start | bytes 1179652
  109.0 2.5 copy-start.18
  115.1 26.0 %collective-permute-start.7 = (bf16[256,512]{1,0:T(8,128)(2,1)}, bf16[256,512]{1,0:T(8,128)(2,1)S(1)}, u32[]{:S(2)}, u32[]{:S(2)}) collective-permute-start(bf16[256,512]{1,0:T(8,128)(2,1)} %get-tuple-element.38.own), channel_id=1, source_target_pairs={{0,1},{1,0},{2,3},{3,2},{4,5},{5,4},{6,7},{7,6},{8,9},{9,8},{10,11... | collective-permute-start | bytes 786440 | tf_op jit(solution)/shard_map/ppermute | solution.py:205
  145.2 2.2 copy-start.1
  150.2 1.0 copy-start.3
  151.2 19.8 %all-to-all-start.2 = ((bf16[4,256,512]{2,1,0:T(8,128)(2,1)}), bf16[4,256,512]{2,1,0:T(8,128)(2,1)S(1)}, u32[]{:S(2)}, u32[]{:S(2)}) async-start(bf16[4,256,512]{2,1,0:T(8,128)(2,1)} %copy-done.3), calls=%async_computation.2 | async-start | bytes 2097152 | tf_op jit(solution)/shard_map/all_to_all | solution.py:278
  188.9 2.2 copy-start.2
  192.4 25.5 %copy-start.7 = (f32[256,128]{1,0:T(8,128)S(1)}, f32[256,128]{1,0:T(8,128)}, u32[]{:S(2)}) copy-start(f32[256,128]{1,0:T(8,128)} %get-tuple-element.53.cos) | copy-start | bytes 393220
  192.4 25.5 %copy-start.8 = (f32[256,128]{1,0:T(8,128)S(1)}, f32[256,128]{1,0:T(8,128)}, u32[]{:S(2)}) copy-start(f32[256,128]{1,0:T(8,128)} %get-tuple-element.54.sin) | copy-start | bytes 393220
  192.4 25.5 %copy-start.9 = (f32[4,256,256]{2,1,0:T(8,128)S(1)}, f32[4,256,256]{2,1,0:T(8,128)}, u32[]{:S(2)}) copy-start(f32[4,256,256]{2,1,0:T(8,128)} %get-tuple-element.45.prob_ref) | copy-start | bytes 3145732
  192.4 25.5 %copy-start.13 = (bf16[256,512]{1,0:T(8,128)(2,1)S(1)}, bf16[256,512]{1,0:T(8,128)(2,1)}, u32[]{:S(2)}) copy-start(bf16[256,512]{1,0:T(8,128)(2,1)} %get-tuple-element.43.q_ref) | copy-start | bytes 786436
  192.4 25.5 %copy-start.14 = (bf16[256,128]{1,0:T(8,128)(2,1)S(1)}, bf16[256,128]{1,0:T(8,128)(2,1)}, u32[]{:S(2)}) copy-start(bf16[256,128]{1,0:T(8,128)(2,1)} %get-tuple-element.44.v_ref) | copy-start | bytes 196612
  192.4 25.5 %collective-permute-start.9 = (bf16[256,512]{1,0:T(8,128)(2,1)S(1)}, bf16[256,512]{1,0:T(8,128)(2,1)S(1)}, u32[]{:S(2)}, u32[]{:S(2)}) collective-permute-start(bf16[256,512]{1,0:T(8,128)(2,1)S(1)} %shard_map.130), channel_id=1, source_target_pairs={{0,1},{1,0},{2,3},{3,2},{4,5},{5,4},{6,7},{7,6},{8,9},{9,8},{10,11... | collective-permute-start | bytes 786440 | tf_op jit(solution)/shard_map/ppermute | solution.py:205
  205.8 27.6 %copy-start.5 = (bf16[256,1024]{1,0:T(8,128)(2,1)S(1)}, bf16[256,1024]{1,0:T(8,128)(2,1)}, u32[]{:S(2)}) copy-start(bf16[256,1024]{1,0:T(8,128)(2,1)} %copy-done.4) | copy-start | bytes 1572868
  219.0 44.9 %copy-start.15 = (s32[16,128]{1,0:T(8,128)S(1)}, s32[16,128]{1,0:T(8,128)}, u32[]{:S(2)}) copy-start(s32[16,128]{1,0:T(8,128)} %codes.1) | copy-start | bytes 24580
  235.5 3.2 %collective-permute-start.10 = (bf16[512,128]{1,0:T(8,128)(2,1)S(1)}, bf16[512,128]{1,0:T(8,128)(2,1)S(1)}, u32[]{:S(2)}, u32[]{:S(2)}) collective-permute-start(bf16[512,128]{1,0:T(8,128)(2,1)S(1)} %get-tuple-element.47), channel_id=1, source_target_pairs={{0,8},{8,0},{1,9},{9,1},{2,10},{10,2},{3,11},{11,3},{4,12},{12,4},... | collective-permute-start | bytes 393224 | tf_op jit(solution)/shard_map/ppermute | solution.py:205
  (3 other events, 2.7 us)
Sparse Core Ops, SparseCore 0:
  109.1 36.0 all-gather.1

commit v3 on v2

--- a/solution.py
+++ b/solution.py
@@ -39,12 +39,39 @@
     return kept.astype(BF16)
 
 
-def mask_qkv_kernel(qw, kw, vw, qc, kc, vc, out):
+def compact_qkv_kernel(qw, kw, vw, qc, kc, vc, out):
     weight = jnp.concatenate([qw[...], kw[...], vw[...]], axis=1)
     codes = jnp.concatenate([qc[...], kc[...], vc[...]], axis=1)
-    kept = masked(weight, codes)
+    groups, rows = codes.shape[0], weight.shape[0]
+    at_group = lax.broadcasted_iota(jnp.int32, (groups, rows), 0)
+    at_row = lax.broadcasted_iota(jnp.int32, (groups, rows), 1)
+    plane = []
+    for within in range(4):
+        pick = jnp.where(at_row == 4 * at_group + within, 1.0, 0.0).astype(BF16)
+        plane.append(jnp.dot(pick, weight, preferred_element_type=F32))
+    first = jnp.where(codes < 3, plane[0], jnp.where(codes < 5, plane[1], plane[2]))
+    second = jnp.where((codes == 1) | (codes == 3), plane[2], plane[3])
+    second = jnp.where(codes == 0, plane[1], second)
+    kept = jnp.concatenate([first, second, codes.astype(F32)], axis=0).astype(BF16)
     for copy in range(out.shape[0]):
         out[copy] = kept
+
+
+def spread(kept):
+    pieces, rows, width = kept.shape
+    groups = rows // 3
+    first, second, code = (
+        kept[:, at * groups : (at + 1) * groups, :].astype(F32).reshape(pieces * groups, width)
+        for at in range(3)
+    )
+    mid = (code == 3) | (code == 4)
+    planes = (
+        jnp.where(code < 3, first, 0.0),
+        jnp.where(code == 0, second, jnp.where(mid, first, 0.0)),
+        jnp.where((code == 1) | (code == 3), second, jnp.where(code == 5, first, 0.0)),
+        jnp.where((code == 2) | (code > 3), second, 0.0),
+    )
+    return jnp.concatenate(planes, axis=0).astype(BF16)
 
 
 def mask_out_kernel(ow, oc, out):
@@ -59,23 +86,21 @@
 
 def split_hidden_kernel(at_ref, hidden, *outs):
     shifts = len(outs)
-    tokens, width = outs[0].shape
-    n_z = width // 128
-    half = width // 2
-    low = lax.broadcasted_iota(jnp.int32, (tokens, 128), 1) < 64
-    own = low == (at_ref[2] == 0)
-    for shift in range(shifts):
+    depth = outs[0].shape[1]
+    n_z = depth // 128
+    row = lax.broadcasted_iota(jnp.int32, (depth, 1), 0)
+    z, core, group, within = row // 128, row % 128 // 64, row % 64 // 4, row % 4
+    place = jnp.where(core == at_ref[2], 0, depth // 2) + within * (depth // 8) + z * 16 + group
+    column = lax.broadcasted_iota(jnp.int32, (depth, depth), 1)
+    order = jnp.where(column == place, 1.0, 0.0).astype(BF16)
+    for shift, out in enumerate(outs):
         y_to = lax.rem(at_ref[0] + shift, shifts)
-        for pair in range(n_z // 2):
-            both = []
-            for z in (2 * pair, 2 * pair + 1):
-                lane = pl.multiple_of((z * shifts + y_to) * 128, 128)
-                both.append(hidden[:, pl.ds(lane, 128)].astype(F32))
-            mine = [jnp.where(own, v, pltpu.roll(v, 64, 1)) for v in both]
-            rest = [jnp.where(own, pltpu.roll(v, 64, 1), v) for v in both]
-            for part, (first, last) in enumerate((mine, rest)):
-                start = part * half + pair * 128
-                outs[shift][:, start : start + 128] = jnp.where(low, first, last).astype(BF16)
+        parts = []
+        for z in range(n_z):
+            lane = pl.multiple_of((z * shifts + y_to) * 128, 128)
+            parts.append(hidden[:, pl.ds(lane, 128)])
+        columns = jnp.concatenate(parts, axis=1)
+        out[...] = jnp.dot(columns, order, preferred_element_type=F32).astype(BF16)
 
 
 def rotate(values, cos, sin):
@@ -83,10 +108,11 @@
 
 
 def project_kernel(w_own, w_oth, s0, s1, s2, s3, p0, p1, p2, p3):
-    half = w_own.shape[0]
+    own, oth = spread(w_own), spread(w_oth)
+    half = own.shape[0]
     for slot, term in ((s2, p2), (s1, p1), (s3, p3), (s0, p0)):
-        total = jnp.dot(slot[:, :half], w_own[...], preferred_element_type=F32)
-        total += jnp.dot(slot[:, half:], w_oth[...], preferred_element_type=F32)
+        total = jnp.dot(slot[:, :half], own, preferred_element_type=F32)
+        total += jnp.dot(slot[:, half:], oth, preferred_element_type=F32)
         term[...] = total.astype(term.dtype)
 
 
@@ -154,19 +180,28 @@
 
 
 def grad_kernel(at_ref, s0, s1, s2, s3, d_keys, own, oth):
-    half = own.shape[0]
+    pieces, rows = own.shape[:2]
+    half, groups = pieces * rows, rows // 4
     n_y = d_keys.shape[0]
     for at, out in ((half, oth), (0, own)):
-        total = jnp.zeros(out.shape, F32)
+        total = jnp.zeros((half, out.shape[2]), F32)
         for shift, slot in enumerate((s0, s1, s2, s3)):
             d_key = d_keys[lax.rem(at_ref[0] + n_y - shift, n_y)]
             total += lax.dot_general(slot[:, at : at + half], d_key, TN, preferred_element_type=F32)
-        out[...] = total.astype(out.dtype)
+        total = total.astype(out.dtype)
+        for within in range(4):
+            for z in range(pieces):
+                start = (within * pieces + z) * groups
+                out[z, within * groups : (within + 1) * groups] = total[start : start + groups]
 
 
 def final_kernel(parts, codes, out):
     total = jnp.sum(parts[...].astype(F32), axis=0)
-    out[...] = jnp.where(keep_mask(codes[...], out.shape[0]), total, 0.0)
+    groups = codes.shape[0]
+    for within in range(4):
+        keep = (lax.shift_right_logical(jnp.full(codes.shape, KEEP_BITS[within], jnp.int32), codes[...]) & 1) == 1
+        rows = total[within * groups : (within + 1) * groups]
+        out[pl.ds(within, groups, stride=4), :] = jnp.where(keep, rows, 0.0)
 
 
 def doc_layout(lengths, row_total):
@@ -223,12 +258,17 @@
     heads = q_width // HEAD_DIM
     depth = n_z * n_c * rows
 
-    mine = call(mask_qkv_kernel, shape((n_z, rows, width)), qw, kw, vw, qc, kc, vc, mib=58)
+    mine = call(compact_qkv_kernel, shape((n_z, 3 * rows // 4, width)), qw, kw, vw, qc, kc, vc, mib=58)
     w_own = lax.all_to_all(mine, "zl", 0, 0)
 
-    split = call(split_hidden_kernel, [shape((tokens, depth))] * n_y, hidden, at=at)
+    split = call(split_hidden_kernel, [shape((tokens, depth))] * n_y, hidden, at=at, mib=40)
     slots = [split[0]] + [shifted(split[s], "y", s) for s in range(1, n_y)]
-    w_own, *slots = lax.optimization_barrier((w_own, *slots))
+    segment, doc_pos, live = doc_layout(doc_lengths[0], tokens)
+    cos, sin = angles(doc_pos)
+    spot = jnp.arange(tokens)
+    allow = (segment[:, None] == segment[None, :]) & (spot[None, :] <= spot[:, None])
+    allow = allow.astype(F32)
+    w_own, cos, sin, allow, *slots = lax.optimization_barrier((w_own, cos, sin, allow, *slots))
 
     out_mine = call(mask_out_kernel, shape((ow.shape[1], ow.shape[0])), ow, oc)
     trade = []
@@ -244,8 +284,8 @@
     terms = call(
         project_kernel,
         [shape((tokens, width), F32)] + [shape((tokens, width))] * (n_y - 1),
-        w_own.reshape(-1, width),
-        w_oth.reshape(-1, width),
+        w_own,
+        w_oth,
         *slots,
     )
     terms = [terms[0]] + [shifted(terms[s], "y", -s) for s in range(1, n_y)]
@@ -253,10 +293,6 @@
     out_z = after(out_z, *terms).reshape(n_z // 2, 2, ow.shape[1], ow.shape[0])
     out_w = lax.all_gather(out_z, ("y", "c"), axis=0)
 
-    segment, doc_pos, live = doc_layout(doc_lengths[0], tokens)
-    cos, sin = angles(doc_pos)
-    spot = jnp.arange(tokens)
-    allow = (segment[:, None] == segment[None, :]) & (spot[None, :] <= spot[:, None])
     queries, values, prob, att = call(
         attend_kernel,
         (
@@ -268,7 +304,7 @@
         *terms,
         cos,
         sin,
-        allow.astype(F32),
+        allow,
         mib=58,
     )
 
@@ -293,10 +329,10 @@
         key_grad_kernel, shape((n_y, tokens, HEAD_DIM)), d_own, d_oth, queries, values, prob, cos, sin
     )
     d_keys = lax.all_to_all(d_key, "y", 0, 0)
-    half = (depth // 2, HEAD_DIM)
+    half = (n_z, rows, HEAD_DIM)
     g_own, g_oth = call(grad_kernel, (shape(half, F32), shape(half)), *slots, d_keys, at=at)
     grad = (g_own + shifted(g_oth, "c", 1).astype(F32)).astype(BF16)
-    grad = lax.all_to_all(grad.reshape(n_z, rows, HEAD_DIM), "zl", 0, 0)
+    grad = lax.all_to_all(grad, "zl", 0, 0)
     grad_key = call(final_kernel, shape((rows, HEAD_DIM), F32), grad, kc)
     return block_out, grad_key
 

time: 273 us -> 268 us (0.982)
  blocking collectives: 56.5 us -> 47.9 us
  starting transfers between devices: 76.4 us -> 79.6 us
    all_to_all x1, waiting for transfers between devices: 5.7 us -> 0.01 us  [shards(): w_own = lax.all_to_all(mine, 'zl', 0, 0)]
    all_to_all x1, blocking collectives: 14.3 us -> 9.33 us  [shards(): d_keys = lax.all_to_all(d_key, 'y', 0, 0)]
    ppermute x10, waiting for transfers between devices: 61.8 us -> 66.3 us  [shifted(): lax.ppermute(value, axis, [(i, (i + by) % size) for i in range(size)])]
    all_to_all x1, blocking collectives: 25.2 us -> 21.5 us  [shards(): grad = lax.all_to_all(grad, 'zl', 0, 0)]
    all_gather x1, waiting for transfers between devices: 4.09 us -> 7.37 us  [shards(): out_w = lax.all_gather(out_z, ('y', 'c'), axis=0)]
    ppermute x10, starting transfers between devices: 42.7 us -> 45.9 us  [shifted(): lax.ppermute(value, axis, [(i, (i + by) % size) for i in range(size)])]
    unnamed x42 -> x44, local copies, waits for them, and re-layouts: 12.2 us -> 9.81 us
  transfers between devices with their start and end apart: 15 -> 15, of which waited for: 11 -> 10; matrix products, arithmetic and copies ran while one was open for 2% -> 1% of each run, Pallas kernels for 4% -> 5%
where the time goes in v3:
time: 268 us; the launch traced here: 267 us
  waiting for transfers between devices  89 us (33%)
  starting transfers between devices  79.6 us (30%)
  blocking collectives  47.9 us (18%)
  Pallas kernels  22.7 us (8%)
  between operations  14.4 us (5%)
  local copies, waits for them, and re-layouts  10.8 us (4%)
    ppermute x10, waiting for transfers between devices, shifted(): lax.ppermute(value, axis, [(i, (i + by) % size) for i in range(size)])  66.3 us
    ppermute x10, starting transfers between devices, shifted(): lax.ppermute(value, axis, [(i, (i + by) % size) for i in range(size)])  45.9 us
    pallas_call x12, Pallas kernels, call(): pl.pallas_call(kernel, out_shape=out_shape, in_specs=specs, compiler_para...  22.7 us
    all_to_all x1, blocking collectives, shards(): grad = lax.all_to_all(grad, 'zl', 0, 0)  21.5 us
    all_to_all x1, blocking collectives, shards(): errors = lax.all_to_all(error, 'x', 0, 0)  17.1 us
    all_to_all x1, waiting for transfers between devices, shards(): blocks = lax.all_to_all(part, 'x', 0, 0)  15.3 us
    all_to_all x1, starting transfers between devices, shards(): w_own = lax.all_to_all(mine, 'zl', 0, 0)  12.8 us
    all_to_all x1, starting transfers between devices, shards(): out_z = lax.all_to_all(copies(out_mine, n_z), 'zl', 0, 0)  9.91 us
  transfers between devices with their start and end apart: 15, of which 10 were waited for; matrix products, arithmetic and copies ran while one was open for 1% of the time, Pallas kernels for 5%

profile of v3, /device:TPU:32, one launch (start us, length us, event | category | flops | bytes accessed | tf_op | source)
XLA Modules:
  0.0 266.9 jit_solution(788296697609528716)
XLA Ops:
  7.2 2.1 shard_map.122
  9.3 12.8 %all-to-all-start = ((bf16[8,48,768]{2,1,0:T(8,128)(2,1)}), bf16[8,48,768]{2,1,0:T(8,128)(2,1)S(1)}, u32[]{:S(2)}, u32[]{:S(2)}) async-start(bf16[8,48,768]{2,1,0:T(8,128)(2,1)} %shard_map.122), calls=%async_computation | async-start | bytes 1179648 | tf_op jit(solution)/shard_map/all_to_all | solution.py:262
  23.7 4.0 %shard_map.123 = (bf16[256,1024]{1,0:T(8,128)(2,1)S(1)}, bf16[256,1024]{1,0:T(8,128)(2,1)}, bf16[256,1024]{1,0:T(8,128)(2,1)}, bf16[256,1024]{1,0:T(8,128)(2,1)}) custom-call(s32[3]{0:T(128)S(1)} %pad_add_fusion.at_ref, bf16[256,4096]{1,0:T(8,128)(2,1)S(1)} %copy-done.6), custom_call_target="tpu_custom_call" | custom-call | tf_op jit(solution)/shard_map/pallas_call | solution.py:229
  27.7 3.5 %collective-permute-start = (bf16[256,1024]{1,0:T(8,128)(2,1)}, bf16[256,1024]{1,0:T(8,128)(2,1)}, u32[]{:S(2)}, u32[]{:S(2)}) collective-permute-start(bf16[256,1024]{1,0:T(8,128)(2,1)} %get-tuple-element.29), channel_id=1, source_target_pairs={{0,16},{16,32},{32,48},{48,0},{1,17},{17,33},{33,49},{49,1},{2,18}... | collective-permute-start | bytes 1572872 | tf_op jit(solution)/shard_map/ppermute | solution.py:240
  31.2 4.8 %collective-permute-start.1 = (bf16[256,1024]{1,0:T(8,128)(2,1)}, bf16[256,1024]{1,0:T(8,128)(2,1)}, u32[]{:S(2)}, u32[]{:S(2)}) collective-permute-start(bf16[256,1024]{1,0:T(8,128)(2,1)} %get-tuple-element.30), channel_id=1, source_target_pairs={{0,32},{16,48},{32,0},{48,16},{1,33},{17,49},{33,1},{49,17},{2,34}... | collective-permute-start | bytes 1572872 | tf_op jit(solution)/shard_map/ppermute | solution.py:240
  36.0 3.3 %collective-permute-start.2 = (bf16[256,1024]{1,0:T(8,128)(2,1)}, bf16[256,1024]{1,0:T(8,128)(2,1)}, u32[]{:S(2)}, u32[]{:S(2)}) collective-permute-start(bf16[256,1024]{1,0:T(8,128)(2,1)} %get-tuple-element.31), channel_id=1, source_target_pairs={{0,48},{16,0},{32,16},{48,32},{1,49},{17,1},{33,17},{49,33},{2,50}... | collective-permute-start | bytes 1572872 | tf_op jit(solution)/shard_map/ppermute | solution.py:240
  39.9 6.8 %collective-permute-start.8 = (bf16[64,512]{1,0:T(8,128)(2,1)S(1)}, bf16[64,512]{1,0:T(8,128)(2,1)S(1)}, u32[]{:S(2)}, u32[]{:S(2)}) collective-permute-start(bf16[64,512]{1,0:T(8,128)(2,1)S(1)} %shard_map.126), channel_id=1, source_target_pairs={{0,0},{1,64},{64,1},{65,65},{128,128},{129,192},{192,129},{193,193... | collective-permute-start | bytes 196616 | tf_op jit(solution)/shard_map/ppermute | solution.py:279
  49.2 7.5 %collective-permute-done.1.s2 = bf16[256,1024]{1,0:T(8,128)(2,1)} collective-permute-done((bf16[256,1024]{1,0:T(8,128)(2,1)}, bf16[256,1024]{1,0:T(8,128)(2,1)}, u32[]{:S(2)}, u32[]{:S(2)}) %collective-permute-start.1) | collective-permute-done | bytes 524320 | tf_op jit(solution)/shard_map/ppermute | solution.py:240
  58.9 9.9 %all-to-all-start.1 = ((bf16[8,64,512]{2,1,0:T(8,128)(2,1)}), bf16[8,64,512]{2,1,0:T(8,128)(2,1)}, u32[]{:S(2)}, u32[]{:S(2)}) async-start(bf16[8,64,512]{2,1,0:T(8,128)(2,1)} %broadcast_in_dim.19), calls=%async_computation.1 | async-start | bytes 1048576 | tf_op jit(solution)/shard_map/all_to_all | solution.py:281
  68.9 1.9 collective-permute-start.3
  70.8 2.0 collective-permute-done.3.w_oth
  72.7 3.5 %shard_map.124 = (f32[256,768]{1,0:T(8,128)S(1)}, bf16[256,768]{1,0:T(8,128)(2,1)S(1)}, bf16[256,768]{1,0:T(8,128)(2,1)S(1)}, bf16[256,768]{1,0:T(8,128)(2,1)S(1)}) custom-call(bf16[8,48,768]{2,1,0:T(8,128)(2,1)S(1)} %all-to-all-done.w_own, bf16[8,48,768]{2,1,0:T(8,128)(2,1)S(1)} %collective-permute-done.3.w_oth, ...), custom_call_target="tpu_custom_call" | custom-call | tf_op jit(solution)/shard_map/pallas_call | solution.py:229
  77.1 4.5 %collective-permute-start.4 = (bf16[256,768]{1,0:T(8,128)(2,1)S(1)}, bf16[256,768]{1,0:T(8,128)(2,1)S(1)}, u32[]{:S(2)}, u32[]{:S(2)}) collective-permute-start(bf16[256,768]{1,0:T(8,128)(2,1)S(1)} %get-tuple-element.38), channel_id=1, source_target_pairs={{0,48},{16,0},{32,16},{48,32},{1,49},{17,1},{33,17},{49,33},{2,50}... | collective-permute-start | bytes 1179656 | tf_op jit(solution)/shard_map/ppermute | solution.py:240
  81.7 3.8 %collective-permute-start.5 = (bf16[256,768]{1,0:T(8,128)(2,1)S(1)}, bf16[256,768]{1,0:T(8,128)(2,1)S(1)}, u32[]{:S(2)}, u32[]{:S(2)}) collective-permute-start(bf16[256,768]{1,0:T(8,128)(2,1)S(1)} %get-tuple-element.39), channel_id=1, source_target_pairs={{0,32},{16,48},{32,0},{48,16},{1,33},{17,49},{33,1},{49,17},{2,34}... | collective-permute-start | bytes 1179656 | tf_op jit(solution)/shard_map/ppermute | solution.py:240
  85.5 1.9 collective-permute-start.6
  87.4 11.4 %collective-permute-done.4.p1 = bf16[256,768]{1,0:T(8,128)(2,1)S(1)} collective-permute-done((bf16[256,768]{1,0:T(8,128)(2,1)S(1)}, bf16[256,768]{1,0:T(8,128)(2,1)S(1)}, u32[]{:S(2)}, u32[]{:S(2)}) %collective-permute-start.4) | collective-permute-done | bytes 393248 | tf_op jit(solution)/shard_map/ppermute | solution.py:240
  98.8 5.6 %collective-permute-done.6.p3 = bf16[256,768]{1,0:T(8,128)(2,1)S(1)} collective-permute-done((bf16[256,768]{1,0:T(8,128)(2,1)S(1)}, bf16[256,768]{1,0:T(8,128)(2,1)S(1)}, u32[]{:S(2)}, u32[]{:S(2)}) %collective-permute-start.6) | collective-permute-done | bytes 393248 | tf_op jit(solution)/shard_map/ppermute | solution.py:240
  105.2 3.6 %shard_map.125 = (bf16[256,512]{1,0:T(8,128)(2,1)}, bf16[256,128]{1,0:T(8,128)(2,1)}, f32[4,256,256]{2,1,0:T(8,128)}, bf16[256,512]{1,0:T(8,128)(2,1)}) custom-call(f32[256,768]{1,0:T(8,128)} %copy-done.10, bf16[256,768]{1,0:T(8,128)(2,1)} %copy-done.15, bf16[256,768]{1,0:T(8,128)(2,1)} %copy-done.16, bf16[256,768]{1,0:T(8,128)(2,1)} %copy-done.17, ...), custom_call_target="tpu_custom_call" | custom-call | tf_op jit(solution)/shard_map/pallas_call | solution.py:229
  108.8 8.2 %collective-permute-start.7 = (bf16[256,512]{1,0:T(8,128)(2,1)}, bf16[256,512]{1,0:T(8,128)(2,1)S(1)}, u32[]{:S(2)}, u32[]{:S(2)}) collective-permute-start(bf16[256,512]{1,0:T(8,128)(2,1)} %get-tuple-element.44.own), channel_id=1, source_target_pairs={{0,1},{1,0},{2,3},{3,2},{4,5},{5,4},{6,7},{7,6},{8,9},{9,8},{10,11... | collective-permute-start | bytes 786440 | tf_op jit(solution)/shard_map/ppermute | solution.py:240
  117.0 17.5 %collective-permute-done.7.oth = bf16[256,512]{1,0:T(8,128)(2,1)S(1)} collective-permute-done((bf16[256,512]{1,0:T(8,128)(2,1)}, bf16[256,512]{1,0:T(8,128)(2,1)S(1)}, u32[]{:S(2)}, u32[]{:S(2)}) %collective-permute-start.7) | collective-permute-done | bytes 262176 | tf_op jit(solution)/shard_map/ppermute | solution.py:240
  134.5 7.4 %all-gather.2.cloned.1.call-done.weight = bf16[8,4,2,64,512]{4,3,2,1,0:T(8,128)(2,1)} async-done(((bf16[1,4,2,64,512]{4,3,2,1,0:T(8,128)(2,1)}), bf16[8,4,2,64,512]{4,3,2,1,0:T(8,128)(2,1)}) %all-gather.2.cloned.1.call-update) | async-done | bytes 4194320 | tf_op jit(solution)/shard_map/all_gather | solution.py:294
  141.9 2.2 copy-done.1
  147.9 4.2 %all-to-all-start.2 = ((bf16[4,256,512]{2,1,0:T(8,128)(2,1)}), bf16[4,256,512]{2,1,0:T(8,128)(2,1)S(1)}, u32[]{:S(2)}, u32[]{:S(2)}) async-start(bf16[4,256,512]{2,1,0:T(8,128)(2,1)} %copy-done.3), calls=%async_computation.2 | async-start | bytes 2097152 | tf_op jit(solution)/shard_map/all_to_all | solution.py:314
  152.3 15.3 %all-to-all-done.2.blocks = bf16[4,256,512]{2,1,0:T(8,128)(2,1)S(1)} async-done(((bf16[4,256,512]{2,1,0:T(8,128)(2,1)}), bf16[4,256,512]{2,1,0:T(8,128)(2,1)S(1)}, u32[]{:S(2)}, u32[]{:S(2)}) %all-to-all-start.2) | async-done | bytes 1048608 | tf_op jit(solution)/shard_map/all_to_all | solution.py:314
  168.6 17.1 %all_to_all.30.errors = bf16[4,256,512]{2,1,0:T(8,128)(2,1)S(1)} all-to-all(bf16[4,256,512]{2,1,0:T(8,128)(2,1)S(1)} %get-tuple-element.48), channel_id=1, replica_groups=mesh['zl'=8,'y'=4,'c'=2,'x'=4,'zh'=2] {'x'}, dimensions={0} | all-to-all | bytes 2097152 | tf_op jit(solution)/shard_map/all_to_all | solution.py:323
  185.6 2.2 copy-done.2
  189.1 12.0 %collective-permute-start.9 = (bf16[256,512]{1,0:T(8,128)(2,1)S(1)}, bf16[256,512]{1,0:T(8,128)(2,1)S(1)}, u32[]{:S(2)}, u32[]{:S(2)}) collective-permute-start(bf16[256,512]{1,0:T(8,128)(2,1)S(1)} %shard_map.130), channel_id=1, source_target_pairs={{0,1},{1,0},{2,3},{3,2},{4,5},{5,4},{6,7},{7,6},{8,9},{9,8},{10,11... | collective-permute-start | bytes 786440 | tf_op jit(solution)/shard_map/ppermute | solution.py:240
  202.4 19.6 %collective-permute-done.9.d_other = bf16[256,512]{1,0:T(8,128)(2,1)S(1)} collective-permute-done((bf16[256,512]{1,0:T(8,128)(2,1)S(1)}, bf16[256,512]{1,0:T(8,128)(2,1)S(1)}, u32[]{:S(2)}, u32[]{:S(2)}) %collective-permute-start.9) | collective-permute-done | bytes 262176 | tf_op jit(solution)/shard_map/ppermute | solution.py:240
  223.2 9.3 %all_to_all.31.d_keys = bf16[4,256,128]{2,1,0:T(8,128)(2,1)S(1)} all-to-all(bf16[4,256,128]{2,1,0:T(8,128)(2,1)S(1)} %shard_map.131), channel_id=1, replica_groups=mesh['zl'=8,'y'=4,'c'=2,'x'=4,'zh'=2] {'y'}, dimensions={0} | all-to-all | bytes 524288 | tf_op jit(solution)/shard_map/all_to_all | solution.py:331
  232.5 2.1 shard_map.132
  234.7 1.9 collective-permute-start.10
  238.0 21.5 %all_to_all.32.parts = bf16[8,64,128]{2,1,0:T(8,128)(2,1)S(1)} all-to-all(bf16[8,64,128]{2,1,0:T(8,128)(2,1)S(1)} %add_convert_fusion), channel_id=1, replica_groups=mesh['zl'=8,'y'=4,'c'=2,'x'=4,'zh'=2] {'zl'}, dimensions={0} | all-to-all | bytes 262144 | tf_op jit(solution)/shard_map/all_to_all | solution.py:335
  (71 shorter events, 19.1 us)
Async XLA Ops:
  7.2 145.1 %copy-start = (bf16[256,4096]{1,0:T(8,128)(2,1)S(1)}, bf16[256,4096]{1,0:T(8,128)(2,1)}, u32[]{:S(2)}) copy-start(bf16[256,4096]{1,0:T(8,128)(2,1)} %param.12) | copy-start | bytes 6291460
  7.2 32.1 %copy-start.18 = (bf16[512,64]{0,1:T(8,128)(2,1)S(1)}, bf16[512,64]{0,1:T(8,128)(2,1)}, u32[]{:S(2)}) copy-start(bf16[512,64]{0,1:T(8,128)(2,1)} %param.16) | copy-start | bytes 196612
  7.2 32.2 %copy-start.19 = (s32[128,64]{0,1:T(8,128)S(1)}, s32[128,64]{0,1:T(8,128)}, u32[]{:S(2)}) copy-start(s32[128,64]{0,1:T(8,128)} %param.20) | copy-start | bytes 98308
  9.3 37.4 %copy-start.20 = (s32[1,3]{1,0:T(1,128)S(1)}, s32[1,3]{1,0:T(1,128)}, u32[]{:S(2)}) copy-start(s32[1,3]{1,0:T(1,128)} %param.21) | copy-start | bytes 40
  9.3 48.8 %all-to-all-start = ((bf16[8,48,768]{2,1,0:T(8,128)(2,1)}), bf16[8,48,768]{2,1,0:T(8,128)(2,1)S(1)}, u32[]{:S(2)}, u32[]{:S(2)}) async-start(bf16[8,48,768]{2,1,0:T(8,128)(2,1)} %shard_map.122), calls=%async_computation | async-start | bytes 1179648 | tf_op jit(solution)/shard_map/all_to_all | solution.py:262
  22.1 1.6 copy-start.6
  27.7 48.5 %copy-start.4 = (bf16[256,1024]{1,0:T(8,128)(2,1)}, bf16[256,1024]{1,0:T(8,128)(2,1)S(1)}, u32[]{:S(2)}) copy-start(bf16[256,1024]{1,0:T(8,128)(2,1)S(1)} %get-tuple-element.33.s0) | copy-start | bytes 1572868
  27.7 21.5 %collective-permute-start = (bf16[256,1024]{1,0:T(8,128)(2,1)}, bf16[256,1024]{1,0:T(8,128)(2,1)}, u32[]{:S(2)}, u32[]{:S(2)}) collective-permute-start(bf16[256,1024]{1,0:T(8,128)(2,1)} %get-tuple-element.29), channel_id=1, source_target_pairs={{0,16},{16,32},{32,48},{48,0},{1,17},{17,33},{33,49},{49,1},{2,18}... | collective-permute-start | bytes 1572872 | tf_op jit(solution)/shard_map/ppermute | solution.py:240
  31.2 25.5 %collective-permute-start.1 = (bf16[256,1024]{1,0:T(8,128)(2,1)}, bf16[256,1024]{1,0:T(8,128)(2,1)}, u32[]{:S(2)}, u32[]{:S(2)}) collective-permute-start(bf16[256,1024]{1,0:T(8,128)(2,1)} %get-tuple-element.30), channel_id=1, source_target_pairs={{0,32},{16,48},{32,0},{48,16},{1,33},{17,49},{33,1},{49,17},{2,34}... | collective-permute-start | bytes 1572872 | tf_op jit(solution)/shard_map/ppermute | solution.py:240
  36.0 22.1 %collective-permute-start.2 = (bf16[256,1024]{1,0:T(8,128)(2,1)}, bf16[256,1024]{1,0:T(8,128)(2,1)}, u32[]{:S(2)}, u32[]{:S(2)}) collective-permute-start(bf16[256,1024]{1,0:T(8,128)(2,1)} %get-tuple-element.31), channel_id=1, source_target_pairs={{0,48},{16,0},{32,16},{48,32},{1,49},{17,1},{33,17},{49,33},{2,50}... | collective-permute-start | bytes 1572872 | tf_op jit(solution)/shard_map/ppermute | solution.py:240
  39.9 18.2 %collective-permute-start.8 = (bf16[64,512]{1,0:T(8,128)(2,1)S(1)}, bf16[64,512]{1,0:T(8,128)(2,1)S(1)}, u32[]{:S(2)}, u32[]{:S(2)}) collective-permute-start(bf16[64,512]{1,0:T(8,128)(2,1)S(1)} %shard_map.126), channel_id=1, source_target_pairs={{0,0},{1,64},{64,1},{65,65},{128,128},{129,192},{192,129},{193,193... | collective-permute-start | bytes 196616 | tf_op jit(solution)/shard_map/ppermute | solution.py:279
  58.9 45.4 %all-to-all-start.1 = ((bf16[8,64,512]{2,1,0:T(8,128)(2,1)}), bf16[8,64,512]{2,1,0:T(8,128)(2,1)}, u32[]{:S(2)}, u32[]{:S(2)}) async-start(bf16[8,64,512]{2,1,0:T(8,128)(2,1)} %broadcast_in_dim.19), calls=%async_computation.1 | async-start | bytes 1048576 | tf_op jit(solution)/shard_map/all_to_all | solution.py:281
  68.8 73.1 %all-gather.2.cloned.1.call-start = ((), (), s32[]{:S(2)}) async-start(), calls=%async_computation.6 | async-start | bytes 4718592 | tf_op jit(solution)/shard_map/all_gather | solution.py:294
  68.9 3.9 %collective-permute-start.3 = (bf16[8,48,768]{2,1,0:T(8,128)(2,1)S(1)}, bf16[8,48,768]{2,1,0:T(8,128)(2,1)S(1)}, u32[]{:S(2)}, u32[]{:S(2)}) collective-permute-start(bf16[8,48,768]{2,1,0:T(8,128)(2,1)S(1)} %all-to-all-done.w_own), channel_id=1, source_target_pairs={{0,8},{8,0},{1,9},{9,1},{2,10},{10,2},{3,11},{11,3},{4,12},{12,4},... | collective-permute-start | bytes 1769480 | tf_op jit(solution)/shard_map/ppermute | solution.py:240
  77.1 21.6 %collective-permute-start.4 = (bf16[256,768]{1,0:T(8,128)(2,1)S(1)}, bf16[256,768]{1,0:T(8,128)(2,1)S(1)}, u32[]{:S(2)}, u32[]{:S(2)}) collective-permute-start(bf16[256,768]{1,0:T(8,128)(2,1)S(1)} %get-tuple-element.38), channel_id=1, source_target_pairs={{0,48},{16,0},{32,16},{48,32},{1,49},{17,1},{33,17},{49,33},{2,50}... | collective-permute-start | bytes 1179656 | tf_op jit(solution)/shard_map/ppermute | solution.py:240
  81.7 17.1 %collective-permute-start.5 = (bf16[256,768]{1,0:T(8,128)(2,1)S(1)}, bf16[256,768]{1,0:T(8,128)(2,1)S(1)}, u32[]{:S(2)}, u32[]{:S(2)}) collective-permute-start(bf16[256,768]{1,0:T(8,128)(2,1)S(1)} %get-tuple-element.39), channel_id=1, source_target_pairs={{0,32},{16,48},{32,0},{48,16},{1,33},{17,49},{33,1},{49,17},{2,34}... | collective-permute-start | bytes 1179656 | tf_op jit(solution)/shard_map/ppermute | solution.py:240
  85.5 18.9 %collective-permute-start.6 = (bf16[256,768]{1,0:T(8,128)(2,1)S(1)}, bf16[256,768]{1,0:T(8,128)(2,1)S(1)}, u32[]{:S(2)}, u32[]{:S(2)}) collective-permute-start(bf16[256,768]{1,0:T(8,128)(2,1)S(1)} %get-tuple-element.40), channel_id=1, source_target_pairs={{0,16},{16,32},{32,48},{48,0},{1,17},{17,33},{33,49},{49,1},{2,18}... | collective-permute-start | bytes 1179656 | tf_op jit(solution)/shard_map/ppermute | solution.py:240
  98.8 5.6 %copy-start.15 = (bf16[256,768]{1,0:T(8,128)(2,1)}, bf16[256,768]{1,0:T(8,128)(2,1)S(1)}, u32[]{:S(2)}) copy-start(bf16[256,768]{1,0:T(8,128)(2,1)S(1)} %collective-permute-done.4.p1) | copy-start | bytes 1179652
  98.8 5.6 %copy-start.16 = (bf16[256,768]{1,0:T(8,128)(2,1)}, bf16[256,768]{1,0:T(8,128)(2,1)S(1)}, u32[]{:S(2)}) copy-start(bf16[256,768]{1,0:T(8,128)(2,1)S(1)} %collective-permute-done.5.p2) | copy-start | bytes 1179652
  108.8 25.8 %collective-permute-start.7 = (bf16[256,512]{1,0:T(8,128)(2,1)}, bf16[256,512]{1,0:T(8,128)(2,1)S(1)}, u32[]{:S(2)}, u32[]{:S(2)}) collective-permute-start(bf16[256,512]{1,0:T(8,128)(2,1)} %get-tuple-element.44.own), channel_id=1, source_target_pairs={{0,1},{1,0},{2,3},{3,2},{4,5},{5,4},{6,7},{7,6},{8,9},{9,8},{10,11... | collective-permute-start | bytes 786440 | tf_op jit(solution)/shard_map/ppermute | solution.py:240
  141.9 2.2 copy-start.1
  147.9 19.8 %all-to-all-start.2 = ((bf16[4,256,512]{2,1,0:T(8,128)(2,1)}), bf16[4,256,512]{2,1,0:T(8,128)(2,1)S(1)}, u32[]{:S(2)}, u32[]{:S(2)}) async-start(bf16[4,256,512]{2,1,0:T(8,128)(2,1)} %copy-done.3), calls=%async_computation.2 | async-start | bytes 2097152 | tf_op jit(solution)/shard_map/all_to_all | solution.py:314
  185.6 2.2 copy-start.2
  189.1 33.0 %copy-start.7 = (f32[256,128]{1,0:T(8,128)S(1)}, f32[256,128]{1,0:T(8,128)}, u32[]{:S(2)}) copy-start(f32[256,128]{1,0:T(8,128)} %get-tuple-element.41.cos) | copy-start | bytes 393220
  189.1 33.0 %copy-start.8 = (f32[256,128]{1,0:T(8,128)S(1)}, f32[256,128]{1,0:T(8,128)}, u32[]{:S(2)}) copy-start(f32[256,128]{1,0:T(8,128)} %get-tuple-element.42.sin) | copy-start | bytes 393220
  189.1 33.0 %copy-start.9 = (f32[4,256,256]{2,1,0:T(8,128)S(1)}, f32[4,256,256]{2,1,0:T(8,128)}, u32[]{:S(2)}) copy-start(f32[4,256,256]{2,1,0:T(8,128)} %get-tuple-element.51.prob_ref) | copy-start | bytes 3145732
  189.1 33.0 %copy-start.12 = (bf16[256,512]{1,0:T(8,128)(2,1)S(1)}, bf16[256,512]{1,0:T(8,128)(2,1)}, u32[]{:S(2)}) copy-start(bf16[256,512]{1,0:T(8,128)(2,1)} %get-tuple-element.49.q_ref) | copy-start | bytes 786436
  189.1 33.0 %copy-start.13 = (bf16[256,128]{1,0:T(8,128)(2,1)S(1)}, bf16[256,128]{1,0:T(8,128)(2,1)}, u32[]{:S(2)}) copy-start(bf16[256,128]{1,0:T(8,128)(2,1)} %get-tuple-element.50.v_ref) | copy-start | bytes 196612
  189.1 32.9 %collective-permute-start.9 = (bf16[256,512]{1,0:T(8,128)(2,1)S(1)}, bf16[256,512]{1,0:T(8,128)(2,1)S(1)}, u32[]{:S(2)}, u32[]{:S(2)}) collective-permute-start(bf16[256,512]{1,0:T(8,128)(2,1)S(1)} %shard_map.130), channel_id=1, source_target_pairs={{0,1},{1,0},{2,3},{3,2},{4,5},{5,4},{6,7},{7,6},{8,9},{9,8},{10,11... | collective-permute-start | bytes 786440 | tf_op jit(solution)/shard_map/ppermute | solution.py:240
  202.4 30.1 %copy-start.5 = (bf16[256,1024]{1,0:T(8,128)(2,1)S(1)}, bf16[256,1024]{1,0:T(8,128)(2,1)}, u32[]{:S(2)}) copy-start(bf16[256,1024]{1,0:T(8,128)(2,1)} %copy-done.4) | copy-start | bytes 1572868
  223.2 36.3 %copy-start.14 = (s32[16,128]{1,0:T(8,128)S(1)}, s32[16,128]{1,0:T(8,128)}, u32[]{:S(2)}) copy-start(s32[16,128]{1,0:T(8,128)} %codes.1) | copy-start | bytes 24580
  234.7 3.2 %collective-permute-start.10 = (bf16[8,64,128]{2,1,0:T(8,128)(2,1)S(1)}, bf16[8,64,128]{2,1,0:T(8,128)(2,1)S(1)}, u32[]{:S(2)}, u32[]{:S(2)}) collective-permute-start(bf16[8,64,128]{2,1,0:T(8,128)(2,1)S(1)} %get-tuple-element.53), channel_id=1, source_target_pairs={{0,8},{8,0},{1,9},{9,1},{2,10},{10,2},{3,11},{11,3},{4,12},{12,4},... | collective-permute-start | bytes 393224 | tf_op jit(solution)/shard_map/ppermute | solution.py:240
  (4 other events, 3.6 us)
Sparse Core Ops, SparseCore 0:
  104.5 37.3 all-gather.1

commit v4 on v3

--- a/solution.py
+++ b/solution.py
@@ -268,7 +268,8 @@
     spot = jnp.arange(tokens)
     allow = (segment[:, None] == segment[None, :]) & (spot[None, :] <= spot[:, None])
     allow = allow.astype(F32)
-    w_own, cos, sin, allow, *slots = lax.optimization_barrier((w_own, cos, sin, allow, *slots))
+    w_oth = shifted(w_own, "c", 1)
+    w_own, w_oth, cos, sin, allow, *slots = lax.optimization_barrier((w_own, w_oth, cos, sin, allow, *slots))
 
     out_mine = call(mask_out_kernel, shape((ow.shape[1], ow.shape[0])), ow, oc)
     trade = []
@@ -280,7 +281,6 @@
     out_mine = after(out_mine, w_own)
     out_z = lax.all_to_all(copies(out_mine, n_z), "zl", 0, 0)
 
-    w_oth = shifted(w_own, "c", 1)
     terms = call(
         project_kernel,
         [shape((tokens, width), F32)] + [shape((tokens, width))] * (n_y - 1),

time: 268 us -> 265 us (0.989)
  waiting for transfers between devices: 89 us -> 84.4 us
    ppermute x10, waiting for transfers between devices: 66.3 us -> 57.3 us  [shifted(): lax.ppermute(value, axis, [(i, (i + by) % size) for i in range(size)])]
    all_to_all x1, waiting for transfers between devices: 0.01 us -> 4.36 us  [shards(): w_own = lax.all_to_all(mine, 'zl', 0, 0)]
    unnamed x44 -> x48, local copies, waits for them, and re-layouts: 9.81 us -> 11.7 us
where the time goes in v4:
time: 265 us; the launch traced here: 264 us
  waiting for transfers between devices  84.4 us (32%)
  starting transfers between devices  79.6 us (30%)
  blocking collectives  48.1 us (18%)
  Pallas kernels  22.6 us (9%)
  between operations  14.4 us (5%)
  local copies, waits for them, and re-layouts  12.7 us (5%)
    ppermute x10, waiting for transfers between devices, shifted(): lax.ppermute(value, axis, [(i, (i + by) % size) for i in range(size)])  57.3 us
    ppermute x10, starting transfers between devices, shifted(): lax.ppermute(value, axis, [(i, (i + by) % size) for i in range(size)])  45.9 us
    pallas_call x12, Pallas kernels, call(): pl.pallas_call(kernel, out_shape=out_shape, in_specs=specs, compiler_para...  22.6 us
    all_to_all x1, blocking collectives, shards(): grad = lax.all_to_all(grad, 'zl', 0, 0)  21.5 us
    all_to_all x1, blocking collectives, shards(): errors = lax.all_to_all(error, 'x', 0, 0)  17.1 us
    all_to_all x1, waiting for transfers between devices, shards(): blocks = lax.all_to_all(part, 'x', 0, 0)  15.3 us
    all_to_all x1, starting transfers between devices, shards(): w_own = lax.all_to_all(mine, 'zl', 0, 0)  12.8 us
    unnamed x48, local copies, waits for them, and re-layouts  11.7 us
  transfers between devices with their start and end apart: 15, of which 10 were waited for; matrix products, arithmetic and copies ran while one was open for 1% of the time, Pallas kernels for 5%

profile of v4, /device:TPU:32, one launch (start us, length us, event | category | flops | bytes accessed | tf_op | source)
XLA Modules:
  0.0 264.4 jit_solution(384926405625598311)
XLA Ops:
  7.2 2.0 shard_map.122
  9.3 12.8 %all-to-all-start = ((bf16[8,48,768]{2,1,0:T(8,128)(2,1)}), bf16[8,48,768]{2,1,0:T(8,128)(2,1)S(1)}, u32[]{:S(2)}, u32[]{:S(2)}) async-start(bf16[8,48,768]{2,1,0:T(8,128)(2,1)} %shard_map.122), calls=%async_computation | async-start | bytes 1179648 | tf_op jit(solution)/shard_map/all_to_all | solution.py:262
  23.7 4.0 %shard_map.123 = (bf16[256,1024]{1,0:T(8,128)(2,1)S(1)}, bf16[256,1024]{1,0:T(8,128)(2,1)}, bf16[256,1024]{1,0:T(8,128)(2,1)}, bf16[256,1024]{1,0:T(8,128)(2,1)}) custom-call(s32[3]{0:T(128)S(1)} %pad_add_fusion.at_ref, bf16[256,4096]{1,0:T(8,128)(2,1)S(1)} %copy-done.6), custom_call_target="tpu_custom_call" | custom-call | tf_op jit(solution)/shard_map/pallas_call | solution.py:229
  27.7 3.5 %collective-permute-start.1 = (bf16[256,1024]{1,0:T(8,128)(2,1)}, bf16[256,1024]{1,0:T(8,128)(2,1)}, u32[]{:S(2)}, u32[]{:S(2)}) collective-permute-start(bf16[256,1024]{1,0:T(8,128)(2,1)} %get-tuple-element.30), channel_id=1, source_target_pairs={{0,16},{16,32},{32,48},{48,0},{1,17},{17,33},{33,49},{49,1},{2,18}... | collective-permute-start | bytes 1572872 | tf_op jit(solution)/shard_map/ppermute | solution.py:240
  31.2 4.8 %collective-permute-start.2 = (bf16[256,1024]{1,0:T(8,128)(2,1)}, bf16[256,1024]{1,0:T(8,128)(2,1)}, u32[]{:S(2)}, u32[]{:S(2)}) collective-permute-start(bf16[256,1024]{1,0:T(8,128)(2,1)} %get-tuple-element.31), channel_id=1, source_target_pairs={{0,32},{16,48},{32,0},{48,16},{1,33},{17,49},{33,1},{49,17},{2,34}... | collective-permute-start | bytes 1572872 | tf_op jit(solution)/shard_map/ppermute | solution.py:240
  36.0 3.3 %collective-permute-start.3 = (bf16[256,1024]{1,0:T(8,128)(2,1)}, bf16[256,1024]{1,0:T(8,128)(2,1)}, u32[]{:S(2)}, u32[]{:S(2)}) collective-permute-start(bf16[256,1024]{1,0:T(8,128)(2,1)} %get-tuple-element.32), channel_id=1, source_target_pairs={{0,48},{16,0},{32,16},{48,32},{1,49},{17,1},{33,17},{49,33},{2,50}... | collective-permute-start | bytes 1572872 | tf_op jit(solution)/shard_map/ppermute | solution.py:240
  39.9 6.8 %collective-permute-start.8 = (bf16[64,512]{1,0:T(8,128)(2,1)S(1)}, bf16[64,512]{1,0:T(8,128)(2,1)S(1)}, u32[]{:S(2)}, u32[]{:S(2)}) collective-permute-start(bf16[64,512]{1,0:T(8,128)(2,1)S(1)} %shard_map.126), channel_id=1, source_target_pairs={{0,0},{1,64},{64,1},{65,65},{128,128},{129,192},{192,129},{193,193... | collective-permute-start | bytes 196616 | tf_op jit(solution)/shard_map/ppermute | solution.py:280
  47.8 4.4 %all-to-all-done.w_own = bf16[8,48,768]{2,1,0:T(8,128)(2,1)S(1)} async-done(((bf16[8,48,768]{2,1,0:T(8,128)(2,1)}), bf16[8,48,768]{2,1,0:T(8,128)(2,1)S(1)}, u32[]{:S(2)}, u32[]{:S(2)}) %all-to-all-start) | async-done | bytes 589856 | tf_op jit(solution)/shard_map/all_to_all | solution.py:262
  52.1 1.9 collective-permute-start
  59.8 9.9 %all-to-all-start.1 = ((bf16[8,64,512]{2,1,0:T(8,128)(2,1)}), bf16[8,64,512]{2,1,0:T(8,128)(2,1)}, u32[]{:S(2)}, u32[]{:S(2)}) async-start(bf16[8,64,512]{2,1,0:T(8,128)(2,1)} %broadcast_in_dim.19), calls=%async_computation.1 | async-start | bytes 1048576 | tf_op jit(solution)/shard_map/all_to_all | solution.py:282
  70.8 3.5 %shard_map.124 = (f32[256,768]{1,0:T(8,128)S(1)}, bf16[256,768]{1,0:T(8,128)(2,1)S(1)}, bf16[256,768]{1,0:T(8,128)(2,1)S(1)}, bf16[256,768]{1,0:T(8,128)(2,1)S(1)}) custom-call(bf16[8,48,768]{2,1,0:T(8,128)(2,1)S(1)} %all-to-all-done.w_own, bf16[8,48,768]{2,1,0:T(8,128)(2,1)S(1)} %copy-done.12, bf16[256,1024]{1,0:T(8,128)(2,1)S(1)} %get-tuple-element.35.s0, ...), custom_call_target="tpu_custom_call" | custom-call | tf_op jit(solution)/shard_map/pallas_call | solution.py:229
  75.2 4.5 %collective-permute-start.4 = (bf16[256,768]{1,0:T(8,128)(2,1)S(1)}, bf16[256,768]{1,0:T(8,128)(2,1)S(1)}, u32[]{:S(2)}, u32[]{:S(2)}) collective-permute-start(bf16[256,768]{1,0:T(8,128)(2,1)S(1)} %get-tuple-element.40), channel_id=1, source_target_pairs={{0,48},{16,0},{32,16},{48,32},{1,49},{17,1},{33,17},{49,33},{2,50}... | collective-permute-start | bytes 1179656 | tf_op jit(solution)/shard_map/ppermute | solution.py:240
  79.7 3.8 %collective-permute-start.5 = (bf16[256,768]{1,0:T(8,128)(2,1)S(1)}, bf16[256,768]{1,0:T(8,128)(2,1)S(1)}, u32[]{:S(2)}, u32[]{:S(2)}) collective-permute-start(bf16[256,768]{1,0:T(8,128)(2,1)S(1)} %get-tuple-element.41), channel_id=1, source_target_pairs={{0,32},{16,48},{32,0},{48,16},{1,33},{17,49},{33,1},{49,17},{2,34}... | collective-permute-start | bytes 1179656 | tf_op jit(solution)/shard_map/ppermute | solution.py:240
  83.5 1.9 collective-permute-start.6
  85.5 10.7 %collective-permute-done.4.p1 = bf16[256,768]{1,0:T(8,128)(2,1)S(1)} collective-permute-done((bf16[256,768]{1,0:T(8,128)(2,1)S(1)}, bf16[256,768]{1,0:T(8,128)(2,1)S(1)}, u32[]{:S(2)}, u32[]{:S(2)}) %collective-permute-start.4) | collective-permute-done | bytes 393248 | tf_op jit(solution)/shard_map/ppermute | solution.py:240
  96.2 5.6 %collective-permute-done.6.p3 = bf16[256,768]{1,0:T(8,128)(2,1)S(1)} collective-permute-done((bf16[256,768]{1,0:T(8,128)(2,1)S(1)}, bf16[256,768]{1,0:T(8,128)(2,1)S(1)}, u32[]{:S(2)}, u32[]{:S(2)}) %collective-permute-start.6) | collective-permute-done | bytes 393248 | tf_op jit(solution)/shard_map/ppermute | solution.py:240
  102.5 3.6 %shard_map.125 = (bf16[256,512]{1,0:T(8,128)(2,1)}, bf16[256,128]{1,0:T(8,128)(2,1)}, f32[4,256,256]{2,1,0:T(8,128)}, bf16[256,512]{1,0:T(8,128)(2,1)}) custom-call(f32[256,768]{1,0:T(8,128)} %copy-done.10, bf16[256,768]{1,0:T(8,128)(2,1)} %copy-done.17, bf16[256,768]{1,0:T(8,128)(2,1)} %copy-done.18, bf16[256,768]{1,0:T(8,128)(2,1)} %copy-done.19, ...), custom_call_target="tpu_custom_call" | custom-call | tf_op jit(solution)/shard_map/pallas_call | solution.py:229
  106.1 8.2 %collective-permute-start.7 = (bf16[256,512]{1,0:T(8,128)(2,1)}, bf16[256,512]{1,0:T(8,128)(2,1)S(1)}, u32[]{:S(2)}, u32[]{:S(2)}) collective-permute-start(bf16[256,512]{1,0:T(8,128)(2,1)} %get-tuple-element.46.own), channel_id=1, source_target_pairs={{0,1},{1,0},{2,3},{3,2},{4,5},{5,4},{6,7},{7,6},{8,9},{9,8},{10,11... | collective-permute-start | bytes 786440 | tf_op jit(solution)/shard_map/ppermute | solution.py:240
  114.3 17.6 %collective-permute-done.7.oth = bf16[256,512]{1,0:T(8,128)(2,1)S(1)} collective-permute-done((bf16[256,512]{1,0:T(8,128)(2,1)}, bf16[256,512]{1,0:T(8,128)(2,1)S(1)}, u32[]{:S(2)}, u32[]{:S(2)}) %collective-permute-start.7) | collective-permute-done | bytes 262176 | tf_op jit(solution)/shard_map/ppermute | solution.py:240
  131.9 7.4 %all-gather.2.cloned.1.call-done.weight = bf16[8,4,2,64,512]{4,3,2,1,0:T(8,128)(2,1)} async-done(((bf16[1,4,2,64,512]{4,3,2,1,0:T(8,128)(2,1)}), bf16[8,4,2,64,512]{4,3,2,1,0:T(8,128)(2,1)}) %all-gather.2.cloned.1.call-update) | async-done | bytes 4194320 | tf_op jit(solution)/shard_map/all_gather | solution.py:294
  139.3 2.2 copy-done.1
  142.4 1.8 shard_map.127
  145.2 4.2 %all-to-all-start.2 = ((bf16[4,256,512]{2,1,0:T(8,128)(2,1)}), bf16[4,256,512]{2,1,0:T(8,128)(2,1)S(1)}, u32[]{:S(2)}, u32[]{:S(2)}) async-start(bf16[4,256,512]{2,1,0:T(8,128)(2,1)} %copy-done.3), calls=%async_computation.2 | async-start | bytes 2097152 | tf_op jit(solution)/shard_map/all_to_all | solution.py:314
  149.7 15.3 %all-to-all-done.2.blocks = bf16[4,256,512]{2,1,0:T(8,128)(2,1)S(1)} async-done(((bf16[4,256,512]{2,1,0:T(8,128)(2,1)}), bf16[4,256,512]{2,1,0:T(8,128)(2,1)S(1)}, u32[]{:S(2)}, u32[]{:S(2)}) %all-to-all-start.2) | async-done | bytes 1048608 | tf_op jit(solution)/shard_map/all_to_all | solution.py:314
  165.9 17.1 %all_to_all.30.errors = bf16[4,256,512]{2,1,0:T(8,128)(2,1)S(1)} all-to-all(bf16[4,256,512]{2,1,0:T(8,128)(2,1)S(1)} %get-tuple-element.50), channel_id=1, replica_groups=mesh['zl'=8,'y'=4,'c'=2,'x'=4,'zh'=2] {'x'}, dimensions={0} | all-to-all | bytes 2097152 | tf_op jit(solution)/shard_map/all_to_all | solution.py:323
  183.0 2.2 copy-done.2
  186.5 12.0 %collective-permute-start.9 = (bf16[256,512]{1,0:T(8,128)(2,1)S(1)}, bf16[256,512]{1,0:T(8,128)(2,1)S(1)}, u32[]{:S(2)}, u32[]{:S(2)}) collective-permute-start(bf16[256,512]{1,0:T(8,128)(2,1)S(1)} %shard_map.130), channel_id=1, source_target_pairs={{0,1},{1,0},{2,3},{3,2},{4,5},{5,4},{6,7},{7,6},{8,9},{9,8},{10,11... | collective-permute-start | bytes 786440 | tf_op jit(solution)/shard_map/ppermute | solution.py:240
  199.8 19.5 %collective-permute-done.9.d_other = bf16[256,512]{1,0:T(8,128)(2,1)S(1)} collective-permute-done((bf16[256,512]{1,0:T(8,128)(2,1)S(1)}, bf16[256,512]{1,0:T(8,128)(2,1)S(1)}, u32[]{:S(2)}, u32[]{:S(2)}) %collective-permute-start.9) | collective-permute-done | bytes 262176 | tf_op jit(solution)/shard_map/ppermute | solution.py:240
  220.4 9.5 %all_to_all.31.d_keys = bf16[4,256,128]{2,1,0:T(8,128)(2,1)S(1)} all-to-all(bf16[4,256,128]{2,1,0:T(8,128)(2,1)S(1)} %shard_map.131), channel_id=1, replica_groups=mesh['zl'=8,'y'=4,'c'=2,'x'=4,'zh'=2] {'y'}, dimensions={0} | all-to-all | bytes 524288 | tf_op jit(solution)/shard_map/all_to_all | solution.py:331
  229.9 2.1 shard_map.132
  232.1 1.9 collective-permute-start.10
  235.4 21.5 %all_to_all.32.parts = bf16[8,64,128]{2,1,0:T(8,128)(2,1)S(1)} all-to-all(bf16[8,64,128]{2,1,0:T(8,128)(2,1)S(1)} %add_convert_fusion), channel_id=1, replica_groups=mesh['zl'=8,'y'=4,'c'=2,'x'=4,'zh'=2] {'zl'}, dimensions={0} | all-to-all | bytes 262144 | tf_op jit(solution)/shard_map/all_to_all | solution.py:335
  (75 shorter events, 20.4 us)
Async XLA Ops:
  7.2 142.5 %copy-start = (bf16[256,4096]{1,0:T(8,128)(2,1)S(1)}, bf16[256,4096]{1,0:T(8,128)(2,1)}, u32[]{:S(2)}) copy-start(bf16[256,4096]{1,0:T(8,128)(2,1)} %param.12) | copy-start | bytes 6291460
  7.2 32.1 %copy-start.20 = (bf16[512,64]{0,1:T(8,128)(2,1)S(1)}, bf16[512,64]{0,1:T(8,128)(2,1)}, u32[]{:S(2)}) copy-start(bf16[512,64]{0,1:T(8,128)(2,1)} %param.16) | copy-start | bytes 196612
  7.2 32.2 %copy-start.21 = (s32[128,64]{0,1:T(8,128)S(1)}, s32[128,64]{0,1:T(8,128)}, u32[]{:S(2)}) copy-start(s32[128,64]{0,1:T(8,128)} %param.20) | copy-start | bytes 98308
  9.3 37.4 %copy-start.22 = (s32[1,3]{1,0:T(1,128)S(1)}, s32[1,3]{1,0:T(1,128)}, u32[]{:S(2)}) copy-start(s32[1,3]{1,0:T(1,128)} %param.21) | copy-start | bytes 40
  9.3 42.9 %all-to-all-start = ((bf16[8,48,768]{2,1,0:T(8,128)(2,1)}), bf16[8,48,768]{2,1,0:T(8,128)(2,1)S(1)}, u32[]{:S(2)}, u32[]{:S(2)}) async-start(bf16[8,48,768]{2,1,0:T(8,128)(2,1)} %shard_map.122), calls=%async_computation | async-start | bytes 1179648 | tf_op jit(solution)/shard_map/all_to_all | solution.py:262
  22.1 1.6 copy-start.6
  27.7 46.6 %copy-start.4 = (bf16[256,1024]{1,0:T(8,128)(2,1)}, bf16[256,1024]{1,0:T(8,128)(2,1)S(1)}, u32[]{:S(2)}) copy-start(bf16[256,1024]{1,0:T(8,128)(2,1)S(1)} %get-tuple-element.35.s0) | copy-start | bytes 1572868
  27.7 27.8 %collective-permute-start.1 = (bf16[256,1024]{1,0:T(8,128)(2,1)}, bf16[256,1024]{1,0:T(8,128)(2,1)}, u32[]{:S(2)}, u32[]{:S(2)}) collective-permute-start(bf16[256,1024]{1,0:T(8,128)(2,1)} %get-tuple-element.30), channel_id=1, source_target_pairs={{0,16},{16,32},{32,48},{48,0},{1,17},{17,33},{33,49},{49,1},{2,18}... | collective-permute-start | bytes 1572872 | tf_op jit(solution)/shard_map/ppermute | solution.py:240
  31.2 25.5 %collective-permute-start.2 = (bf16[256,1024]{1,0:T(8,128)(2,1)}, bf16[256,1024]{1,0:T(8,128)(2,1)}, u32[]{:S(2)}, u32[]{:S(2)}) collective-permute-start(bf16[256,1024]{1,0:T(8,128)(2,1)} %get-tuple-element.31), channel_id=1, source_target_pairs={{0,32},{16,48},{32,0},{48,16},{1,33},{17,49},{33,1},{49,17},{2,34}... | collective-permute-start | bytes 1572872 | tf_op jit(solution)/shard_map/ppermute | solution.py:240
  36.0 22.0 %collective-permute-start.3 = (bf16[256,1024]{1,0:T(8,128)(2,1)}, bf16[256,1024]{1,0:T(8,128)(2,1)}, u32[]{:S(2)}, u32[]{:S(2)}) collective-permute-start(bf16[256,1024]{1,0:T(8,128)(2,1)} %get-tuple-element.32), channel_id=1, source_target_pairs={{0,48},{16,0},{32,16},{48,32},{1,49},{17,1},{33,17},{49,33},{2,50}... | collective-permute-start | bytes 1572872 | tf_op jit(solution)/shard_map/ppermute | solution.py:240
  39.9 19.0 %collective-permute-start.8 = (bf16[64,512]{1,0:T(8,128)(2,1)S(1)}, bf16[64,512]{1,0:T(8,128)(2,1)S(1)}, u32[]{:S(2)}, u32[]{:S(2)}) collective-permute-start(bf16[64,512]{1,0:T(8,128)(2,1)S(1)} %shard_map.126), channel_id=1, source_target_pairs={{0,0},{1,64},{64,1},{65,65},{128,128},{129,192},{192,129},{193,193... | collective-permute-start | bytes 196616 | tf_op jit(solution)/shard_map/ppermute | solution.py:280
  52.1 6.0 %collective-permute-start = (bf16[8,48,768]{2,1,0:T(8,128)(2,1)S(1)}, bf16[8,48,768]{2,1,0:T(8,128)(2,1)S(1)}, u32[]{:S(2)}, u32[]{:S(2)}) collective-permute-start(bf16[8,48,768]{2,1,0:T(8,128)(2,1)S(1)} %all-to-all-done.w_own), channel_id=1, source_target_pairs={{0,8},{8,0},{1,9},{9,1},{2,10},{10,2},{3,11},{11,3},{4,12},{12,4},... | collective-permute-start | bytes 1769480 | tf_op jit(solution)/shard_map/ppermute | solution.py:240
  59.8 41.9 %all-to-all-start.1 = ((bf16[8,64,512]{2,1,0:T(8,128)(2,1)}), bf16[8,64,512]{2,1,0:T(8,128)(2,1)}, u32[]{:S(2)}, u32[]{:S(2)}) async-start(bf16[8,64,512]{2,1,0:T(8,128)(2,1)} %broadcast_in_dim.19), calls=%async_computation.1 | async-start | bytes 1048576 | tf_op jit(solution)/shard_map/all_to_all | solution.py:282
  69.7 69.6 %all-gather.2.cloned.1.call-start = ((), (), s32[]{:S(2)}) async-start(), calls=%async_computation.6 | async-start | bytes 4718592 | tf_op jit(solution)/shard_map/all_gather | solution.py:294
  75.2 21.0 %collective-permute-start.4 = (bf16[256,768]{1,0:T(8,128)(2,1)S(1)}, bf16[256,768]{1,0:T(8,128)(2,1)S(1)}, u32[]{:S(2)}, u32[]{:S(2)}) collective-permute-start(bf16[256,768]{1,0:T(8,128)(2,1)S(1)} %get-tuple-element.40), channel_id=1, source_target_pairs={{0,48},{16,0},{32,16},{48,32},{1,49},{17,1},{33,17},{49,33},{2,50}... | collective-permute-start | bytes 1179656 | tf_op jit(solution)/shard_map/ppermute | solution.py:240
  79.7 16.4 %collective-permute-start.5 = (bf16[256,768]{1,0:T(8,128)(2,1)S(1)}, bf16[256,768]{1,0:T(8,128)(2,1)S(1)}, u32[]{:S(2)}, u32[]{:S(2)}) collective-permute-start(bf16[256,768]{1,0:T(8,128)(2,1)S(1)} %get-tuple-element.41), channel_id=1, source_target_pairs={{0,32},{16,48},{32,0},{48,16},{1,33},{17,49},{33,1},{49,17},{2,34}... | collective-permute-start | bytes 1179656 | tf_op jit(solution)/shard_map/ppermute | solution.py:240
  83.5 18.2 %collective-permute-start.6 = (bf16[256,768]{1,0:T(8,128)(2,1)S(1)}, bf16[256,768]{1,0:T(8,128)(2,1)S(1)}, u32[]{:S(2)}, u32[]{:S(2)}) collective-permute-start(bf16[256,768]{1,0:T(8,128)(2,1)S(1)} %get-tuple-element.42), channel_id=1, source_target_pairs={{0,16},{16,32},{32,48},{48,0},{1,17},{17,33},{33,49},{49,1},{2,18}... | collective-permute-start | bytes 1179656 | tf_op jit(solution)/shard_map/ppermute | solution.py:240
  96.1 5.6 %copy-start.17 = (bf16[256,768]{1,0:T(8,128)(2,1)}, bf16[256,768]{1,0:T(8,128)(2,1)S(1)}, u32[]{:S(2)}) copy-start(bf16[256,768]{1,0:T(8,128)(2,1)S(1)} %collective-permute-done.4.p1) | copy-start | bytes 1179652
  96.2 5.6 %copy-start.18 = (bf16[256,768]{1,0:T(8,128)(2,1)}, bf16[256,768]{1,0:T(8,128)(2,1)S(1)}, u32[]{:S(2)}) copy-start(bf16[256,768]{1,0:T(8,128)(2,1)S(1)} %collective-permute-done.5.p2) | copy-start | bytes 1179652
  106.1 25.8 %collective-permute-start.7 = (bf16[256,512]{1,0:T(8,128)(2,1)}, bf16[256,512]{1,0:T(8,128)(2,1)S(1)}, u32[]{:S(2)}, u32[]{:S(2)}) collective-permute-start(bf16[256,512]{1,0:T(8,128)(2,1)} %get-tuple-element.46.own), channel_id=1, source_target_pairs={{0,1},{1,0},{2,3},{3,2},{4,5},{5,4},{6,7},{7,6},{8,9},{9,8},{10,11... | collective-permute-start | bytes 786440 | tf_op jit(solution)/shard_map/ppermute | solution.py:240
  139.3 2.2 copy-start.1
  145.2 19.8 %all-to-all-start.2 = ((bf16[4,256,512]{2,1,0:T(8,128)(2,1)}), bf16[4,256,512]{2,1,0:T(8,128)(2,1)S(1)}, u32[]{:S(2)}, u32[]{:S(2)}) async-start(bf16[4,256,512]{2,1,0:T(8,128)(2,1)} %copy-done.3), calls=%async_computation.2 | async-start | bytes 2097152 | tf_op jit(solution)/shard_map/all_to_all | solution.py:314
  183.0 2.2 copy-start.2
  186.4 32.9 %copy-start.7 = (f32[256,128]{1,0:T(8,128)S(1)}, f32[256,128]{1,0:T(8,128)}, u32[]{:S(2)}) copy-start(f32[256,128]{1,0:T(8,128)} %get-tuple-element.43.cos) | copy-start | bytes 393220
  186.4 32.9 %copy-start.8 = (f32[256,128]{1,0:T(8,128)S(1)}, f32[256,128]{1,0:T(8,128)}, u32[]{:S(2)}) copy-start(f32[256,128]{1,0:T(8,128)} %get-tuple-element.44.sin) | copy-start | bytes 393220
  186.4 32.9 %copy-start.9 = (f32[4,256,256]{2,1,0:T(8,128)S(1)}, f32[4,256,256]{2,1,0:T(8,128)}, u32[]{:S(2)}) copy-start(f32[4,256,256]{2,1,0:T(8,128)} %get-tuple-element.53.prob_ref) | copy-start | bytes 3145732
  186.4 32.9 %copy-start.14 = (bf16[256,512]{1,0:T(8,128)(2,1)S(1)}, bf16[256,512]{1,0:T(8,128)(2,1)}, u32[]{:S(2)}) copy-start(bf16[256,512]{1,0:T(8,128)(2,1)} %get-tuple-element.51.q_ref) | copy-start | bytes 786436
  186.5 32.9 %copy-start.15 = (bf16[256,128]{1,0:T(8,128)(2,1)S(1)}, bf16[256,128]{1,0:T(8,128)(2,1)}, u32[]{:S(2)}) copy-start(bf16[256,128]{1,0:T(8,128)(2,1)} %get-tuple-element.52.v_ref) | copy-start | bytes 196612
  186.5 32.8 %collective-permute-start.9 = (bf16[256,512]{1,0:T(8,128)(2,1)S(1)}, bf16[256,512]{1,0:T(8,128)(2,1)S(1)}, u32[]{:S(2)}, u32[]{:S(2)}) collective-permute-start(bf16[256,512]{1,0:T(8,128)(2,1)S(1)} %shard_map.130), channel_id=1, source_target_pairs={{0,1},{1,0},{2,3},{3,2},{4,5},{5,4},{6,7},{7,6},{8,9},{9,8},{10,11... | collective-permute-start | bytes 786440 | tf_op jit(solution)/shard_map/ppermute | solution.py:240
  199.8 30.2 %copy-start.5 = (bf16[256,1024]{1,0:T(8,128)(2,1)S(1)}, bf16[256,1024]{1,0:T(8,128)(2,1)}, u32[]{:S(2)}) copy-start(bf16[256,1024]{1,0:T(8,128)(2,1)} %copy-done.4) | copy-start | bytes 1572868
  220.4 36.4 %copy-start.16 = (s32[16,128]{1,0:T(8,128)S(1)}, s32[16,128]{1,0:T(8,128)}, u32[]{:S(2)}) copy-start(s32[16,128]{1,0:T(8,128)} %codes.1) | copy-start | bytes 24580
  232.1 3.2 %collective-permute-start.10 = (bf16[8,64,128]{2,1,0:T(8,128)(2,1)S(1)}, bf16[8,64,128]{2,1,0:T(8,128)(2,1)S(1)}, u32[]{:S(2)}, u32[]{:S(2)}) collective-permute-start(bf16[8,64,128]{2,1,0:T(8,128)(2,1)S(1)} %get-tuple-element.55), channel_id=1, source_target_pairs={{0,8},{8,0},{1,9},{9,1},{2,10},{10,2},{3,11},{11,3},{4,12},{12,4},... | collective-permute-start | bytes 393224 | tf_op jit(solution)/shard_map/ppermute | solution.py:240
  (6 other events, 5.5 us)
Sparse Core Ops, SparseCore 0:
  101.9 37.3 all-gather.1

commit v5 on v4

--- a/solution.py
+++ b/solution.py
@@ -290,7 +290,7 @@
     )
     terms = [terms[0]] + [shifted(terms[s], "y", -s) for s in range(1, n_y)]
 
-    out_z = after(out_z, *terms).reshape(n_z // 2, 2, ow.shape[1], ow.shape[0])
+    out_z = after(out_z, terms[1]).reshape(n_z // 2, 2, ow.shape[1], ow.shape[0])
     out_w = lax.all_gather(out_z, ("y", "c"), axis=0)
 
     queries, values, prob, att = call(
@@ -306,6 +306,7 @@
         sin,
         allow,
         mib=58,
+        flops=10**11,
     )
 
     att_oth = shifted(att, "zh", 1)

time: 265 us -> 264 us (level)
  waiting for transfers between devices: 84.4 us -> 72.5 us
  blocking collectives: 48.1 us -> 57.8 us
    all_to_all x1, blocking collectives: 21.5 us -> 31.1 us  [shards(): grad = lax.all_to_all(grad, 'zl', 0, 0)]
    ppermute x10, waiting for transfers between devices: 57.3 us -> 49.5 us  [shifted(): lax.ppermute(value, axis, [(i, (i + by) % size) for i in range(size)])]
    all_gather x1, waiting for transfers between devices: 7.4 us -> 3.36 us  [shards(): out_w = lax.all_gather(out_z, ('y', 'c'), axis=0)]
where the time goes in v5:
time: 264 us; the launch traced here: 263 us
  starting transfers between devices  79.6 us (30%)
  waiting for transfers between devices  72.5 us (27%)
  blocking collectives  57.8 us (22%)
  Pallas kernels  23.1 us (9%)
  between operations  14.4 us (5%)
  local copies, waits for them, and re-layouts  12.8 us (5%)
    ppermute x10, waiting for transfers between devices, shifted(): lax.ppermute(value, axis, [(i, (i + by) % size) for i in range(size)])  49.5 us
    ppermute x10, starting transfers between devices, shifted(): lax.ppermute(value, axis, [(i, (i + by) % size) for i in range(size)])  45.9 us
    all_to_all x1, blocking collectives, shards(): grad = lax.all_to_all(grad, 'zl', 0, 0)  31.1 us
    pallas_call x12, Pallas kernels, call(): pl.pallas_call(kernel, out_shape=out_shape, in_specs=specs, compiler_para...  23.1 us
    all_to_all x1, blocking collectives, shards(): errors = lax.all_to_all(error, 'x', 0, 0)  17.1 us
    all_to_all x1, waiting for transfers between devices, shards(): blocks = lax.all_to_all(part, 'x', 0, 0)  15.3 us
    all_to_all x1, starting transfers between devices, shards(): w_own = lax.all_to_all(mine, 'zl', 0, 0)  12.8 us
    unnamed x48, local copies, waits for them, and re-layouts  11.8 us
  transfers between devices with their start and end apart: 15, of which 10 were waited for; matrix products, arithmetic and copies ran while one was open for 1% of the time, Pallas kernels for 5%

profile of v5, /device:TPU:32, one launch (start us, length us, event | category | flops | bytes accessed | tf_op | source)
XLA Modules:
  0.0 262.8 jit_solution(3405528919559898511)
XLA Ops:
  7.2 2.0 shard_map.122
  9.3 12.8 %all-to-all-start = ((bf16[8,48,768]{2,1,0:T(8,128)(2,1)}), bf16[8,48,768]{2,1,0:T(8,128)(2,1)S(1)}, u32[]{:S(2)}, u32[]{:S(2)}) async-start(bf16[8,48,768]{2,1,0:T(8,128)(2,1)} %shard_map.122), calls=%async_computation | async-start | bytes 1179648 | tf_op jit(solution)/shard_map/all_to_all | solution.py:262
  23.7 4.0 %shard_map.123 = (bf16[256,1024]{1,0:T(8,128)(2,1)S(1)}, bf16[256,1024]{1,0:T(8,128)(2,1)}, bf16[256,1024]{1,0:T(8,128)(2,1)}, bf16[256,1024]{1,0:T(8,128)(2,1)}) custom-call(s32[3]{0:T(128)S(1)} %pad_add_fusion.at_ref, bf16[256,4096]{1,0:T(8,128)(2,1)S(1)} %copy-done.6), custom_call_target="tpu_custom_call" | custom-call | tf_op jit(solution)/shard_map/pallas_call | solution.py:229
  27.7 3.5 %collective-permute-start.1 = (bf16[256,1024]{1,0:T(8,128)(2,1)}, bf16[256,1024]{1,0:T(8,128)(2,1)}, u32[]{:S(2)}, u32[]{:S(2)}) collective-permute-start(bf16[256,1024]{1,0:T(8,128)(2,1)} %get-tuple-element.30), channel_id=1, source_target_pairs={{0,16},{16,32},{32,48},{48,0},{1,17},{17,33},{33,49},{49,1},{2,18}... | collective-permute-start | bytes 1572872 | tf_op jit(solution)/shard_map/ppermute | solution.py:240
  31.2 4.8 %collective-permute-start.2 = (bf16[256,1024]{1,0:T(8,128)(2,1)}, bf16[256,1024]{1,0:T(8,128)(2,1)}, u32[]{:S(2)}, u32[]{:S(2)}) collective-permute-start(bf16[256,1024]{1,0:T(8,128)(2,1)} %get-tuple-element.31), channel_id=1, source_target_pairs={{0,32},{16,48},{32,0},{48,16},{1,33},{17,49},{33,1},{49,17},{2,34}... | collective-permute-start | bytes 1572872 | tf_op jit(solution)/shard_map/ppermute | solution.py:240
  36.0 3.3 %collective-permute-start.3 = (bf16[256,1024]{1,0:T(8,128)(2,1)}, bf16[256,1024]{1,0:T(8,128)(2,1)}, u32[]{:S(2)}, u32[]{:S(2)}) collective-permute-start(bf16[256,1024]{1,0:T(8,128)(2,1)} %get-tuple-element.32), channel_id=1, source_target_pairs={{0,48},{16,0},{32,16},{48,32},{1,49},{17,1},{33,17},{49,33},{2,50}... | collective-permute-start | bytes 1572872 | tf_op jit(solution)/shard_map/ppermute | solution.py:240
  39.9 6.8 %collective-permute-start.8 = (bf16[64,512]{1,0:T(8,128)(2,1)S(1)}, bf16[64,512]{1,0:T(8,128)(2,1)S(1)}, u32[]{:S(2)}, u32[]{:S(2)}) collective-permute-start(bf16[64,512]{1,0:T(8,128)(2,1)S(1)} %shard_map.126), channel_id=1, source_target_pairs={{0,0},{1,64},{64,1},{65,65},{128,128},{129,192},{192,129},{193,193... | collective-permute-start | bytes 196616 | tf_op jit(solution)/shard_map/ppermute | solution.py:280
  47.8 4.4 %all-to-all-done.w_own = bf16[8,48,768]{2,1,0:T(8,128)(2,1)S(1)} async-done(((bf16[8,48,768]{2,1,0:T(8,128)(2,1)}), bf16[8,48,768]{2,1,0:T(8,128)(2,1)S(1)}, u32[]{:S(2)}, u32[]{:S(2)}) %all-to-all-start) | async-done | bytes 589856 | tf_op jit(solution)/shard_map/all_to_all | solution.py:262
  52.1 1.9 collective-permute-start
  59.8 9.9 %all-to-all-start.1 = ((bf16[8,64,512]{2,1,0:T(8,128)(2,1)}), bf16[8,64,512]{2,1,0:T(8,128)(2,1)}, u32[]{:S(2)}, u32[]{:S(2)}) async-start(bf16[8,64,512]{2,1,0:T(8,128)(2,1)} %broadcast_in_dim.19), calls=%async_computation.1 | async-start | bytes 1048576 | tf_op jit(solution)/shard_map/all_to_all | solution.py:282
  70.8 4.0 %shard_map.124 = (f32[256,768]{1,0:T(8,128)S(1)}, bf16[256,768]{1,0:T(8,128)(2,1)S(1)}, bf16[256,768]{1,0:T(8,128)(2,1)}, bf16[256,768]{1,0:T(8,128)(2,1)}) custom-call(bf16[8,48,768]{2,1,0:T(8,128)(2,1)S(1)} %all-to-all-done.w_own, bf16[8,48,768]{2,1,0:T(8,128)(2,1)S(1)} %copy-done.9, bf16[256,1024]{1,0:T(8,128)(2,1)S(1)} %get-tuple-element.35.s0, ...), custom_call_target="tpu_custom_call" | custom-call | tf_op jit(solution)/shard_map/pallas_call | solution.py:229
  75.7 4.5 %collective-permute-start.4 = (bf16[256,768]{1,0:T(8,128)(2,1)S(1)}, bf16[256,768]{1,0:T(8,128)(2,1)S(1)}, u32[]{:S(2)}, u32[]{:S(2)}) collective-permute-start(bf16[256,768]{1,0:T(8,128)(2,1)S(1)} %get-tuple-element.40), channel_id=1, source_target_pairs={{0,48},{16,0},{32,16},{48,32},{1,49},{17,1},{33,17},{49,33},{2,50}... | collective-permute-start | bytes 1179656 | tf_op jit(solution)/shard_map/ppermute | solution.py:240
  80.2 3.8 %collective-permute-start.5 = (bf16[256,768]{1,0:T(8,128)(2,1)}, bf16[256,768]{1,0:T(8,128)(2,1)S(1)}, u32[]{:S(2)}, u32[]{:S(2)}) collective-permute-start(bf16[256,768]{1,0:T(8,128)(2,1)} %get-tuple-element.41), channel_id=1, source_target_pairs={{0,32},{16,48},{32,0},{48,16},{1,33},{17,49},{33,1},{49,17},{2,34}... | collective-permute-start | bytes 1179656 | tf_op jit(solution)/shard_map/ppermute | solution.py:240
  84.0 1.9 collective-permute-start.6
  86.0 10.7 %collective-permute-done.4.p1 = bf16[256,768]{1,0:T(8,128)(2,1)S(1)} collective-permute-done((bf16[256,768]{1,0:T(8,128)(2,1)S(1)}, bf16[256,768]{1,0:T(8,128)(2,1)S(1)}, u32[]{:S(2)}, u32[]{:S(2)}) %collective-permute-start.4) | collective-permute-done | bytes 393248 | tf_op jit(solution)/shard_map/ppermute | solution.py:240
  96.7 5.7 %collective-permute-done.6.p3 = bf16[256,768]{1,0:T(8,128)(2,1)S(1)} collective-permute-done((bf16[256,768]{1,0:T(8,128)(2,1)}, bf16[256,768]{1,0:T(8,128)(2,1)S(1)}, u32[]{:S(2)}, u32[]{:S(2)}) %collective-permute-start.6) | collective-permute-done | bytes 393248 | tf_op jit(solution)/shard_map/ppermute | solution.py:240
  103.2 3.6 %shard_map.125 = (bf16[256,512]{1,0:T(8,128)(2,1)}, bf16[256,128]{1,0:T(8,128)(2,1)}, f32[4,256,256]{2,1,0:T(8,128)}, bf16[256,512]{1,0:T(8,128)(2,1)}) custom-call(f32[256,768]{1,0:T(8,128)} %copy-done.16, bf16[256,768]{1,0:T(8,128)(2,1)} %copy-done.20, bf16[256,768]{1,0:T(8,128)(2,1)} %copy-done.21, bf16[256,768]{1,0:T(8,128)(2,1)} %copy-done.22, ...), custom_call_target="tpu_custom_call" | custom-call | flops 99999997952 | tf_op jit(solution)/shard_map/pallas_call | solution.py:229
  106.8 8.2 %collective-permute-start.7 = (bf16[256,512]{1,0:T(8,128)(2,1)}, bf16[256,512]{1,0:T(8,128)(2,1)S(1)}, u32[]{:S(2)}, u32[]{:S(2)}) collective-permute-start(bf16[256,512]{1,0:T(8,128)(2,1)} %get-tuple-element.46.own), channel_id=1, source_target_pairs={{0,1},{1,0},{2,3},{3,2},{4,5},{5,4},{6,7},{7,6},{8,9},{9,8},{10,11... | collective-permute-start | bytes 786440 | tf_op jit(solution)/shard_map/ppermute | solution.py:240
  115.0 17.6 %collective-permute-done.7.oth = bf16[256,512]{1,0:T(8,128)(2,1)S(1)} collective-permute-done((bf16[256,512]{1,0:T(8,128)(2,1)}, bf16[256,512]{1,0:T(8,128)(2,1)S(1)}, u32[]{:S(2)}, u32[]{:S(2)}) %collective-permute-start.7) | collective-permute-done | bytes 262176 | tf_op jit(solution)/shard_map/ppermute | solution.py:240
  132.6 3.4 %all-gather.2.cloned.1.call-done.weight = bf16[8,4,2,64,512]{4,3,2,1,0:T(8,128)(2,1)} async-done(((bf16[1,4,2,64,512]{4,3,2,1,0:T(8,128)(2,1)}), bf16[8,4,2,64,512]{4,3,2,1,0:T(8,128)(2,1)}) %all-gather.2.cloned.1.call-update) | async-done | bytes 4194320 | tf_op jit(solution)/shard_map/all_gather | solution.py:294
  135.9 2.2 copy-done.1
  139.1 1.8 shard_map.127
  141.9 4.2 %all-to-all-start.2 = ((bf16[4,256,512]{2,1,0:T(8,128)(2,1)}), bf16[4,256,512]{2,1,0:T(8,128)(2,1)S(1)}, u32[]{:S(2)}, u32[]{:S(2)}) async-start(bf16[4,256,512]{2,1,0:T(8,128)(2,1)} %copy-done.3), calls=%async_computation.2 | async-start | bytes 2097152 | tf_op jit(solution)/shard_map/all_to_all | solution.py:315
  146.3 15.3 %all-to-all-done.2.blocks = bf16[4,256,512]{2,1,0:T(8,128)(2,1)S(1)} async-done(((bf16[4,256,512]{2,1,0:T(8,128)(2,1)}), bf16[4,256,512]{2,1,0:T(8,128)(2,1)S(1)}, u32[]{:S(2)}, u32[]{:S(2)}) %all-to-all-start.2) | async-done | bytes 1048608 | tf_op jit(solution)/shard_map/all_to_all | solution.py:315
  162.6 17.1 %all_to_all.30.errors = bf16[4,256,512]{2,1,0:T(8,128)(2,1)S(1)} all-to-all(bf16[4,256,512]{2,1,0:T(8,128)(2,1)S(1)} %get-tuple-element.50), channel_id=1, replica_groups=mesh['zl'=8,'y'=4,'c'=2,'x'=4,'zh'=2] {'x'}, dimensions={0} | all-to-all | bytes 2097152 | tf_op jit(solution)/shard_map/all_to_all | solution.py:324
  179.6 2.2 copy-done.2
  183.1 12.0 %collective-permute-start.9 = (bf16[256,512]{1,0:T(8,128)(2,1)S(1)}, bf16[256,512]{1,0:T(8,128)(2,1)S(1)}, u32[]{:S(2)}, u32[]{:S(2)}) collective-permute-start(bf16[256,512]{1,0:T(8,128)(2,1)S(1)} %shard_map.130), channel_id=1, source_target_pairs={{0,1},{1,0},{2,3},{3,2},{4,5},{5,4},{6,7},{7,6},{8,9},{9,8},{10,11... | collective-permute-start | bytes 786440 | tf_op jit(solution)/shard_map/ppermute | solution.py:240
  196.4 11.6 %collective-permute-done.9.d_other = bf16[256,512]{1,0:T(8,128)(2,1)S(1)} collective-permute-done((bf16[256,512]{1,0:T(8,128)(2,1)S(1)}, bf16[256,512]{1,0:T(8,128)(2,1)S(1)}, u32[]{:S(2)}, u32[]{:S(2)}) %collective-permute-start.9) | collective-permute-done | bytes 262176 | tf_op jit(solution)/shard_map/ppermute | solution.py:240
  209.1 9.7 %all_to_all.31.d_keys = bf16[4,256,128]{2,1,0:T(8,128)(2,1)S(1)} all-to-all(bf16[4,256,128]{2,1,0:T(8,128)(2,1)S(1)} %shard_map.131), channel_id=1, replica_groups=mesh['zl'=8,'y'=4,'c'=2,'x'=4,'zh'=2] {'y'}, dimensions={0} | all-to-all | bytes 524288 | tf_op jit(solution)/shard_map/all_to_all | solution.py:332
  218.8 2.1 shard_map.132
  220.9 1.9 collective-permute-start.10
  224.2 31.1 %all_to_all.32.parts = bf16[8,64,128]{2,1,0:T(8,128)(2,1)S(1)} all-to-all(bf16[8,64,128]{2,1,0:T(8,128)(2,1)S(1)} %add_convert_fusion), channel_id=1, replica_groups=mesh['zl'=8,'y'=4,'c'=2,'x'=4,'zh'=2] {'zl'}, dimensions={0} | all-to-all | bytes 262144 | tf_op jit(solution)/shard_map/all_to_all | solution.py:336
  (75 shorter events, 20.5 us)
Async XLA Ops:
  7.2 139.1 %copy-start = (bf16[256,4096]{1,0:T(8,128)(2,1)S(1)}, bf16[256,4096]{1,0:T(8,128)(2,1)}, u32[]{:S(2)}) copy-start(bf16[256,4096]{1,0:T(8,128)(2,1)} %param.12) | copy-start | bytes 6291460
  7.2 32.1 %copy-start.17 = (bf16[512,64]{0,1:T(8,128)(2,1)S(1)}, bf16[512,64]{0,1:T(8,128)(2,1)}, u32[]{:S(2)}) copy-start(bf16[512,64]{0,1:T(8,128)(2,1)} %param.16) | copy-start | bytes 196612
  7.2 32.2 %copy-start.18 = (s32[128,64]{0,1:T(8,128)S(1)}, s32[128,64]{0,1:T(8,128)}, u32[]{:S(2)}) copy-start(s32[128,64]{0,1:T(8,128)} %param.20) | copy-start | bytes 98308
  9.3 37.4 %copy-start.19 = (s32[1,3]{1,0:T(1,128)S(1)}, s32[1,3]{1,0:T(1,128)}, u32[]{:S(2)}) copy-start(s32[1,3]{1,0:T(1,128)} %param.21) | copy-start | bytes 40
  9.3 42.9 %all-to-all-start = ((bf16[8,48,768]{2,1,0:T(8,128)(2,1)}), bf16[8,48,768]{2,1,0:T(8,128)(2,1)S(1)}, u32[]{:S(2)}, u32[]{:S(2)}) async-start(bf16[8,48,768]{2,1,0:T(8,128)(2,1)} %shard_map.122), calls=%async_computation | async-start | bytes 1179648 | tf_op jit(solution)/shard_map/all_to_all | solution.py:262
  22.1 1.6 copy-start.6
  27.7 47.1 %copy-start.4 = (bf16[256,1024]{1,0:T(8,128)(2,1)}, bf16[256,1024]{1,0:T(8,128)(2,1)S(1)}, u32[]{:S(2)}) copy-start(bf16[256,1024]{1,0:T(8,128)(2,1)S(1)} %get-tuple-element.35.s0) | copy-start | bytes 1572868
  27.7 27.8 %collective-permute-start.1 = (bf16[256,1024]{1,0:T(8,128)(2,1)}, bf16[256,1024]{1,0:T(8,128)(2,1)}, u32[]{:S(2)}, u32[]{:S(2)}) collective-permute-start(bf16[256,1024]{1,0:T(8,128)(2,1)} %get-tuple-element.30), channel_id=1, source_target_pairs={{0,16},{16,32},{32,48},{48,0},{1,17},{17,33},{33,49},{49,1},{2,18}... | collective-permute-start | bytes 1572872 | tf_op jit(solution)/shard_map/ppermute | solution.py:240
  31.2 25.5 %collective-permute-start.2 = (bf16[256,1024]{1,0:T(8,128)(2,1)}, bf16[256,1024]{1,0:T(8,128)(2,1)}, u32[]{:S(2)}, u32[]{:S(2)}) collective-permute-start(bf16[256,1024]{1,0:T(8,128)(2,1)} %get-tuple-element.31), channel_id=1, source_target_pairs={{0,32},{16,48},{32,0},{48,16},{1,33},{17,49},{33,1},{49,17},{2,34}... | collective-permute-start | bytes 1572872 | tf_op jit(solution)/shard_map/ppermute | solution.py:240
  36.0 22.0 %collective-permute-start.3 = (bf16[256,1024]{1,0:T(8,128)(2,1)}, bf16[256,1024]{1,0:T(8,128)(2,1)}, u32[]{:S(2)}, u32[]{:S(2)}) collective-permute-start(bf16[256,1024]{1,0:T(8,128)(2,1)} %get-tuple-element.32), channel_id=1, source_target_pairs={{0,48},{16,0},{32,16},{48,32},{1,49},{17,1},{33,17},{49,33},{2,50}... | collective-permute-start | bytes 1572872 | tf_op jit(solution)/shard_map/ppermute | solution.py:240
  39.9 19.0 %collective-permute-start.8 = (bf16[64,512]{1,0:T(8,128)(2,1)S(1)}, bf16[64,512]{1,0:T(8,128)(2,1)S(1)}, u32[]{:S(2)}, u32[]{:S(2)}) collective-permute-start(bf16[64,512]{1,0:T(8,128)(2,1)S(1)} %shard_map.126), channel_id=1, source_target_pairs={{0,0},{1,64},{64,1},{65,65},{128,128},{129,192},{192,129},{193,193... | collective-permute-start | bytes 196616 | tf_op jit(solution)/shard_map/ppermute | solution.py:280
  52.1 6.0 %collective-permute-start = (bf16[8,48,768]{2,1,0:T(8,128)(2,1)S(1)}, bf16[8,48,768]{2,1,0:T(8,128)(2,1)S(1)}, u32[]{:S(2)}, u32[]{:S(2)}) collective-permute-start(bf16[8,48,768]{2,1,0:T(8,128)(2,1)S(1)} %all-to-all-done.w_own), channel_id=1, source_target_pairs={{0,8},{8,0},{1,9},{9,1},{2,10},{10,2},{3,11},{11,3},{4,12},{12,4},... | collective-permute-start | bytes 1769480 | tf_op jit(solution)/shard_map/ppermute | solution.py:240
  59.8 36.9 %all-to-all-start.1 = ((bf16[8,64,512]{2,1,0:T(8,128)(2,1)}), bf16[8,64,512]{2,1,0:T(8,128)(2,1)}, u32[]{:S(2)}, u32[]{:S(2)}) async-start(bf16[8,64,512]{2,1,0:T(8,128)(2,1)} %broadcast_in_dim.19), calls=%async_computation.1 | async-start | bytes 1048576 | tf_op jit(solution)/shard_map/all_to_all | solution.py:282
  69.7 66.2 %all-gather.2.cloned.1.call-start = ((), (), s32[]{:S(2)}) async-start(), calls=%async_computation.6 | async-start | bytes 4718592 | tf_op jit(solution)/shard_map/all_gather | solution.py:294
  75.7 21.0 %collective-permute-start.4 = (bf16[256,768]{1,0:T(8,128)(2,1)S(1)}, bf16[256,768]{1,0:T(8,128)(2,1)S(1)}, u32[]{:S(2)}, u32[]{:S(2)}) collective-permute-start(bf16[256,768]{1,0:T(8,128)(2,1)S(1)} %get-tuple-element.40), channel_id=1, source_target_pairs={{0,48},{16,0},{32,16},{48,32},{1,49},{17,1},{33,17},{49,33},{2,50}... | collective-permute-start | bytes 1179656 | tf_op jit(solution)/shard_map/ppermute | solution.py:240
  80.2 16.5 %collective-permute-start.5 = (bf16[256,768]{1,0:T(8,128)(2,1)}, bf16[256,768]{1,0:T(8,128)(2,1)S(1)}, u32[]{:S(2)}, u32[]{:S(2)}) collective-permute-start(bf16[256,768]{1,0:T(8,128)(2,1)} %get-tuple-element.41), channel_id=1, source_target_pairs={{0,32},{16,48},{32,0},{48,16},{1,33},{17,49},{33,1},{49,17},{2,34}... | collective-permute-start | bytes 1179656 | tf_op jit(solution)/shard_map/ppermute | solution.py:240
  84.0 18.4 %collective-permute-start.6 = (bf16[256,768]{1,0:T(8,128)(2,1)}, bf16[256,768]{1,0:T(8,128)(2,1)S(1)}, u32[]{:S(2)}, u32[]{:S(2)}) collective-permute-start(bf16[256,768]{1,0:T(8,128)(2,1)} %get-tuple-element.42), channel_id=1, source_target_pairs={{0,16},{16,32},{32,48},{48,0},{1,17},{17,33},{33,49},{49,1},{2,18}... | collective-permute-start | bytes 1179656 | tf_op jit(solution)/shard_map/ppermute | solution.py:240
  96.6 5.8 %copy-start.20 = (bf16[256,768]{1,0:T(8,128)(2,1)}, bf16[256,768]{1,0:T(8,128)(2,1)S(1)}, u32[]{:S(2)}) copy-start(bf16[256,768]{1,0:T(8,128)(2,1)S(1)} %collective-permute-done.4.p1) | copy-start | bytes 1179652
  96.7 5.8 %copy-start.21 = (bf16[256,768]{1,0:T(8,128)(2,1)}, bf16[256,768]{1,0:T(8,128)(2,1)S(1)}, u32[]{:S(2)}) copy-start(bf16[256,768]{1,0:T(8,128)(2,1)S(1)} %collective-permute-done.5.p2) | copy-start | bytes 1179652
  106.8 25.8 %collective-permute-start.7 = (bf16[256,512]{1,0:T(8,128)(2,1)}, bf16[256,512]{1,0:T(8,128)(2,1)S(1)}, u32[]{:S(2)}, u32[]{:S(2)}) collective-permute-start(bf16[256,512]{1,0:T(8,128)(2,1)} %get-tuple-element.46.own), channel_id=1, source_target_pairs={{0,1},{1,0},{2,3},{3,2},{4,5},{5,4},{6,7},{7,6},{8,9},{9,8},{10,11... | collective-permute-start | bytes 786440 | tf_op jit(solution)/shard_map/ppermute | solution.py:240
  135.9 2.2 copy-start.1
  141.9 19.7 %all-to-all-start.2 = ((bf16[4,256,512]{2,1,0:T(8,128)(2,1)}), bf16[4,256,512]{2,1,0:T(8,128)(2,1)S(1)}, u32[]{:S(2)}, u32[]{:S(2)}) async-start(bf16[4,256,512]{2,1,0:T(8,128)(2,1)} %copy-done.3), calls=%async_computation.2 | async-start | bytes 2097152 | tf_op jit(solution)/shard_map/all_to_all | solution.py:315
  179.6 2.2 copy-start.2
  183.1 24.9 %copy-start.7 = (f32[4,256,256]{2,1,0:T(8,128)S(1)}, f32[4,256,256]{2,1,0:T(8,128)}, u32[]{:S(2)}) copy-start(f32[4,256,256]{2,1,0:T(8,128)} %get-tuple-element.53.prob_ref) | copy-start | bytes 3145732
  183.1 24.9 %copy-start.10 = (f32[256,128]{1,0:T(8,128)S(1)}, f32[256,128]{1,0:T(8,128)}, u32[]{:S(2)}) copy-start(f32[256,128]{1,0:T(8,128)} %get-tuple-element.43.cos) | copy-start | bytes 393220
  183.1 24.9 %copy-start.11 = (f32[256,128]{1,0:T(8,128)S(1)}, f32[256,128]{1,0:T(8,128)}, u32[]{:S(2)}) copy-start(f32[256,128]{1,0:T(8,128)} %get-tuple-element.44.sin) | copy-start | bytes 393220
  183.1 24.9 %copy-start.13 = (bf16[256,512]{1,0:T(8,128)(2,1)S(1)}, bf16[256,512]{1,0:T(8,128)(2,1)}, u32[]{:S(2)}) copy-start(bf16[256,512]{1,0:T(8,128)(2,1)} %get-tuple-element.51.q_ref) | copy-start | bytes 786436
  183.1 24.9 %copy-start.14 = (bf16[256,128]{1,0:T(8,128)(2,1)S(1)}, bf16[256,128]{1,0:T(8,128)(2,1)}, u32[]{:S(2)}) copy-start(bf16[256,128]{1,0:T(8,128)(2,1)} %get-tuple-element.52.v_ref) | copy-start | bytes 196612
  183.1 24.9 %collective-permute-start.9 = (bf16[256,512]{1,0:T(8,128)(2,1)S(1)}, bf16[256,512]{1,0:T(8,128)(2,1)S(1)}, u32[]{:S(2)}, u32[]{:S(2)}) collective-permute-start(bf16[256,512]{1,0:T(8,128)(2,1)S(1)} %shard_map.130), channel_id=1, source_target_pairs={{0,1},{1,0},{2,3},{3,2},{4,5},{5,4},{6,7},{7,6},{8,9},{9,8},{10,11... | collective-permute-start | bytes 786440 | tf_op jit(solution)/shard_map/ppermute | solution.py:240
  196.4 22.4 %copy-start.5 = (bf16[256,1024]{1,0:T(8,128)(2,1)S(1)}, bf16[256,1024]{1,0:T(8,128)(2,1)}, u32[]{:S(2)}) copy-start(bf16[256,1024]{1,0:T(8,128)(2,1)} %copy-done.4) | copy-start | bytes 1572868
  209.1 46.2 %copy-start.15 = (s32[16,128]{1,0:T(8,128)S(1)}, s32[16,128]{1,0:T(8,128)}, u32[]{:S(2)}) copy-start(s32[16,128]{1,0:T(8,128)} %codes.1) | copy-start | bytes 24580
  220.9 3.2 %collective-permute-start.10 = (bf16[8,64,128]{2,1,0:T(8,128)(2,1)S(1)}, bf16[8,64,128]{2,1,0:T(8,128)(2,1)S(1)}, u32[]{:S(2)}, u32[]{:S(2)}) collective-permute-start(bf16[8,64,128]{2,1,0:T(8,128)(2,1)S(1)} %get-tuple-element.55), channel_id=1, source_target_pairs={{0,8},{8,0},{1,9},{9,1},{2,10},{10,2},{3,11},{11,3},{4,12},{12,4},... | collective-permute-start | bytes 393224 | tf_op jit(solution)/shard_map/ppermute | solution.py:240
  (6 other events, 5.5 us)
Sparse Core Ops, SparseCore 0:
  96.8 39.0 all-gather.1
